TPU v7x, 512 devices: a whole 4x4x16 slice. The times are simulated.
512 devices in a mesh: row: 32 (over x, y, core), col: 16 (over z).
Axes of the slice: x: 4, y: 4, z: 16, core: 2. Of those that a mesh axis runs over, the one named last changes fastest.
Arguments:
- features: bfloat16 [65536, 128], P(('row', 'col')), may hold values from -6 to 6
- tile_values: bfloat16 [32, 16, 96, 128, 128], P('row', 'col'), may hold values from -0.109375 to 0.109375
- tile_rows: int32 [32, 16, 96], P('row', 'col'), may hold values from 0 to 15
- tile_cols: int32 [32, 16, 96], P('row', 'col'), may hold values from 0 to 31
- tile_rels: int32 [32, 16, 96], P('row', 'col'), may hold values from 0 to 3
- live: int32 [32, 16], P('row', 'col'), may hold values from 24 to 96, as said below
- weights: bfloat16 [4, 128, 128], replicated, may hold values from -0.25 to 0.25
- bias: float32 [128], replicated, may hold values from -3 to 3
- out_grad: bfloat16 [65536, 128], P(('row', 'col')), may hold values from -6 to 6
Outputs:
- activated: bfloat16 [65536, 128], P(('row', 'col'))
- feature_grad: float32 [65536, 128], P(('row', 'col'))
- weight_grad: float32 [4, 128, 128], replicated
- bias_grad: float32 [128], replicated
Inputs may be any that keep to these rules, and one draw needn't show every extreme that they name: Each grid cell uses the first live of its 96 tile slots; some cell uses all 96.
All inputs are finite; a program needn't handle non-finite values.
Results may differ from a plain program's by a relative error of at most 0.008.
Values may be sent and summed in bfloat16 or wider, within the bound.
No kernel may reach another device: no remote copies, remote signals or barrier semaphores. Data moves between devices by JAX's collectives and lax.ppermute only.
A program may use at most 64 MiB of HBM per device.

v0:
```python
import jax
import jax.numpy as jnp
from jax import lax
from jax.sharding import PartitionSpec as P

RB = 16


def silu_slope(z_values):
    sigma = jax.nn.sigmoid(z_values)
    return sigma * (1.0 + z_values * (1.0 - sigma))


def on_device(
    features, tile_values, tile_rows, tile_cols, tile_rels, live, weights, bias, out_grad
):
    ntiles = tile_rows.shape[2]
    values = tile_values.reshape(ntiles, 128, 128)
    row_ids = tile_rows.reshape(ntiles)
    col_ids = tile_cols.reshape(ntiles)
    rel_ids = tile_rels.reshape(ntiles)
    keeping = (jnp.arange(ntiles, dtype=jnp.int32) < live.reshape(())).astype(jnp.bfloat16)
    values = values * keeping[:, None, None]
    gathered = lax.all_gather(features, "row", axis=0, tiled=True)
    blocks = gathered.reshape(-1, 128, 128)
    col_blocks = blocks.shape[0]
    picked = jnp.take(blocks, col_ids, axis=0)
    products = jnp.einsum("kij,kjf->kif", values, picked, preferred_element_type=jnp.float32)
    slot_ids = rel_ids * RB + row_ids
    onehot = (jnp.arange(4 * RB, dtype=jnp.int32)[:, None] == slot_ids[None, :]).astype(jnp.float32)
    partial_value = jnp.dot(onehot, products.reshape(ntiles, -1), precision=lax.Precision.HIGHEST)
    partial_value = partial_value.reshape(4, RB * 128, 128)
    wide_weights = weights.astype(jnp.float32)
    z_part = jnp.einsum("rnf,rfg->ng", partial_value, wide_weights, precision=lax.Precision.HIGHEST)
    z_piece = lax.psum_scatter(z_part, "col", scatter_dimension=0, tiled=True) + bias
    grad_piece = (out_grad.astype(jnp.float32) * silu_slope(z_piece)).astype(jnp.bfloat16)
    grad_rows = lax.all_gather(grad_piece, "col", axis=0, tiled=True)
    activated = (z_piece * jax.nn.sigmoid(z_piece)).astype(jnp.bfloat16)
    grad_wide = grad_rows.astype(jnp.float32)
    weight_part = jnp.einsum(
        "rnf,ng->rfg", partial_value, grad_wide, precision=lax.Precision.HIGHEST
    )
    bias_part = jnp.sum(grad_piece.astype(jnp.float32), axis=0)
    weight_grad, bias_grad = lax.psum((weight_part, bias_part), ("row", "col"))
    back_rows = jnp.einsum("ng,rfg->rnf", grad_rows, weights, preferred_element_type=jnp.float32)
    back_rows = back_rows.astype(jnp.bfloat16).reshape(4 * RB, 128, 128)
    back_tiles = jnp.take(back_rows, slot_ids, axis=0)
    tile_terms = jnp.einsum("kji,kjf->kif", values, back_tiles, preferred_element_type=jnp.float32)
    flat_terms = tile_terms.reshape(ntiles, -1)
    colhot = (jnp.arange(col_blocks, dtype=jnp.int32)[:, None] == col_ids[None, :]).astype(
        jnp.float32
    )
    col_sums = jnp.dot(colhot, flat_terms, precision=lax.Precision.HIGHEST)
    col_sums = col_sums.reshape(col_blocks * 128, 128)
    feature_grad = lax.psum_scatter(col_sums, "row", scatter_dimension=0, tiled=True)
    return (activated, feature_grad, weight_grad, bias_grad)


def solution(mesh):
    placed = (
        P(("row", "col"), None),
        P("row", "col", None, None, None),
        P("row", "col", None),
        P("row", "col", None),
        P("row", "col", None),
        P("row", "col"),
        P(),
        P(),
        P(("row", "col"), None),
    )
    return jax.shard_map(
        on_device,
        mesh=mesh,
        in_specs=placed,
        out_specs=(P(("row", "col"), None), P(("row", "col"), None), P(), P()),
        check_vma=False,
    )
```

profile of v0, /device:TPU:1, one launch (start us, length us, event | category | flops | bytes accessed | tf_op | source)
XLA Modules:
  0.0 774.0 jit_solution(16071888279757993658)
XLA Ops:
  7.2 0.0 copy-start
  7.2 0.0 all-gather.2.cloned.1.call-start
  7.2 0.7 all-gather.2.cloned.1.call-update
  7.9 0.0 reduce-scatter.3.cloned.1.call-start
  8.6 0.7 fusion.21
  9.3 0.7 compare_and_fusion.1
  9.9 0.7 fusion.25
  10.6 64.4 %all-gather.2.cloned.1.call-done = bf16[4096,128]{1,0:T(8,128)(2,1)} async-done(((bf16[128,128]{1,0:T(8,128)(2,1)}), bf16[4096,128]{1,0:T(8,128)(2,1)}) %all-gather.2.cloned.1.call-update) | async-done | bytes 1048592 | tf_op jit(solution)/shard_map/all_gather | solution.py:24
  75.0 2.4 gather_fusion
  77.4 2.9 fusion.8
  80.3 9.7 %fusion.3 = f32[64,16384]{1,0:T(8,128)} fusion(f32[12,8,128,128]{3,2,1,0:T(8,128)S(1)} %bitcast.43, s32[96]{0:T(128)S(1)} %fusion.25), kind=kOutput, calls=%fused_computation.5 | convolution fusion | flops 1207965696 | bytes 10486144 | tf_op jit(solution)/shard_map/dot_general | solution.py:31
  90.0 4.9 reshape.139
  94.9 0.0 copy-done
  94.9 0.0 copy-start.4
  94.9 0.0 copy-start.5
  94.9 0.0 copy-start.1
  94.9 0.0 copy-start.3
  94.9 5.2 convolution_bitcast_fusion
  100.1 0.0 reduce-scatter.3.cloned.1.call-update
  100.1 0.0 all-reduce.2.cloned.1.call-start
  100.2 0.0 copy-done.4
  100.2 0.0 copy-done.5
  100.2 59.5 %reduce-scatter.3.cloned.1.call-done = f32[128,128]{1,0:T(8,128)} async-done(((f32[2048,128]{1,0:T(8,128)}), f32[128,128]{1,0:T(8,128)}) %reduce-scatter.3.cloned.1.call-update) | async-done | bytes 65552 | tf_op jit(solution)/shard_map/reduce_scatter | solution.py:35
  159.7 0.0 copy-done.1
  159.7 0.0 copy-done.3
  159.7 1.5 convert_reduce_fusion
  161.2 24.4 %all_gather.7 = bf16[2048,128]{1,0:T(8,128)(2,1)S(1)} all-gather(bf16[128,128]{1,0:T(8,128)(2,1)S(1)} %get-tuple-element.5), channel_id=1, replica_groups=mesh['row'=32,'col'=16] {'col'}, dimensions={0}, use_global_device_ids=true | all-gather | bytes 557056 | tf_op jit(solution)/shard_map/all_gather | solution.py:37
  185.6 6.3 fusion.16
  191.9 0.7 convolution_convert_fusion
  192.6 0.0 all-reduce.2.cloned.1.call-update
  192.6 0.0 reduce-scatter.5.cloned.1.call-start
  192.7 2.7 gather_fusion.1
  195.4 0.0 copy-start.2
  195.4 4.3 fusion.6
  199.7 0.0 copy-done.2
  199.7 5.9 fusion
  205.5 1.5 reshape.142
  207.0 0.0 reduce-scatter.5.cloned.1.call-update
  207.1 117.0 %psum.15 = f32[128]{0:T(128)} all-reduce(f32[128]{0:T(128)S(1)} %get-tuple-element.4), channel_id=1, replica_groups=mesh['row'=32,'col'=16] {'row','col'}, use_global_device_ids=true, to_apply=%region_4.5 | all-reduce | flops 128 | bytes 1024 | tf_op jit(solution)/shard_map/psum | solution.py:44
  324.1 339.5 %all-reduce.2.cloned.1.call-done = f32[4,128,128]{2,1,0:T(8,128)} async-done(((f32[4,128,128]{2,1,0:T(8,128)}), f32[4,128,128]{2,1,0:T(8,128)}) %all-reduce.2.cloned.1.call-update) | async-done | bytes 262160 | tf_op jit(solution)/shard_map/psum | solution.py:44
  663.6 102.2 %reduce-scatter.5.cloned.1.call-done = f32[128,128]{1,0:T(8,128)} async-done(((f32[4096,128]{1,0:T(8,128)}), f32[128,128]{1,0:T(8,128)}) %reduce-scatter.5.cloned.1.call-update) | async-done | bytes 65552 | tf_op jit(solution)/shard_map/reduce_scatter | solution.py:55
  765.8 1.7 copy.29
  (4 shorter events, 0.0 us)
Async XLA Ops:
  7.2 87.7 %copy-start = (bf16[4,128,128]{2,1,0:T(8,128)(2,1)S(1)}, bf16[4,128,128]{2,1,0:T(8,128)(2,1)}, u32[]{:S(2)}) copy-start(bf16[4,128,128]{2,1,0:T(8,128)(2,1)} %param.15) | copy-start | bytes 393220
  7.2 67.8 %all-gather.2.cloned.1.call-start = ((), (), s32[]{:S(2)}) async-start(), calls=%async_computation.2 | async-start | bytes 1081344 | tf_op jit(solution)/shard_map/all_gather | solution.py:24
  7.9 151.8 %reduce-scatter.3.cloned.1.call-start = ((), (), s32[]{:S(2)}) async-start(), calls=%async_computation.3 | async-start | bytes 1114112 | tf_op jit(solution)/shard_map/reduce_scatter | solution.py:35
  94.9 5.3 copy-start.4
  94.9 5.3 copy-start.5
  94.9 64.8 %copy-start.1 = (bf16[128,128]{1,0:T(8,128)(2,1)S(1)}, bf16[128,128]{1,0:T(8,128)(2,1)}, u32[]{:S(2)}) copy-start(bf16[128,128]{1,0:T(8,128)(2,1)} %param.17) | copy-start | bytes 98308
  94.9 64.8 %copy-start.3 = (f32[128]{0:T(128)S(1)}, f32[128]{0:T(128)}, u32[]{:S(2)}) copy-start(f32[128]{0:T(128)} %param.16) | copy-start | bytes 1540
  100.1 563.5 %all-reduce.2.cloned.1.call-start = ((), (), s32[]{:S(2)}) async-start(), calls=%async_computation.5 | async-start | bytes 524288 | tf_op jit(solution)/shard_map/psum | solution.py:44
  192.6 573.2 %reduce-scatter.5.cloned.1.call-start = ((), (), s32[]{:S(2)}) async-start(), calls=%async_computation.4 | async-start | bytes 2162688 | tf_op jit(solution)/shard_map/reduce_scatter | solution.py:55
  195.4 4.3 copy-start.2
Sparse Core Ops, SparseCore 0:
  11.2 63.8 all-gather.1
  100.2 59.4 reduce-scatter.2
  192.8 470.8 all-reduce.1
  668.5 97.3 reduce-scatter.4
where the time goes:
time: 775 us; the launch traced here: 774 us
  waiting for transfers between devices  566 us (73%)
  blocking collectives  141 us (18%)
  matrix products  34.9 us (5%)
  between operations  14.5 us (2%)
  local copies, waits for them, and re-layouts  13.2 us (2%)
    psum x1, waiting for transfers between devices, on_device(): weight_grad, bias_grad = lax.psum((weight_part, bias_part), ('row', 'col'))  340 us
    psum x1, blocking collectives, on_device(): weight_grad, bias_grad = lax.psum((weight_part, bias_part), ('row', 'col'))  117 us
    reduce_scatter x1, waiting for transfers between devices, on_device(): lax.psum_scatter(col_sums, 'row', scatter_dimension=0, tiled=True)  102 us
    all_gather x1, waiting for transfers between devices, on_device(): gathered = lax.all_gather(features, 'row', axis=0, tiled=True)  64.4 us
    reduce_scatter x1, waiting for transfers between devices, on_device(): lax.psum_scatter(z_part, 'col', scatter_dimension=0, tiled=True) + bias  59.5 us
    all_gather x1, blocking collectives, on_device(): grad_rows = lax.all_gather(grad_piece, 'col', axis=0, tiled=True)  24.4 us
  transfers between devices with their start and end apart: 4, of which 4 were waited for; matrix products, arithmetic and copies ran while one was open for 2% of the time, Pallas kernels for 0%

commit v1 on v0

v1 whole, which is shorter than its diff:
```python
import jax
import jax.numpy as jnp
from jax import lax
from jax.experimental import pallas as pl
from jax.experimental.pallas import tpu as pltpu
from jax.sharding import PartitionSpec as P

RB = 16
CB = 32
RELS = 4
B = 128
STEP = 4
SLICE = CB // RELS
PART = B // SLICE


def dot(a, b):
    return jnp.dot(a, b, preferred_element_type=jnp.float32)


def forward_kernel(rows, cols, rels, live, x, v, w, z, p, acc):
    acc[...] = jnp.zeros_like(acc)
    count = live[0, 0]

    def group(step, carry):
        first = step * STEP
        for u in range(STEP):
            k = first + u
            row = rows[0, 0, k]
            lane = pl.multiple_of(rels[0, 0, k] * B, B)
            product = dot(v[0, 0, k], x[cols[0, 0, k]])
            product = jnp.where(k < count, product, 0.0)
            acc[row, :, pl.ds(lane, B)] += product
        return carry

    lax.fori_loop(0, (count + STEP - 1) // STEP, group, 0)
    wide = w[...]

    def finish(row, carry):
        held = acc[row].astype(jnp.bfloat16)
        p[row] = held
        z[row] = dot(held, wide).astype(jnp.bfloat16)
        return carry

    lax.fori_loop(0, RB, finish, 0, unroll=2)


def middle_kernel(parts, bias, out_grad, activated, grad_t, bias_row):
    z = parts[0].astype(jnp.float32)
    for c in range(1, parts.shape[0]):
        z = z + parts[c].astype(jnp.float32)
    z = z + bias[...]
    s = jax.nn.sigmoid(z)
    activated[...] = (z * s).astype(jnp.bfloat16)
    slope = s * (1.0 + z * (1.0 - s))
    grad = (out_grad[...].astype(jnp.float32) * slope).astype(jnp.bfloat16)
    wide = grad.astype(jnp.float32)
    grad_t[...] = wide.T.astype(jnp.bfloat16)
    total = jnp.sum(wide, axis=0, keepdims=True)
    keep = lax.broadcasted_iota(jnp.int32, (8, B), 0) == 0
    bias_row[...] = jnp.where(keep, total, 0.0)


def backward_kernel(rows, cols, rels, live, grad_t, v, p, w, out, back, acc, wgrad):
    acc[...] = jnp.zeros_like(acc)
    wgrad[...] = jnp.zeros_like(wgrad)
    wide = w[...]
    count = live[0, 0]

    def start(row, carry):
        g = grad_t[row]
        back[row] = dot(wide, g).astype(jnp.bfloat16)
        wgrad[...] += dot(g, p[row])
        return carry

    lax.fori_loop(0, RB, start, 0, unroll=2)

    def group(step, carry):
        first = step * STEP
        for u in range(STEP):
            k = first + u
            at = pl.multiple_of(rels[0, 0, k] * B, B)
            product = dot(back[rows[0, 0, k], pl.ds(at, B), :], v[0, 0, k])
            product = jnp.where(k < count, product, 0.0)
            acc[cols[0, 0, k]] += product
        return carry

    lax.fori_loop(0, (count + STEP - 1) // STEP, group, 0)
    out[:, :B, :] = acc[...].astype(jnp.bfloat16)
    for b in range(CB):
        rel, part = b // SLICE, b % SLICE
        term = wgrad[part * PART : (part + 1) * PART, rel * B : (rel + 1) * B]
        high = term.astype(jnp.bfloat16)
        low = (term - high.astype(jnp.float32)).astype(jnp.bfloat16)
        out[b, B : B + PART, :] = high
        out[b, B + PART : B + 2 * PART, :] = low


VMEM = pl.BlockSpec(memory_space=pltpu.VMEM)
SMEM = pl.BlockSpec(memory_space=pltpu.SMEM)
PARAMS = pltpu.CompilerParams(vmem_limit_bytes=32 * 1024 * 1024)


def copies(block, axis, count):
    wide = jnp.broadcast_to(block[None], (count,) + block.shape)
    return lax.all_to_all(wide, axis, 0, 0, tiled=True)


def on_device(
    features, tile_values, tile_rows, tile_cols, tile_rels, live, weights, bias, out_grad
):
    ncol = RB
    wide_weights = weights.reshape(RELS * B, B)
    blocks = copies(features, "row", CB)
    z_parts, p_wide = pl.pallas_call(
        forward_kernel,
        out_shape=(
            jax.ShapeDtypeStruct((RB, B, B), jnp.bfloat16),
            jax.ShapeDtypeStruct((RB, B, RELS * B), jnp.bfloat16),
        ),
        in_specs=[SMEM] * 4 + [VMEM] * 3,
        out_specs=(VMEM, VMEM),
        scratch_shapes=[pltpu.VMEM((RB, B, RELS * B), jnp.float32)],
        compiler_params=PARAMS,
        name="forward",
    )(tile_rows, tile_cols, tile_rels, live, blocks, tile_values, wide_weights)
    z_parts = lax.all_to_all(z_parts, "col", 0, 0, tiled=True)
    activated, grad_t, bias_row = pl.pallas_call(
        middle_kernel,
        out_shape=(
            jax.ShapeDtypeStruct((B, B), jnp.bfloat16),
            jax.ShapeDtypeStruct((B, B), jnp.bfloat16),
            jax.ShapeDtypeStruct((8, B), jnp.float32),
        ),
        in_specs=[VMEM] * 3,
        out_specs=(VMEM,) * 3,
        compiler_params=PARAMS,
        name="middle",
    )(z_parts, bias.reshape(1, B), out_grad)
    grad_all = lax.all_gather(grad_t, "col", axis=0, tiled=False)
    sent = pl.pallas_call(
        backward_kernel,
        out_shape=jax.ShapeDtypeStruct((CB, B + 2 * PART, B), jnp.bfloat16),
        in_specs=[SMEM] * 4 + [VMEM] * 4,
        out_specs=VMEM,
        scratch_shapes=[
            pltpu.VMEM((RB, RELS * B, B), jnp.bfloat16),
            pltpu.VMEM((CB, B, B), jnp.float32),
            pltpu.VMEM((B, RELS * B), jnp.float32),
        ],
        compiler_params=PARAMS,
        name="backward",
    )(tile_rows, tile_cols, tile_rels, live, grad_all, tile_values, p_wide, wide_weights)
    received = lax.all_to_all(sent, "row", 0, 0, tiled=True)
    summed = jnp.sum(received.astype(jnp.float32), axis=0)
    feature_grad = summed[:B].T
    own = summed[B : B + PART] + summed[B + PART :]
    own = jnp.concatenate([own, bias_row], axis=0)
    own = jnp.sum(copies(own, "col", ncol), axis=0)
    every = copies(own, "row", CB)
    weight_grad = every[:, :PART].reshape(RELS, B, B).transpose(0, 2, 1)
    bias_grad = jnp.sum(every[:, PART], axis=0)
    return (activated, feature_grad, weight_grad, bias_grad)


def solution(mesh):
    placed = (
        P(("row", "col"), None),
        P("row", "col", None, None, None),
        P("row", "col", None),
        P("row", "col", None),
        P("row", "col", None),
        P("row", "col"),
        P(),
        P(),
        P(("row", "col"), None),
    )
    return jax.shard_map(
        on_device,
        mesh=mesh,
        in_specs=placed,
        out_specs=(P(("row", "col"), None), P(("row", "col"), None), P(), P()),
        check_vma=False,
    )
```

time: 775 us -> 183 us (0.24)
  waiting for transfers between devices: 566 us -> 26 us
  matrix products: 34.9 us -> 0 us
  blocking collectives: 141 us -> 119 us
  starting transfers between devices: 0.16 us -> 18.2 us
  between operations: 14.5 us -> 1.41 us
  Pallas kernels: 0 us -> 11.9 us
    psum x1 -> x0, waiting for transfers between devices: 340 us -> none  [on_device(): weight_grad, bias_grad = lax.psum((weight_part, bias_part), ('row', 'col'))]
    reduce_scatter x2 -> x0, waiting for transfers between devices: 162 us -> none  [the longest x1 102 us: on_device(): lax.psum_scatter(col_sums, 'row', scatter_dimension=0, tiled=True)]
    psum x1 -> x0, blocking collectives: 117 us -> none  [on_device(): weight_grad, bias_grad = lax.psum((weight_part, bias_part), ('row', 'col'))]
    all_to_all x0 -> x3, blocking collectives: none -> 90.7 us  [the longest x1 39.8 us: on_device(): received = lax.all_to_all(sent, 'row', 0, 0, tiled=True)]
    all_gather x1 -> x0, waiting for transfers between devices: 64.4 us -> none  [on_device(): gathered = lax.all_gather(features, 'row', axis=0, tiled=True)]
    dot_general x7 -> x0, matrix products: 34.9 us -> none  [the longest x1 9.68 us: on_device(): jnp.dot(onehot, products.reshape(ntiles, -1), precision=lax.Precision.HIG...]
    all_to_all x0 -> x2, waiting for transfers between devices: none -> 26 us  [copies(): return lax.all_to_all(wide, axis, 0, 0, tiled=True)]
    all_to_all x0 -> x2, starting transfers between devices: none -> 18.2 us  [copies(): return lax.all_to_all(wide, axis, 0, 0, tiled=True)]
  transfers between devices with their start and end apart: 4 -> 2, of which waited for: 4 -> 2; matrix products, arithmetic and copies ran while one was open for 2% -> 0% of each run, Pallas kernels for 0% -> 0%
where the time goes in v1:
time: 183 us
  blocking collectives  119 us (65%)
  waiting for transfers between devices  26 us (14%)
  starting transfers between devices  18.2 us (10%)
  Pallas kernels  11.9 us (7%)
  local copies, waits for them, and re-layouts  5.46 us (3%)
    all_to_all x1, blocking collectives, on_device(): received = lax.all_to_all(sent, 'row', 0, 0, tiled=True)  39.8 us
    all_to_all x1, blocking collectives, on_device(): z_parts = lax.all_to_all(z_parts, 'col', 0, 0, tiled=True)  34.7 us
    all_gather x1, blocking collectives, on_device(): grad_all = lax.all_gather(grad_t, 'col', axis=0, tiled=False)  28.3 us
    all_to_all x2, waiting for transfers between devices, copies(): return lax.all_to_all(wide, axis, 0, 0, tiled=True)  26 us
    all_to_all x2, starting transfers between devices, copies(): return lax.all_to_all(wide, axis, 0, 0, tiled=True)  18.2 us
    all_to_all x1, blocking collectives, copies(): return lax.all_to_all(wide, axis, 0, 0, tiled=True)  16.2 us
    pallas_call x1, Pallas kernels, on_device(): pl.pallas_call(forward_kernel, out_shape=(jax.ShapeDtypeStruct((RB, B, B)...  5.81 us
    pallas_call x1, Pallas kernels, on_device(): pl.pallas_call(backward_kernel, out_shape=jax.ShapeDtypeStruct((CB, B + 2...  5.37 us
  transfers between devices with their start and end apart: 2, of which 2 were waited for; matrix products, arithmetic and copies ran while one was open for 0% of the time, Pallas kernels for 0%

profile of v1, /device:TPU:1, one launch (start us, length us, event | category | flops | bytes accessed | tf_op | source)
XLA Modules:
  0.0 182.7 jit_solution(5272444153749891324)
XLA Ops:
  0.6 0.0 copy-start.5
  0.6 0.0 copy-start.4
  0.7 0.0 copy-start.3
  0.7 0.0 copy-start
  0.7 2.2 %broadcast_in_dim.6 = bf16[32,128,128]{2,1,0:T(8,128)(2,1)} broadcast(bf16[128,128]{1,0:T(8,128)(2,1)} %param.9), dimensions={1,2} | broadcast | bytes 1081344 | tf_op jit(solution)/shard_map/broadcast_in_dim | solution.py:105
  2.8 11.1 %all-to-all-start = ((bf16[32,128,128]{2,1,0:T(8,128)(2,1)}), bf16[32,128,128]{2,1,0:T(8,128)(2,1)}, u32[]{:S(2)}, u32[]{:S(2)}) async-start(bf16[32,128,128]{2,1,0:T(8,128)(2,1)} %broadcast_in_dim.6), calls=%async_computation | async-start | bytes 2097152 | tf_op jit(solution)/shard_map/all_to_all | solution.py:106
  14.6 16.4 %all-to-all-done.x = bf16[32,128,128]{2,1,0:T(8,128)(2,1)} async-done(((bf16[32,128,128]{2,1,0:T(8,128)(2,1)}), bf16[32,128,128]{2,1,0:T(8,128)(2,1)}, u32[]{:S(2)}, u32[]{:S(2)}) %all-to-all-start) | async-done | bytes 1048608 | tf_op jit(solution)/shard_map/all_to_all | solution.py:106
  31.0 0.0 copy-done.5
  31.0 0.0 copy-done.4
  31.0 0.0 copy-done.3
  31.0 0.0 copy-done
  31.0 0.0 copy-start.1
  31.0 0.9 copy-done.1
  31.9 0.0 copy-start.2
  31.9 0.0 copy-start.6
  31.9 5.8 %forward.1 = (bf16[16,128,128]{2,1,0:T(8,128)(2,1)S(1)}, bf16[16,128,512]{2,1,0:T(8,128)(2,1)S(1)}) custom-call(s32[1,1,96]{2,1,0:T(1,128)S(1)} %copy-done.3, s32[1,1,96]{2,1,0:T(1,128)S(1)} %copy-done.4, s32[1,1,96]{2,1,0:T(1,128)S(1)} %copy-done.5, s32[1,1]{1,0:T(1,128)S(6)} %copy.22.live, bf16[32,128,128]{2,1,0:T(8,128)(2,1)} %all-to-all-done.x, ...), custom_call_target="tpu_custom_call" | custom-call | tf_op jit(solution)/shard_map/forward/pallas_call | solution.py:115
  37.8 34.7 %all_to_all.25.parts = bf16[16,128,128]{2,1,0:T(8,128)(2,1)S(1)} all-to-all(bf16[16,128,128]{2,1,0:T(8,128)(2,1)S(1)} %get-tuple-element.9), channel_id=1, replica_groups=mesh['row'=32,'col'=16] {'col'}, dimensions={0} | all-to-all | bytes 1048576 | tf_op jit(solution)/shard_map/all_to_all | solution.py:127
  72.5 0.0 copy-done.2
  72.5 0.0 copy-done.6
  72.5 0.7 middle.1
  73.2 28.3 %all-gather = bf16[2048,128]{1,0:T(8,128)(2,1)S(1)} all-gather(bf16[128,128]{1,0:T(8,128)(2,1)S(1)} %get-tuple-element.11), channel_id=2, replica_groups=mesh['row'=32,'col'=16] {'col'}, dimensions={0}, use_global_device_ids=true | all-gather | bytes 557056 | tf_op jit(solution)/shard_map/all_gather | solution.py:140
  101.5 5.4 %backward.1 = bf16[32,160,128]{2,1,0:T(8,128)(2,1)S(1)} custom-call(s32[1,1,96]{2,1,0:T(1,128)S(1)} %copy-done.3, s32[1,1,96]{2,1,0:T(1,128)S(1)} %copy-done.4, s32[1,1,96]{2,1,0:T(1,128)S(1)} %copy-done.5, s32[1,1]{1,0:T(1,128)S(6)} %copy.22.live, bf16[16,128,128]{2,1,0:T(8,128)(2,1)S(1)} %bitcast.8, bf16[1,1,96,128,128]{4,3,2,1,0:T(8,128)(2,1)S(1)} %copy-done, ...), custom_call_target="tpu_custom_call" | custom-call | tf_op jit(solution)/shard_map/backward/pallas_call | solution.py:141
  106.9 39.8 %all_to_all.26 = bf16[32,160,128]{2,1,0:T(8,128)(2,1)S(1)} all-to-all(bf16[32,160,128]{2,1,0:T(8,128)(2,1)S(1)} %backward.1), channel_id=1, replica_groups=mesh['row'=32,'col'=16] {'row'}, dimensions={0} | all-to-all | bytes 2621440 | tf_op jit(solution)/shard_map/all_to_all | solution.py:154
  146.6 0.2 convert_reduce_fusion
  146.9 16.2 %all_to_all.27 = f32[16,24,128]{2,1,0:T(8,128)S(1)} all-to-all(f32[16,24,128]{2,1,0:T(8,128)S(1)} %broadcast_in_dim.7), channel_id=1, replica_groups=mesh['row'=32,'col'=16] {'col'}, dimensions={0} | all-to-all | bytes 393216 | tf_op jit(solution)/shard_map/all_to_all | solution.py:106
  163.1 0.8 broadcast_in_dim.8
  163.9 7.1 %all-to-all-start.4 = ((f32[32,24,128]{2,1,0:T(8,128)}), f32[32,24,128]{2,1,0:T(8,128)S(1)}, u32[]{:S(2)}, u32[]{:S(2)}) async-start(f32[32,24,128]{2,1,0:T(8,128)} %broadcast_in_dim.8), calls=%async_computation.4 | async-start | bytes 786432 | tf_op jit(solution)/shard_map/all_to_all | solution.py:106
  171.0 0.7 copy.20
  171.7 9.6 %all-to-all-done.4 = f32[32,24,128]{2,1,0:T(8,128)S(1)} async-done(((f32[32,24,128]{2,1,0:T(8,128)}), f32[32,24,128]{2,1,0:T(8,128)S(1)}, u32[]{:S(2)}, u32[]{:S(2)}) %all-to-all-start.4) | async-done | bytes 393248 | tf_op jit(solution)/shard_map/all_to_all | solution.py:106
  181.3 0.8 copy.21
  182.1 0.6 slice_reduce_fusion
  (6 shorter events, 0.1 us)
Async XLA Ops:
  0.6 30.4 %copy-start.5 = (s32[1,1,96]{2,1,0:T(1,128)S(1)}, s32[1,1,96]{2,1,0:T(1,128)}, u32[]{:S(2)}) copy-start(s32[1,1,96]{2,1,0:T(1,128)} %rels.3) | copy-start | bytes 1156
  0.6 30.4 %copy-start.4 = (s32[1,1,96]{2,1,0:T(1,128)S(1)}, s32[1,1,96]{2,1,0:T(1,128)}, u32[]{:S(2)}) copy-start(s32[1,1,96]{2,1,0:T(1,128)} %cols.3) | copy-start | bytes 1156
  0.7 30.4 %copy-start.3 = (s32[1,1,96]{2,1,0:T(1,128)S(1)}, s32[1,1,96]{2,1,0:T(1,128)}, u32[]{:S(2)}) copy-start(s32[1,1,96]{2,1,0:T(1,128)} %rows.3) | copy-start | bytes 1156
  0.7 30.4 %copy-start = (bf16[1,1,96,128,128]{4,3,2,1,0:T(8,128)(2,1)S(1)}, bf16[1,1,96,128,128]{4,3,2,1,0:T(8,128)(2,1)}, u32[]{:S(2)}) copy-start(bf16[1,1,96,128,128]{4,3,2,1,0:T(8,128)(2,1)} %v.3) | copy-start | bytes 9437188
  2.8 28.2 %all-to-all-start = ((bf16[32,128,128]{2,1,0:T(8,128)(2,1)}), bf16[32,128,128]{2,1,0:T(8,128)(2,1)}, u32[]{:S(2)}, u32[]{:S(2)}) async-start(bf16[32,128,128]{2,1,0:T(8,128)(2,1)} %broadcast_in_dim.6), calls=%async_computation | async-start | bytes 2097152 | tf_op jit(solution)/shard_map/all_to_all | solution.py:106
  31.0 0.9 copy-start.1
  31.9 40.6 %copy-start.2 = (bf16[128,128]{1,0:T(8,128)(2,1)S(1)}, bf16[128,128]{1,0:T(8,128)(2,1)}, u32[]{:S(2)}) copy-start(bf16[128,128]{1,0:T(8,128)(2,1)} %out_grad.1) | copy-start | bytes 98308
  31.9 40.6 %copy-start.6 = (f32[128]{0:T(128)S(1)}, f32[128]{0:T(128)}, u32[]{:S(2)}) copy-start(f32[128]{0:T(128)} %param.16) | copy-start | bytes 1540
  163.9 17.4 %all-to-all-start.4 = ((f32[32,24,128]{2,1,0:T(8,128)}), f32[32,24,128]{2,1,0:T(8,128)S(1)}, u32[]{:S(2)}, u32[]{:S(2)}) async-start(f32[32,24,128]{2,1,0:T(8,128)} %broadcast_in_dim.8), calls=%async_computation.4 | async-start | bytes 786432 | tf_op jit(solution)/shard_map/all_to_all | solution.py:106

commit v2 on v1

v2 whole, which is shorter than its diff:
```python
import jax
import jax.numpy as jnp
from jax import lax
from jax.experimental import pallas as pl
from jax.experimental.pallas import tpu as pltpu
from jax.sharding import PartitionSpec as P

RB = 16
CB = 32
RELS = 4
B = 128
STEP = 4
SLICE = CB // RELS
PART = B // SLICE


def dot(a, b):
    return jnp.dot(a, b, preferred_element_type=jnp.float32)


def forward_kernel(rows, cols, rels, live, x, v, w, z, p, acc):
    acc[...] = jnp.zeros_like(acc)
    count = live[0, 0]

    def group(step, carry):
        first = step * STEP
        for u in range(STEP):
            k = first + u
            row = rows[0, 0, k]
            lane = pl.multiple_of(rels[0, 0, k] * B, B)
            product = dot(v[0, 0, k], x[cols[0, 0, k]])
            product = jnp.where(k < count, product, 0.0)
            acc[row, :, pl.ds(lane, B)] += product
        return carry

    lax.fori_loop(0, (count + STEP - 1) // STEP, group, 0)
    wide = w[...]

    def finish(row, carry):
        held = acc[row].astype(jnp.bfloat16)
        p[row] = held
        z[row] = dot(held, wide).astype(jnp.bfloat16)
        return carry

    lax.fori_loop(0, RB, finish, 0, unroll=2)


def middle_kernel(parts, bias, out_grad, activated, grad_t):
    z = parts[0].astype(jnp.float32)
    for c in range(1, parts.shape[0]):
        z = z + parts[c].astype(jnp.float32)
    z = z + bias[...]
    s = jax.nn.sigmoid(z)
    activated[...] = (z * s).astype(jnp.bfloat16)
    slope = s * (1.0 + z * (1.0 - s))
    grad = (out_grad[...].astype(jnp.float32) * slope).astype(jnp.bfloat16)
    grad_t[...] = grad.astype(jnp.float32).T.astype(jnp.bfloat16)


def weight_kernel(grad_t, p, out, total):
    total[...] = jnp.zeros_like(total)

    def add(row, carry):
        total[...] += dot(grad_t[row], p[row])
        return carry

    lax.fori_loop(0, RB, add, 0, unroll=2)
    for b in range(CB):
        rel, part = b // SLICE, b % SLICE
        out[b] = total[part * PART : (part + 1) * PART, rel * B : (rel + 1) * B]


def spread_kernel(parts, out):
    total = parts[0]
    for r in range(1, parts.shape[0]):
        total = total + parts[r]
    for c in range(out.shape[0]):
        out[c] = total


def backward_kernel(rows, cols, rels, live, grad_t, v, w, out, bias_sum, back, acc):
    acc[...] = jnp.zeros_like(acc)
    wide = w[...]
    count = live[0, 0]
    ones = jnp.ones((8, B), jnp.bfloat16)
    bias_sum[...] = jnp.zeros_like(bias_sum)

    def start(row, carry):
        g = grad_t[row]
        back[row] = dot(wide, g).astype(jnp.bfloat16)
        bias_sum[...] += lax.dot_general(
            ones, g, (((1,), (1,)), ((), ())), preferred_element_type=jnp.float32
        )
        return carry

    lax.fori_loop(0, RB, start, 0, unroll=2)

    def group(step, carry):
        first = step * STEP
        for u in range(STEP):
            k = first + u
            at = pl.multiple_of(rels[0, 0, k] * B, B)
            product = dot(back[rows[0, 0, k], pl.ds(at, B), :], v[0, 0, k])
            product = jnp.where(k < count, product, 0.0)
            acc[cols[0, 0, k]] += product
        return carry

    lax.fori_loop(0, (count + STEP - 1) // STEP, group, 0)
    out[:, :B, :] = acc[...].astype(jnp.bfloat16)
    out[:, B:, :] = jnp.zeros((CB, 2 * PART, B), jnp.bfloat16)


def append_kernel(sent, parts, bias_sum, out):
    total = parts[0]
    for c in range(1, parts.shape[0]):
        total = total + parts[c]
    row = lax.broadcasted_iota(jnp.int32, (PART, B), 0)
    term = jnp.broadcast_to(bias_sum[0:1, :], (PART, B))
    high = term.astype(jnp.bfloat16).astype(jnp.float32)
    pair = jnp.where(row == 0, high, jnp.where(row == 1, term - high, 0.0))
    both = jnp.concatenate([total, pair], axis=0).astype(jnp.bfloat16)
    for r in range(CB):
        out[r, B:, :] = both


VMEM = pl.BlockSpec(memory_space=pltpu.VMEM)
SMEM = pl.BlockSpec(memory_space=pltpu.SMEM)
PARAMS = pltpu.CompilerParams(vmem_limit_bytes=32 * 1024 * 1024)


def swap(blocks, axis):
    return lax.all_to_all(blocks, axis, 0, 0, tiled=True)


def on_device(
    features, tile_values, tile_rows, tile_cols, tile_rels, live, weights, bias, out_grad
):
    ids = (tile_rows, tile_cols, tile_rels, live)
    wide_weights = weights.reshape(RELS * B, B)
    blocks = swap(jnp.broadcast_to(features[None], (CB, B, B)), "row")
    z_parts, p_wide = pl.pallas_call(
        forward_kernel,
        out_shape=(
            jax.ShapeDtypeStruct((RB, B, B), jnp.bfloat16),
            jax.ShapeDtypeStruct((RB, B, RELS * B), jnp.bfloat16),
        ),
        in_specs=[SMEM] * 4 + [VMEM] * 3,
        out_specs=(VMEM, VMEM),
        scratch_shapes=[pltpu.VMEM((RB, B, RELS * B), jnp.float32)],
        compiler_params=PARAMS,
        name="forward",
    )(*ids, blocks, tile_values, wide_weights)
    activated, grad_t = pl.pallas_call(
        middle_kernel,
        out_shape=(
            jax.ShapeDtypeStruct((B, B), jnp.bfloat16),
            jax.ShapeDtypeStruct((B, B), jnp.bfloat16),
        ),
        in_specs=[VMEM] * 3,
        out_specs=(VMEM,) * 2,
        compiler_params=PARAMS,
        name="middle",
    )(swap(z_parts, "col"), bias.reshape(1, B), out_grad)
    grad_all = lax.all_gather(grad_t, "col", axis=0, tiled=False)
    weight_parts = pl.pallas_call(
        weight_kernel,
        out_shape=jax.ShapeDtypeStruct((CB, PART, B), jnp.float32),
        in_specs=[VMEM] * 2,
        out_specs=VMEM,
        scratch_shapes=[pltpu.VMEM((B, RELS * B), jnp.float32)],
        compiler_params=PARAMS,
        name="weight",
    )(grad_all, p_wide)
    own = pl.pallas_call(
        spread_kernel,
        out_shape=jax.ShapeDtypeStruct((RB, PART, B), jnp.float32),
        in_specs=[VMEM],
        out_specs=VMEM,
        compiler_params=PARAMS,
        name="spread",
    )(swap(weight_parts, "row"))
    own = swap(own, "col")
    sent, bias_sum = pl.pallas_call(
        backward_kernel,
        out_shape=(
            jax.ShapeDtypeStruct((CB, B + 2 * PART, B), jnp.bfloat16),
            jax.ShapeDtypeStruct((8, B), jnp.float32),
        ),
        in_specs=[SMEM] * 4 + [VMEM] * 3,
        out_specs=(VMEM, VMEM),
        scratch_shapes=[
            pltpu.VMEM((RB, RELS * B, B), jnp.bfloat16),
            pltpu.VMEM((CB, B, B), jnp.float32),
        ],
        compiler_params=PARAMS,
        cost_estimate=pl.CostEstimate(flops=10**9, bytes_accessed=10**7, transcendentals=0),
        name="backward",
    )(*ids, grad_all, tile_values, wide_weights)
    sent = pl.pallas_call(
        append_kernel,
        out_shape=jax.ShapeDtypeStruct(sent.shape, sent.dtype),
        in_specs=[VMEM] * 3,
        out_specs=VMEM,
        input_output_aliases={0: 0},
        compiler_params=PARAMS,
        name="append",
    )(sent, own, bias_sum)
    received = swap(sent, "row")
    feature_grad = jnp.sum(received[:, :B].astype(jnp.float32), axis=0).T
    every = received[:, B : B + PART].astype(jnp.float32)
    weight_grad = every.reshape(RELS, B, B).transpose(0, 2, 1)
    bias_grad = jnp.sum(received[:, B + PART : B + PART + 2].astype(jnp.float32), axis=(0, 1))
    return (activated, feature_grad, weight_grad, bias_grad)


def solution(mesh):
    placed = (
        P(("row", "col"), None),
        P("row", "col", None, None, None),
        P("row", "col", None),
        P("row", "col", None),
        P("row", "col", None),
        P("row", "col"),
        P(),
        P(),
        P(("row", "col"), None),
    )
    return jax.shard_map(
        on_device,
        mesh=mesh,
        in_specs=placed,
        out_specs=(P(("row", "col"), None), P(("row", "col"), None), P(), P()),
        check_vma=False,
    )
```

time: 183 us -> 178 us (0.973)
  waiting for transfers between devices: 26 us -> 19.4 us
  Pallas kernels: 11.9 us -> 18.3 us
  blocking collectives: 119 us -> 114 us
  local copies, waits for them, and re-layouts: 5.46 us -> 8.08 us
  starting transfers between devices: 18.2 us -> 15.6 us
    all_to_all x2, waiting for transfers between devices: 26 us -> 19.4 us  [swap(): return lax.all_to_all(blocks, axis, 0, 0, tiled=True)]
    all_to_all x3, blocking collectives: 90.7 us -> 85.5 us  [swap(): return lax.all_to_all(blocks, axis, 0, 0, tiled=True)]
    pallas_call x1 -> x4, Pallas kernels: 5.37 us -> 9.46 us  [the longest x1 6.97 us: on_device(): pl.pallas_call(backward_kernel, out_shape=(jax.ShapeDtypeStruct((CB, B +...]
    all_to_all x2, starting transfers between devices: 18.2 us -> 15.6 us  [swap(): return lax.all_to_all(blocks, axis, 0, 0, tiled=True)]
    unnamed x16 -> x25, local copies, waits for them, and re-layouts: 2.49 us -> 5.08 us
    pallas_call x1, Pallas kernels: 5.81 us -> 8.17 us  [on_device(): pl.pallas_call(forward_kernel, out_shape=(jax.ShapeDtypeStruct((RB, B, B)...]
  transfers between devices with their start and end apart: 2 -> 2, of which waited for: 2 -> 2; matrix products, arithmetic and copies ran while one was open for 0% -> 0% of each run, Pallas kernels for 0% -> 4%
where the time goes in v2:
time: 178 us; the launch traced here: 177 us
  blocking collectives  114 us (64%)
  waiting for transfers between devices  19.4 us (11%)
  Pallas kernels  18.3 us (10%)
  starting transfers between devices  15.6 us (9%)
  local copies, waits for them, and re-layouts  8.08 us (5%)
    all_to_all x3, blocking collectives, swap(): return lax.all_to_all(blocks, axis, 0, 0, tiled=True)  85.5 us
    all_gather x1, blocking collectives, on_device(): grad_all = lax.all_gather(grad_t, 'col', axis=0, tiled=False)  28.1 us
    all_to_all x2, waiting for transfers between devices, swap(): return lax.all_to_all(blocks, axis, 0, 0, tiled=True)  19.4 us
    all_to_all x2, starting transfers between devices, swap(): return lax.all_to_all(blocks, axis, 0, 0, tiled=True)  15.6 us
    pallas_call x1, Pallas kernels, on_device(): pl.pallas_call(forward_kernel, out_shape=(jax.ShapeDtypeStruct((RB, B, B)...  8.17 us
    pallas_call x1, Pallas kernels, on_device(): pl.pallas_call(backward_kernel, out_shape=(jax.ShapeDtypeStruct((CB, B +...  6.97 us
    unnamed x25, local copies, waits for them, and re-layouts  5.08 us
  transfers between devices with their start and end apart: 2, of which 2 were waited for; matrix products, arithmetic and copies ran while one was open for 0% of the time, Pallas kernels for 4%

profile of v2, /device:TPU:1, one launch (start us, length us, event | category | flops | bytes accessed | tf_op | source)
XLA Modules:
  0.0 177.2 jit_solution(13175404425506954119)
XLA Ops:
  0.6 0.0 copy-start
  0.6 2.1 %broadcast_in_dim.2 = bf16[32,128,128]{2,1,0:T(8,128)(2,1)} broadcast(bf16[128,128]{1,0:T(8,128)(2,1)} %param.9), dimensions={1,2} | broadcast | bytes 1081344 | tf_op jit(solution)/shard_map/broadcast_in_dim | solution.py:140
  2.8 0.0 copy-start.8
  2.8 0.0 copy-start.9
  2.8 0.0 copy-start.10
  2.8 11.3 %all-to-all-start = ((bf16[32,128,128]{2,1,0:T(8,128)(2,1)}), bf16[32,128,128]{2,1,0:T(8,128)(2,1)}, u32[]{:S(2)}, u32[]{:S(2)}) async-start(bf16[32,128,128]{2,1,0:T(8,128)(2,1)} %broadcast_in_dim.2), calls=%async_computation | async-start | bytes 2097152 | tf_op jit(solution)/shard_map/all_to_all | solution.py:132
  14.7 16.4 %all-to-all-done.x = bf16[32,128,128]{2,1,0:T(8,128)(2,1)} async-done(((bf16[32,128,128]{2,1,0:T(8,128)(2,1)}), bf16[32,128,128]{2,1,0:T(8,128)(2,1)}, u32[]{:S(2)}, u32[]{:S(2)}) %all-to-all-start) | async-done | bytes 1048608 | tf_op jit(solution)/shard_map/all_to_all | solution.py:132
  31.1 0.0 copy-done
  31.1 0.0 copy-done.8
  31.1 0.0 copy-done.9
  31.1 0.0 copy-done.10
  31.1 0.0 copy-start.5
  31.1 0.9 copy-done.5
  32.0 0.0 copy-start.7
  32.0 0.0 copy-start.11
  32.0 8.2 %forward.1 = (bf16[16,128,128]{2,1,0:T(8,128)(2,1)S(1)}, bf16[16,128,512]{2,1,0:T(8,128)(2,1)S(1)}) custom-call(s32[1,1,96]{2,1,0:T(1,128)S(1)} %copy-done.8, s32[1,1,96]{2,1,0:T(1,128)S(1)} %copy-done.9, s32[1,1,96]{2,1,0:T(1,128)S(1)} %copy-done.10, s32[1,1]{1,0:T(1,128)S(6)} %copy.18.live, bf16[32,128,128]{2,1,0:T(8,128)(2,1)} %all-to-all-done.x, ...), custom_call_target="tpu_custom_call" | custom-call | tf_op jit(solution)/shard_map/forward/pallas_call | solution.py:141
  40.2 33.8 %all_to_all.25.parts = bf16[16,128,128]{2,1,0:T(8,128)(2,1)S(1)} all-to-all(bf16[16,128,128]{2,1,0:T(8,128)(2,1)S(1)} %get-tuple-element.10), channel_id=1, replica_groups=mesh['row'=32,'col'=16] {'col'}, dimensions={0} | all-to-all | bytes 1048576 | tf_op jit(solution)/shard_map/all_to_all | solution.py:132
  74.0 0.0 copy-done.7
  74.0 0.0 copy-done.11
  74.0 0.7 middle.1
  74.7 28.1 %all-gather = bf16[2048,128]{1,0:T(8,128)(2,1)S(1)} all-gather(bf16[128,128]{1,0:T(8,128)(2,1)S(1)} %get-tuple-element.12), channel_id=2, replica_groups=mesh['row'=32,'col'=16] {'col'}, dimensions={0}, use_global_device_ids=true | all-gather | bytes 557056 | tf_op jit(solution)/shard_map/all_gather | solution.py:164
  102.8 0.0 copy-start.3
  102.8 0.0 copy-start.6
  102.8 1.8 weight.1
  104.6 0.0 copy-done.3
  104.6 25.4 %all_to_all.26.parts = f32[32,16,128]{2,1,0:T(8,128)S(1)} all-to-all(f32[32,16,128]{2,1,0:T(8,128)S(1)} %weight.1), channel_id=1, replica_groups=mesh['row'=32,'col'=16] {'row'}, dimensions={0} | all-to-all | bytes 524288 | tf_op jit(solution)/shard_map/all_to_all | solution.py:132
  130.0 0.7 spread.1
  130.7 4.3 %all-to-all-start.3 = ((f32[16,16,128]{2,1,0:T(8,128)}), f32[16,16,128]{2,1,0:T(8,128)S(1)}, u32[]{:S(2)}, u32[]{:S(2)}) async-start(f32[16,16,128]{2,1,0:T(8,128)} %spread.1), calls=%async_computation.3 | async-start | bytes 262144 | tf_op jit(solution)/shard_map/all_to_all | solution.py:132
  135.0 0.0 copy-done.6
  135.0 0.0 copy-start.4
  135.1 1.0 copy-done.4
  136.1 7.0 %backward.1 = (bf16[32,160,128]{2,1,0:T(8,128)(2,1)S(1)}, f32[8,128]{1,0:T(8,128)S(1)}) custom-call(s32[1,1,96]{2,1,0:T(1,128)S(1)} %copy-done.8, s32[1,1,96]{2,1,0:T(1,128)S(1)} %copy-done.9, s32[1,1,96]{2,1,0:T(1,128)S(1)} %copy-done.10, s32[1,1]{1,0:T(1,128)S(6)} %copy.18.live, bf16[16,128,128]{2,1,0:T(8,128)(2,1)S(1)} %bitcast.10, ...), custom_call_target="tpu_custom_call" | custom-call | flops 1000000000 | bytes 10000000 | tf_op jit(solution)/shard_map/backward/pallas_call | solution.py:183
  143.1 0.0 copy-start.1
  143.1 1.1 copy-done.1
  144.1 3.0 %all-to-all-done.3.parts = f32[16,16,128]{2,1,0:T(8,128)S(1)} async-done(((f32[16,16,128]{2,1,0:T(8,128)}), f32[16,16,128]{2,1,0:T(8,128)S(1)}, u32[]{:S(2)}, u32[]{:S(2)}) %all-to-all-start.3) | async-done | bytes 131104 | tf_op jit(solution)/shard_map/all_to_all | solution.py:132
  147.2 0.0 copy-start.2
  147.2 1.3 copy-done.2
  148.5 26.4 %all_to_all.27 = bf16[32,160,128]{2,1,0:T(8,128)(2,1)S(1)} all-to-all(bf16[32,160,128]{2,1,0:T(8,128)(2,1)S(1)} %append.1), channel_id=1, replica_groups=mesh['row'=32,'col'=16] {'row'}, dimensions={0} | all-to-all | bytes 2621440 | tf_op jit(solution)/shard_map/all_to_all | solution.py:132
  174.9 0.2 convert_reduce_fusion
  175.1 0.7 copy.16
  175.8 0.8 copy.15
  176.7 0.6 convert_reduce_fusion.1
  (3 shorter events, 0.1 us)
Async XLA Ops:
  0.6 30.5 %copy-start = (bf16[1,1,96,128,128]{4,3,2,1,0:T(8,128)(2,1)S(1)}, bf16[1,1,96,128,128]{4,3,2,1,0:T(8,128)(2,1)}, u32[]{:S(2)}) copy-start(bf16[1,1,96,128,128]{4,3,2,1,0:T(8,128)(2,1)} %v.3) | copy-start | bytes 9437188
  2.8 28.3 %copy-start.8 = (s32[1,1,96]{2,1,0:T(1,128)S(1)}, s32[1,1,96]{2,1,0:T(1,128)}, u32[]{:S(2)}) copy-start(s32[1,1,96]{2,1,0:T(1,128)} %rows.3) | copy-start | bytes 1156
  2.8 28.3 %copy-start.9 = (s32[1,1,96]{2,1,0:T(1,128)S(1)}, s32[1,1,96]{2,1,0:T(1,128)}, u32[]{:S(2)}) copy-start(s32[1,1,96]{2,1,0:T(1,128)} %cols.3) | copy-start | bytes 1156
  2.8 28.3 %copy-start.10 = (s32[1,1,96]{2,1,0:T(1,128)S(1)}, s32[1,1,96]{2,1,0:T(1,128)}, u32[]{:S(2)}) copy-start(s32[1,1,96]{2,1,0:T(1,128)} %rels.3) | copy-start | bytes 1156
  2.8 28.3 %all-to-all-start = ((bf16[32,128,128]{2,1,0:T(8,128)(2,1)}), bf16[32,128,128]{2,1,0:T(8,128)(2,1)}, u32[]{:S(2)}, u32[]{:S(2)}) async-start(bf16[32,128,128]{2,1,0:T(8,128)(2,1)} %broadcast_in_dim.2), calls=%async_computation | async-start | bytes 2097152 | tf_op jit(solution)/shard_map/all_to_all | solution.py:132
  31.1 0.9 copy-start.5
  32.0 42.0 %copy-start.7 = (bf16[128,128]{1,0:T(8,128)(2,1)S(1)}, bf16[128,128]{1,0:T(8,128)(2,1)}, u32[]{:S(2)}) copy-start(bf16[128,128]{1,0:T(8,128)(2,1)} %out_grad.1) | copy-start | bytes 98308
  32.0 42.0 %copy-start.11 = (f32[128]{0:T(128)S(1)}, f32[128]{0:T(128)}, u32[]{:S(2)}) copy-start(f32[128]{0:T(128)} %param.16) | copy-start | bytes 1540
  102.8 1.8 %copy-start.3 = (bf16[2048,128]{1,0:T(8,128)(2,1)}, bf16[2048,128]{1,0:T(8,128)(2,1)S(1)}, u32[]{:S(2)}) copy-start(bf16[2048,128]{1,0:T(8,128)(2,1)S(1)} %all-gather) | copy-start | bytes 1572868
  102.8 32.2 %copy-start.6 = (bf16[4,128,128]{2,1,0:T(8,128)(2,1)S(1)}, bf16[4,128,128]{2,1,0:T(8,128)(2,1)}, u32[]{:S(2)}) copy-start(bf16[4,128,128]{2,1,0:T(8,128)(2,1)} %param.15) | copy-start | bytes 393220
  130.7 16.5 %all-to-all-start.3 = ((f32[16,16,128]{2,1,0:T(8,128)}), f32[16,16,128]{2,1,0:T(8,128)S(1)}, u32[]{:S(2)}, u32[]{:S(2)}) async-start(f32[16,16,128]{2,1,0:T(8,128)} %spread.1), calls=%async_computation.3 | async-start | bytes 262144 | tf_op jit(solution)/shard_map/all_to_all | solution.py:132
  135.0 1.0 copy-start.4
  143.1 1.1 copy-start.1
  147.2 1.3 copy-start.2

commit v3 on v2

v3 whole, which is shorter than its diff:
```python
import jax
import jax.numpy as jnp
from jax import lax
from jax.experimental import pallas as pl
from jax.experimental.pallas import tpu as pltpu
from jax.sharding import PartitionSpec as P

RB = 16
CB = 32
RELS = 4
B = 128
STEP = 24
TILES = 96
BATCH = 4
GROUPS = TILES // STEP
SLICE = CB // RELS
PART = B // SLICE


def dot(a, b):
    return jnp.dot(a, b, preferred_element_type=jnp.float32)


def place(ids, k):
    code = ids[0, 0, k]
    row, col = code & (RB - 1), (code >> 4) & (CB - 1)
    return row, col, pl.multiple_of((code >> 9) * B, B)


def forward_kernel(ids, live, core, own_x, other_x, v, w, z, p, x, acc, tiles, wide, sems):
    def chunk(g):
        span = pl.ds(g * STEP, STEP)
        return pltpu.make_async_copy(v.at[0, 0, span], tiles.at[span], sems.at[g])

    load_w = pltpu.make_async_copy(w, wide, sems.at[GROUPS])
    for g in range(GROUPS):
        chunk(g).start()
    load_w.start()
    acc[...] = jnp.zeros_like(acc)
    x[0] = own_x[...]
    x[1] = other_x[...]
    count = live[0, 0]
    mine = core[0, 0]

    def group(g, carry):
        chunk(g).wait()
        first = g * STEP

        @pl.when(first < count)
        def _():
            for u in range(STEP):
                k = first + u
                row, col, lane = place(ids, k)
                product = dot(tiles[k], x[(col & 1) ^ mine, col >> 1])
                product = jnp.where(k < count, product, 0.0)
                acc[row, :, pl.ds(lane, B)] += product

        return carry

    lax.fori_loop(0, GROUPS, group, 0)
    load_w.wait()

    def finish(i, carry):
        rows = pl.ds(i * BATCH, BATCH)
        held = acc[rows].astype(jnp.bfloat16)
        p[rows] = held
        part = dot(held.reshape(BATCH * B, RELS * B), wide[...])
        z[rows] = part.astype(jnp.bfloat16).reshape(BATCH, B, B)
        return carry

    lax.fori_loop(0, RB // BATCH, finish, 0, unroll=2)


def middle_kernel(parts, bias, out_grad, activated, grad_t):
    z = parts[0].astype(jnp.float32)
    for c in range(1, parts.shape[0]):
        z = z + parts[c].astype(jnp.float32)
    z = z + bias[...]
    s = jax.nn.sigmoid(z)
    activated[...] = (z * s).astype(jnp.bfloat16)
    slope = s * (1.0 + z * (1.0 - s))
    grad = (out_grad[...].astype(jnp.float32) * slope).astype(jnp.bfloat16)
    grad_t[...] = grad.astype(jnp.float32).T.astype(jnp.bfloat16)


def weight_kernel(grad_t, p, out, total):
    total[...] = jnp.zeros_like(total)

    def add(i, carry):
        g = jnp.concatenate([grad_t[2 * i], grad_t[2 * i + 1]], axis=1)
        total[...] += dot(g, p[pl.ds(2 * i, 2)].reshape(2 * B, RELS * B))
        return carry

    lax.fori_loop(0, RB // 2, add, 0, unroll=2)
    for b in range(CB):
        rel, part = b // SLICE, b % SLICE
        out[b] = total[part * PART : (part + 1) * PART, rel * B : (rel + 1) * B]


def spread_kernel(parts, out):
    total = parts[0]
    for r in range(1, parts.shape[0]):
        total = total + parts[r]
    total = total.astype(jnp.bfloat16)
    for c in range(out.shape[0]):
        out[c] = total


def backward_kernel(
    ids, live, core, grad_t, v, w, kept, given, bias_sum, back, acc, tiles, sems
):
    def chunk(g):
        span = pl.ds(g * STEP, STEP)
        return pltpu.make_async_copy(v.at[0, 0, span], tiles.at[span], sems.at[g])

    for g in range(GROUPS):
        chunk(g).start()
    acc[...] = jnp.zeros_like(acc)
    wide = w[...]
    count = live[0, 0]
    mine = core[0, 0]
    ones = jnp.ones((8, 2 * B), jnp.bfloat16)
    bias_sum[...] = jnp.zeros_like(bias_sum)

    def start(i, carry):
        g = jnp.concatenate([grad_t[2 * i], grad_t[2 * i + 1]], axis=1)
        both = dot(wide, g).astype(jnp.bfloat16)
        back[2 * i] = both[:, :B]
        back[2 * i + 1] = both[:, B:]
        bias_sum[...] += lax.dot_general(
            ones, g, (((1,), (1,)), ((), ())), preferred_element_type=jnp.float32
        )
        return carry

    lax.fori_loop(0, RB // 2, start, 0, unroll=2)

    def group(g, carry):
        chunk(g).wait()
        first = g * STEP

        @pl.when(first < count)
        def _():
            for u in range(STEP):
                k = first + u
                row, col, at = place(ids, k)
                product = dot(back[row, pl.ds(at, B), :], tiles[k])
                product = jnp.where(k < count, product, 0.0)
                acc[(col & 1) ^ mine, col >> 1] += product

        return carry

    lax.fori_loop(0, GROUPS, group, 0)
    kept[...] = acc[0].astype(jnp.bfloat16)
    given[...] = acc[1].astype(jnp.bfloat16)


def join_kernel(kept, taken, out):
    total = kept[...].astype(jnp.float32) + taken[...].astype(jnp.float32)
    out[:, :B, :] = total.astype(jnp.bfloat16)
    out[:, B:, :] = jnp.zeros((out.shape[0], 3 * PART, B), jnp.bfloat16)


def total_kernel(parts, bias_sum, out):
    total = parts[0].astype(jnp.float32)
    for c in range(1, parts.shape[0]):
        total = total + parts[c].astype(jnp.float32)
    out[:PART] = total.astype(jnp.bfloat16)
    row = lax.broadcasted_iota(jnp.int32, (PART, B), 0)
    term = jnp.broadcast_to(bias_sum[0:1, :], (PART, B))
    high = term.astype(jnp.bfloat16).astype(jnp.float32)
    pair = jnp.where(row == 0, high, jnp.where(row == 1, term - high, 0.0))
    out[PART:] = pair.astype(jnp.bfloat16)


def append_kernel(core, sent, own, other, out):
    first = core[0, 0] == 0
    mine = own[...].astype(jnp.float32)
    theirs = other[...].astype(jnp.float32)
    low = jnp.where(first, mine, theirs)
    high = jnp.where(first, theirs, mine)
    row = lax.broadcasted_iota(jnp.int32, (PART, B), 0)
    second = jnp.concatenate([high[PART + 8 :], high[PART : PART + 8]], axis=0)
    pair = jnp.where(row < 8, low[PART:], second)
    rows = jnp.concatenate([low[:PART], high[:PART], pair], axis=0).astype(jnp.bfloat16)
    for r in range(out.shape[0]):
        out[r, B:, :] = rows


def final_kernel(received, feature_grad, weight_grad, bias_grad):
    total = received[0, :B].astype(jnp.float32)
    pair = received[0, B + 2 * PART :].astype(jnp.float32)
    for r in range(1, received.shape[0]):
        total = total + received[r, :B].astype(jnp.float32)
        pair = pair + received[r, B + 2 * PART :].astype(jnp.float32)
    feature_grad[...] = total.T
    bias_grad[...] = jnp.sum(pair, axis=0, keepdims=True)
    each = SLICE // 2
    for rel in range(RELS):
        parts = [received[rel * each + i, B : B + 2 * PART] for i in range(each)]
        weight_grad[rel] = jnp.concatenate(parts, axis=0).astype(jnp.float32).T


VMEM = pl.BlockSpec(memory_space=pltpu.VMEM)
SMEM = pl.BlockSpec(memory_space=pltpu.SMEM)
ANY = pl.BlockSpec(memory_space=pl.ANY)
WIDE = pltpu.CompilerParams(vmem_limit_bytes=48 * 1024 * 1024)
PARAMS = pltpu.CompilerParams(vmem_limit_bytes=32 * 1024 * 1024)


def swap(blocks, axis, groups=None):
    return lax.all_to_all(blocks, axis, 0, 0, tiled=True, axis_index_groups=groups)


def other_core(block):
    return lax.ppermute(block, "row", [(r, r ^ 1) for r in range(CB)])


def on_device(
    features, tile_values, tile_rows, tile_cols, tile_rels, live, weights, bias, out_grad
):
    ids = tile_rows + (tile_cols << 4) + (tile_rels << 9)
    wide_weights = weights.reshape(RELS * B, B)
    chips = CB // 2
    same_core = [[2 * chip + core for chip in range(chips)] for core in range(2)]
    core = jnp.reshape(lax.axis_index("row") % 2, (1, 1)).astype(jnp.int32)
    own_x = swap(jnp.broadcast_to(features[None], (chips, B, B)), "row", same_core)
    other_x = other_core(own_x)
    z_parts, p_wide = pl.pallas_call(
        forward_kernel,
        out_shape=(
            jax.ShapeDtypeStruct((RB, B, B), jnp.bfloat16),
            jax.ShapeDtypeStruct((RB, B, RELS * B), jnp.bfloat16),
        ),
        in_specs=[SMEM] * 3 + [VMEM] * 2 + [ANY] * 2,
        out_specs=(VMEM, VMEM),
        scratch_shapes=[
            pltpu.VMEM((2, chips, B, B), jnp.bfloat16),
            pltpu.VMEM((RB, B, RELS * B), jnp.float32),
            pltpu.VMEM((TILES, B, B), jnp.bfloat16),
            pltpu.VMEM((RELS * B, B), jnp.bfloat16),
            pltpu.SemaphoreType.DMA((GROUPS + 1,)),
        ],
        compiler_params=WIDE,
        name="forward",
    )(ids, live, core, own_x, other_x, tile_values, wide_weights)
    activated, grad_t = pl.pallas_call(
        middle_kernel,
        out_shape=(
            jax.ShapeDtypeStruct((B, B), jnp.bfloat16),
            jax.ShapeDtypeStruct((B, B), jnp.bfloat16),
        ),
        in_specs=[VMEM] * 3,
        out_specs=(VMEM,) * 2,
        compiler_params=PARAMS,
        name="middle",
    )(swap(z_parts, "col"), bias.reshape(1, B), out_grad)
    grad_all = lax.all_gather(grad_t, "col", axis=0, tiled=False)
    weight_parts = pl.pallas_call(
        weight_kernel,
        out_shape=jax.ShapeDtypeStruct((CB, PART, B), jnp.float32),
        in_specs=[VMEM] * 2,
        out_specs=VMEM,
        scratch_shapes=[pltpu.VMEM((B, RELS * B), jnp.float32)],
        compiler_params=PARAMS,
        name="weight",
    )(grad_all, p_wide)
    weight_parts = swap(weight_parts, "row")
    kept, given, bias_sum = pl.pallas_call(
        backward_kernel,
        out_shape=(
            jax.ShapeDtypeStruct((chips, B, B), jnp.bfloat16),
            jax.ShapeDtypeStruct((chips, B, B), jnp.bfloat16),
            jax.ShapeDtypeStruct((8, B), jnp.float32),
        ),
        in_specs=[SMEM] * 3 + [VMEM, ANY, VMEM],
        out_specs=(VMEM,) * 3,
        scratch_shapes=[
            pltpu.VMEM((RB, RELS * B, B), jnp.bfloat16),
            pltpu.VMEM((2, chips, B, B), jnp.float32),
            pltpu.VMEM((TILES, B, B), jnp.bfloat16),
            pltpu.SemaphoreType.DMA((GROUPS,)),
        ],
        compiler_params=PARAMS,
        cost_estimate=pl.CostEstimate(flops=10**9, bytes_accessed=10**7, transcendentals=0),
        name="backward",
    )(ids, live, core, grad_all, tile_values, wide_weights)
    taken = other_core(given)
    own = pl.pallas_call(
        spread_kernel,
        out_shape=jax.ShapeDtypeStruct((RB, PART, B), jnp.bfloat16),
        in_specs=[VMEM],
        out_specs=VMEM,
        compiler_params=PARAMS,
        name="spread",
    )(weight_parts)
    own = swap(own, "col")
    sent = pl.pallas_call(
        join_kernel,
        out_shape=jax.ShapeDtypeStruct((chips, B + 3 * PART, B), jnp.bfloat16),
        in_specs=[VMEM] * 2,
        out_specs=VMEM,
        compiler_params=PARAMS,
        cost_estimate=pl.CostEstimate(flops=10**6, bytes_accessed=10**6, transcendentals=0),
        name="join",
    )(kept, taken)
    own = pl.pallas_call(
        total_kernel,
        out_shape=jax.ShapeDtypeStruct((2 * PART, B), jnp.bfloat16),
        in_specs=[VMEM] * 2,
        out_specs=VMEM,
        compiler_params=PARAMS,
        name="total",
    )(own, bias_sum)
    sent = pl.pallas_call(
        append_kernel,
        out_shape=jax.ShapeDtypeStruct(sent.shape, sent.dtype),
        in_specs=[SMEM] + [VMEM] * 3,
        out_specs=VMEM,
        input_output_aliases={1: 0},
        compiler_params=PARAMS,
        name="append",
    )(core, sent, own, other_core(own))
    feature_grad, weight_grad, bias_grad = pl.pallas_call(
        final_kernel,
        out_shape=(
            jax.ShapeDtypeStruct((B, B), jnp.float32),
            jax.ShapeDtypeStruct((RELS, B, B), jnp.float32),
            jax.ShapeDtypeStruct((1, B), jnp.float32),
        ),
        in_specs=[VMEM],
        out_specs=(VMEM,) * 3,
        compiler_params=PARAMS,
        name="final",
    )(swap(sent, "row", same_core))
    return (activated, feature_grad, weight_grad, bias_grad.reshape(B))


def solution(mesh):
    placed = (
        P(("row", "col"), None),
        P("row", "col", None, None, None),
        P("row", "col", None),
        P("row", "col", None),
        P("row", "col", None),
        P("row", "col"),
        P(),
        P(),
        P(("row", "col"), None),
    )
    return jax.shard_map(
        on_device,
        mesh=mesh,
        in_specs=placed,
        out_specs=(P(("row", "col"), None), P(("row", "col"), None), P(), P()),
        check_vma=False,
    )
```

time: 178 us -> 165 us (0.927)
  waiting for transfers between devices: 19.4 us -> 0.8 us
  blocking collectives: 114 us -> 127 us
  Pallas kernels: 18.3 us -> 10.4 us
  starting transfers between devices: 15.6 us -> 22.5 us
  local copies, waits for them, and re-layouts: 8.08 us -> 1.77 us
    ppermute x0 -> x3, starting transfers between devices: none -> 22.5 us  [other_core(): return lax.ppermute(block, 'row', [(r, r ^ 1) for r in range(CB)])]
    all_to_all x2 -> x0, waiting for transfers between devices: 19.4 us -> none  [swap(): return lax.all_to_all(blocks, axis, 0, 0, tiled=True)]
    all_to_all x2 -> x0, starting transfers between devices: 15.6 us -> none  [swap(): return lax.all_to_all(blocks, axis, 0, 0, tiled=True)]
    all_to_all x3 -> x5, blocking collectives: 85.5 us -> 97.9 us  [swap(): lax.all_to_all(blocks, axis, 0, 0, tiled=True, axis_index_groups=groups)]
    unnamed x25 -> x8, local copies, waits for them, and re-layouts: 5.08 us -> 0.92 us
    pallas_call x1, Pallas kernels: 8.17 us -> 4.28 us  [on_device(): pl.pallas_call(forward_kernel, out_shape=(jax.ShapeDtypeStruct((RB, B, B)...]
    pallas_call x1 -> x4, Pallas kernels: 6.97 us -> 4.4 us  [the longest x1 3.35 us: on_device(): pl.pallas_call(backward_kernel, out_shape=(jax.ShapeDtypeStruct((chips, B...]
  transfers between devices with their start and end apart: 2 -> 3, of which waited for: 2 -> 2; matrix products, arithmetic and copies ran while one was open for 0% -> 0% of each run, Pallas kernels for 4% -> 1%
where the time goes in v3:
time: 165 us; the launch traced here: 164 us
  blocking collectives  127 us (77%)
  starting transfers between devices  22.5 us (14%)
  Pallas kernels  10.4 us (6%)
  local copies, waits for them, and re-layouts  1.77 us (1%)
    all_to_all x5, blocking collectives, swap(): lax.all_to_all(blocks, axis, 0, 0, tiled=True, axis_index_groups=groups)  97.9 us
    all_gather x1, blocking collectives, on_device(): grad_all = lax.all_gather(grad_t, 'col', axis=0, tiled=False)  28.7 us
    ppermute x3, starting transfers between devices, other_core(): return lax.ppermute(block, 'row', [(r, r ^ 1) for r in range(CB)])  22.5 us
    pallas_call x1, Pallas kernels, on_device(): pl.pallas_call(forward_kernel, out_shape=(jax.ShapeDtypeStruct((RB, B, B)...  4.28 us
    pallas_call x1, Pallas kernels, on_device(): pl.pallas_call(backward_kernel, out_shape=(jax.ShapeDtypeStruct((chips, B...  3.35 us
  transfers between devices with their start and end apart: 3, of which 2 were waited for; matrix products, arithmetic and copies ran while one was open for 0% of the time, Pallas kernels for 1%

profile of v3, /device:TPU:1, one launch (start us, length us, event | category | flops | bytes accessed | tf_op | source)
XLA Modules:
  0.0 164.2 jit_solution(17408650314001297493)
XLA Ops:
  0.6 0.9 broadcast_in_dim.2
  1.5 0.0 copy-start.2
  1.5 0.0 copy-start.3
  1.5 16.6 %all_to_all.25.own_x = bf16[16,128,128]{2,1,0:T(8,128)(2,1)S(1)} all-to-all(bf16[16,128,128]{2,1,0:T(8,128)(2,1)S(1)} %broadcast_in_dim.2), channel_id=1, replica_groups={{0,32,64,96,128,160,192,224,256,288,320,352,384,416,448,480},{16,48,80,..., dimensions={0} | all-to-all | bytes 1048576 | tf_op jit(solution)/shard_map/all_to_all | solution.py:211
  18.1 5.1 %collective-permute-start = (bf16[16,128,128]{2,1,0:T(8,128)(2,1)S(1)}, bf16[16,128,128]{2,1,0:T(8,128)(2,1)S(1)}, u32[]{:S(2)}, u32[]{:S(2)}) collective-permute-start(bf16[16,128,128]{2,1,0:T(8,128)(2,1)S(1)} %all_to_all.25.own_x), channel_id=1, source_target_pairs={{0,16},{16,0},{32,48},{48,32},{64,80},{80,64},{96,112},{112,96},{1... | collective-permute-start | bytes 1572872 | tf_op jit(solution)/shard_map/ppermute | solution.py:215
  23.9 0.7 shift-left_add_fusion.ids
  24.6 0.2 collective-permute-done.other_x
  24.8 0.0 copy-start.1
  24.8 0.9 copy-done.1
  25.7 0.0 copy-start
  25.7 4.3 %forward.1 = (bf16[16,128,128]{2,1,0:T(8,128)(2,1)S(1)}, bf16[16,128,512]{2,1,0:T(8,128)(2,1)S(1)}) custom-call(s32[1,1,96]{2,1,0:T(1,128)S(1)} %shift-left_add_fusion.ids, s32[1,1]{1,0:T(1,128)S(6)} %copy.15.live, s32[1,1]{1,0:T(1,128)} %bitcast.core, bf16[16,128,128]{2,1,0:T(8,128)(2,1)S(1)} %all_to_all.25.own_x, ...), custom_call_target="tpu_custom_call" | custom-call | tf_op jit(solution)/shard_map/forward/pallas_call | solution.py:228
  30.0 37.0 %all_to_all.26.parts = bf16[16,128,128]{2,1,0:T(8,128)(2,1)S(1)} all-to-all(bf16[16,128,128]{2,1,0:T(8,128)(2,1)S(1)} %get-tuple-element.14), channel_id=1, replica_groups=mesh['row'=32,'col'=16] {'col'}, dimensions={0} | all-to-all | bytes 1048576 | tf_op jit(solution)/shard_map/all_to_all | solution.py:211
  67.0 0.0 copy-done.2
  67.0 0.0 copy-done.3
  67.0 0.7 middle.1
  67.7 28.7 %all-gather = bf16[2048,128]{1,0:T(8,128)(2,1)S(1)} all-gather(bf16[128,128]{1,0:T(8,128)(2,1)S(1)} %get-tuple-element.16), channel_id=2, replica_groups=mesh['row'=32,'col'=16] {'col'}, dimensions={0}, use_global_device_ids=true | all-gather | bytes 557056 | tf_op jit(solution)/shard_map/all_gather | solution.py:257
  96.4 0.0 copy-done
  96.4 3.4 %backward.1 = (bf16[16,128,128]{2,1,0:T(8,128)(2,1)S(1)}, bf16[16,128,128]{2,1,0:T(8,128)(2,1)S(1)}, f32[8,128]{1,0:T(8,128)S(1)}) custom-call(s32[1,1,96]{2,1,0:T(1,128)S(1)} %shift-left_add_fusion.ids, s32[1,1]{1,0:T(1,128)S(6)} %copy.15.live, s32[1,1]{1,0:T(1,128)} %bitcast.core, bf16[16,128,128]{2,1,0:T(8,128)(2,1)S(1)} %bitcast.5, ...), custom_call_target="tpu_custom_call" | custom-call | flops 1000000000 | bytes 10000000 | tf_op jit(solution)/shard_map/backward/pallas_call | solution.py:268
  99.8 13.5 %collective-permute-start.1 = (bf16[16,128,128]{2,1,0:T(8,128)(2,1)S(1)}, bf16[16,128,128]{2,1,0:T(8,128)(2,1)S(1)}, u32[]{:S(2)}, u32[]{:S(2)}) collective-permute-start(bf16[16,128,128]{2,1,0:T(8,128)(2,1)S(1)} %get-tuple-element.18), channel_id=1, source_target_pairs={{0,16},{16,0},{32,48},{48,32},{64,80},{80,64},{96,112},{112,96},{1... | collective-permute-start | bytes 1572872 | tf_op jit(solution)/shard_map/ppermute | solution.py:215
  113.3 1.0 weight.1
  114.3 13.3 %all_to_all.27.parts = f32[32,16,128]{2,1,0:T(8,128)S(1)} all-to-all(f32[32,16,128]{2,1,0:T(8,128)S(1)} %weight.1), channel_id=1, replica_groups=mesh['row'=32,'col'=16] {'row'}, dimensions={0} | all-to-all | bytes 524288 | tf_op jit(solution)/shard_map/all_to_all | solution.py:211
  127.6 15.6 %all_to_all.28.parts = bf16[16,16,128]{2,1,0:T(8,128)(2,1)S(1)} all-to-all(bf16[16,16,128]{2,1,0:T(8,128)(2,1)S(1)} %spread.1), channel_id=1, replica_groups=mesh['row'=32,'col'=16] {'col'}, dimensions={0} | all-to-all | bytes 131072 | tf_op jit(solution)/shard_map/all_to_all | solution.py:211
  143.2 3.9 %collective-permute-start.2 = (bf16[32,128]{1,0:T(8,128)(2,1)S(1)}, bf16[32,128]{1,0:T(8,128)(2,1)S(1)}, u32[]{:S(2)}, u32[]{:S(2)}) collective-permute-start(bf16[32,128]{1,0:T(8,128)(2,1)S(1)} %total.1.own), channel_id=1, source_target_pairs={{0,16},{16,0},{32,48},{48,32},{64,80},{80,64},{96,112},{112,96},{1... | collective-permute-start | bytes 24584 | tf_op jit(solution)/shard_map/ppermute | solution.py:215
  147.1 0.0 collective-permute-done.1.taken
  147.1 0.1 join.1.sent
  147.3 0.6 collective-permute-done.2.other
  148.0 15.4 %all_to_all.29.received = bf16[16,176,128]{2,1,0:T(8,128)(2,1)S(1)} all-to-all(bf16[16,176,128]{2,1,0:T(8,128)(2,1)S(1)} %append.1), channel_id=1, replica_groups={{0,32,64,96,128,160,192,224,256,288,320,352,384,416,448,480},{16,48,80,..., dimensions={0} | all-to-all | bytes 1441792 | tf_op jit(solution)/shard_map/all_to_all | solution.py:211
  163.3 0.9 final.1
  (3 shorter events, 0.1 us)
Async XLA Ops:
  1.5 65.5 %copy-start.2 = (bf16[128,128]{1,0:T(8,128)(2,1)S(1)}, bf16[128,128]{1,0:T(8,128)(2,1)}, u32[]{:S(2)}) copy-start(bf16[128,128]{1,0:T(8,128)(2,1)} %out_grad.1) | copy-start | bytes 98308
  1.5 65.5 %copy-start.3 = (f32[128]{0:T(128)S(1)}, f32[128]{0:T(128)}, u32[]{:S(2)}) copy-start(f32[128]{0:T(128)} %param.16) | copy-start | bytes 1540
  18.1 6.7 %collective-permute-start = (bf16[16,128,128]{2,1,0:T(8,128)(2,1)S(1)}, bf16[16,128,128]{2,1,0:T(8,128)(2,1)S(1)}, u32[]{:S(2)}, u32[]{:S(2)}) collective-permute-start(bf16[16,128,128]{2,1,0:T(8,128)(2,1)S(1)} %all_to_all.25.own_x), channel_id=1, source_target_pairs={{0,16},{16,0},{32,48},{48,32},{64,80},{80,64},{96,112},{112,96},{1... | collective-permute-start | bytes 1572872 | tf_op jit(solution)/shard_map/ppermute | solution.py:215
  24.8 0.9 copy-start.1
  25.7 70.7 %copy-start = (bf16[1,1,96,128,128]{4,3,2,1,0:T(8,128)(2,1)S(1)}, bf16[1,1,96,128,128]{4,3,2,1,0:T(8,128)(2,1)}, u32[]{:S(2)}) copy-start(bf16[1,1,96,128,128]{4,3,2,1,0:T(8,128)(2,1)} %v.3) | copy-start | bytes 9437188
  99.8 47.4 %collective-permute-start.1 = (bf16[16,128,128]{2,1,0:T(8,128)(2,1)S(1)}, bf16[16,128,128]{2,1,0:T(8,128)(2,1)S(1)}, u32[]{:S(2)}, u32[]{:S(2)}) collective-permute-start(bf16[16,128,128]{2,1,0:T(8,128)(2,1)S(1)} %get-tuple-element.18), channel_id=1, source_target_pairs={{0,16},{16,0},{32,48},{48,32},{64,80},{80,64},{96,112},{112,96},{1... | collective-permute-start | bytes 1572872 | tf_op jit(solution)/shard_map/ppermute | solution.py:215
  143.2 4.7 %collective-permute-start.2 = (bf16[32,128]{1,0:T(8,128)(2,1)S(1)}, bf16[32,128]{1,0:T(8,128)(2,1)S(1)}, u32[]{:S(2)}, u32[]{:S(2)}) collective-permute-start(bf16[32,128]{1,0:T(8,128)(2,1)S(1)} %total.1.own), channel_id=1, source_target_pairs={{0,16},{16,0},{32,48},{48,32},{64,80},{80,64},{96,112},{112,96},{1... | collective-permute-start | bytes 24584 | tf_op jit(solution)/shard_map/ppermute | solution.py:215

commit v4 on v3

--- a/solution.py
+++ b/solution.py
@@ -1,3 +1,5 @@
+import functools
+
 import jax
 import jax.numpy as jnp
 from jax import lax
@@ -12,6 +14,7 @@
 STEP = 24
 TILES = 96
 BATCH = 4
+SHORT = 16
 GROUPS = TILES // STEP
 SLICE = CB // RELS
 PART = B // SLICE
@@ -21,13 +24,14 @@
     return jnp.dot(a, b, preferred_element_type=jnp.float32)
 
 
-def place(ids, k):
-    code = ids[0, 0, k]
-    row, col = code & (RB - 1), (code >> 4) & (CB - 1)
-    return row, col, pl.multiple_of((code >> 9) * B, B)
-
-
-def forward_kernel(ids, live, core, own_x, other_x, v, w, z, p, x, acc, tiles, wide, sems):
+def place(code):
+    row, col, rel = code & (RB - 1), (code >> 4) & (CB - 1), (code >> 9) & (RELS - 1)
+    return row, col, pl.multiple_of(rel * B, B)
+
+
+def forward_kernel(
+    which, ids, live, side, core, own_x, other_x, v, w, z, p, x, acc, tiles, wide, listed, sems
+):
     def chunk(g):
         span = pl.ds(g * STEP, STEP)
         return pltpu.make_async_copy(v.at[0, 0, span], tiles.at[span], sems.at[g])
@@ -39,25 +43,31 @@
     acc[...] = jnp.zeros_like(acc)
     x[0] = own_x[...]
     x[1] = other_x[...]
-    count = live[0, 0]
     mine = core[0, 0]
+    wanted = side[0, 0] ^ which
+
+    def put(k, at):
+        code = ids[0, 0, k]
+        listed[at] = code + (k << 11)
+        return at + jnp.where((code & 1) == wanted, 1, 0)
+
+    count = lax.fori_loop(0, live[0, 0], put, 0)
+    for u in range(SHORT):
+        listed[count + u] = 0
+    for g in range(GROUPS):
+        chunk(g).wait()
 
     def group(g, carry):
-        chunk(g).wait()
-        first = g * STEP
-
-        @pl.when(first < count)
-        def _():
-            for u in range(STEP):
-                k = first + u
-                row, col, lane = place(ids, k)
-                product = dot(tiles[k], x[(col & 1) ^ mine, col >> 1])
-                product = jnp.where(k < count, product, 0.0)
-                acc[row, :, pl.ds(lane, B)] += product
-
-        return carry
-
-    lax.fori_loop(0, GROUPS, group, 0)
+        for u in range(SHORT):
+            i = g * SHORT + u
+            code = listed[i]
+            row, col, lane = place(code)
+            product = dot(tiles[code >> 11], x[(col & 1) ^ mine, col >> 1])
+            product = jnp.where(i < count, product, 0.0)
+            acc[row >> 1, :, pl.ds(lane, B)] += product
+        return carry
+
+    lax.fori_loop(0, (count + SHORT - 1) // SHORT, group, 0)
     load_w.wait()
 
     def finish(i, carry):
@@ -65,10 +75,10 @@
         held = acc[rows].astype(jnp.bfloat16)
         p[rows] = held
         part = dot(held.reshape(BATCH * B, RELS * B), wide[...])
-        z[rows] = part.astype(jnp.bfloat16).reshape(BATCH, B, B)
-        return carry
-
-    lax.fori_loop(0, RB // BATCH, finish, 0, unroll=2)
+        z[rows] = part.astype(z.dtype).reshape(BATCH, B, B)
+        return carry
+
+    lax.fori_loop(0, RB // 2 // BATCH, finish, 0, unroll=2)
 
 
 def middle_kernel(parts, bias, out_grad, activated, grad_t):
@@ -83,12 +93,13 @@
     grad_t[...] = grad.astype(jnp.float32).T.astype(jnp.bfloat16)
 
 
-def weight_kernel(grad_t, p, out, total):
+def weight_kernel(side, grad_t, p_own, p_other, out, total):
     total[...] = jnp.zeros_like(total)
+    mine = side[0, 0]
 
     def add(i, carry):
-        g = jnp.concatenate([grad_t[2 * i], grad_t[2 * i + 1]], axis=1)
-        total[...] += dot(g, p[pl.ds(2 * i, 2)].reshape(2 * B, RELS * B))
+        g = jnp.concatenate([grad_t[2 * i + mine], grad_t[2 * i + 1 - mine]], axis=1)
+        total[...] += dot(g, jnp.concatenate([p_own[i], p_other[i]], axis=0))
         return carry
 
     lax.fori_loop(0, RB // 2, add, 0, unroll=2)
@@ -107,14 +118,8 @@
 
 
 def backward_kernel(
-    ids, live, core, grad_t, v, w, kept, given, bias_sum, back, acc, tiles, sems
+    ids, live, core, grad_t, v, w, kept, given, bias_sum, back, acc
 ):
-    def chunk(g):
-        span = pl.ds(g * STEP, STEP)
-        return pltpu.make_async_copy(v.at[0, 0, span], tiles.at[span], sems.at[g])
-
-    for g in range(GROUPS):
-        chunk(g).start()
     acc[...] = jnp.zeros_like(acc)
     wide = w[...]
     count = live[0, 0]
@@ -135,15 +140,14 @@
     lax.fori_loop(0, RB // 2, start, 0, unroll=2)
 
     def group(g, carry):
-        chunk(g).wait()
         first = g * STEP
 
         @pl.when(first < count)
         def _():
             for u in range(STEP):
                 k = first + u
-                row, col, at = place(ids, k)
-                product = dot(back[row, pl.ds(at, B), :], tiles[k])
+                row, col, at = place(ids[0, 0, k])
+                product = dot(back[row, pl.ds(at, B), :], v[0, 0, k])
                 product = jnp.where(k < count, product, 0.0)
                 acc[(col & 1) ^ mine, col >> 1] += product
 
@@ -203,7 +207,7 @@
 VMEM = pl.BlockSpec(memory_space=pltpu.VMEM)
 SMEM = pl.BlockSpec(memory_space=pltpu.SMEM)
 ANY = pl.BlockSpec(memory_space=pl.ANY)
-WIDE = pltpu.CompilerParams(vmem_limit_bytes=48 * 1024 * 1024)
+WIDE = pltpu.CompilerParams(vmem_limit_bytes=50 * 1024 * 1024)
 PARAMS = pltpu.CompilerParams(vmem_limit_bytes=32 * 1024 * 1024)
 
 
@@ -225,24 +229,39 @@
     core = jnp.reshape(lax.axis_index("row") % 2, (1, 1)).astype(jnp.int32)
     own_x = swap(jnp.broadcast_to(features[None], (chips, B, B)), "row", same_core)
     other_x = other_core(own_x)
-    z_parts, p_wide = pl.pallas_call(
-        forward_kernel,
-        out_shape=(
-            jax.ShapeDtypeStruct((RB, B, B), jnp.bfloat16),
-            jax.ShapeDtypeStruct((RB, B, RELS * B), jnp.bfloat16),
-        ),
-        in_specs=[SMEM] * 3 + [VMEM] * 2 + [ANY] * 2,
-        out_specs=(VMEM, VMEM),
-        scratch_shapes=[
-            pltpu.VMEM((2, chips, B, B), jnp.bfloat16),
-            pltpu.VMEM((RB, B, RELS * B), jnp.float32),
-            pltpu.VMEM((TILES, B, B), jnp.bfloat16),
-            pltpu.VMEM((RELS * B, B), jnp.bfloat16),
-            pltpu.SemaphoreType.DMA((GROUPS + 1,)),
-        ],
-        compiler_params=WIDE,
-        name="forward",
-    )(ids, live, core, own_x, other_x, tile_values, wide_weights)
+    side = jnp.reshape(lax.axis_index("col") % 2, (1, 1)).astype(jnp.int32)
+
+    def forward(which, z_type):
+        return pl.pallas_call(
+            functools.partial(forward_kernel, which),
+            out_shape=(
+                jax.ShapeDtypeStruct((RB // 2, B, B), z_type),
+                jax.ShapeDtypeStruct((RB // 2, B, RELS * B), jnp.bfloat16),
+            ),
+            in_specs=[SMEM] * 4 + [VMEM] * 2 + [ANY] * 2,
+            out_specs=(VMEM, VMEM),
+            scratch_shapes=[
+                pltpu.VMEM((2, chips, B, B), jnp.bfloat16),
+                pltpu.VMEM((RB // 2, B, RELS * B), jnp.float32),
+                pltpu.VMEM((TILES, B, B), jnp.bfloat16),
+                pltpu.VMEM((RELS * B, B), jnp.bfloat16),
+                pltpu.SMEM((TILES + SHORT,), jnp.int32),
+                pltpu.SemaphoreType.DMA((GROUPS + 1,)),
+            ],
+            compiler_params=WIDE,
+            cost_estimate=pl.CostEstimate(flops=10**9, bytes_accessed=10**7, transcendentals=0),
+            name="forward",
+        )(ids, live, side, core, own_x, other_x, tile_values, wide_weights)
+
+    def partner(r, c):
+        return c ^ 1 if r % 2 == 0 else ((c + 1) ^ 1) - 1
+
+    pairs = [(r * RB + c, r * RB + partner(r, c) % RB) for r in range(CB) for c in range(RB)]
+    z_other, p_other = forward(1, jnp.bfloat16)
+    z_other = lax.ppermute(z_other, ("row", "col"), pairs)
+    z_own, p_own = forward(0, jnp.float32)
+    z_parts = (z_own + z_other.astype(jnp.float32)).astype(jnp.bfloat16)
+    same_side = [[2 * i + c for i in range(RB // 2)] for c in range(2)]
     activated, grad_t = pl.pallas_call(
         middle_kernel,
         out_shape=(
@@ -253,17 +272,17 @@
         out_specs=(VMEM,) * 2,
         compiler_params=PARAMS,
         name="middle",
-    )(swap(z_parts, "col"), bias.reshape(1, B), out_grad)
+    )(swap(z_parts, "col", same_side), bias.reshape(1, B), out_grad)
     grad_all = lax.all_gather(grad_t, "col", axis=0, tiled=False)
     weight_parts = pl.pallas_call(
         weight_kernel,
         out_shape=jax.ShapeDtypeStruct((CB, PART, B), jnp.float32),
-        in_specs=[VMEM] * 2,
+        in_specs=[SMEM] + [VMEM] * 3,
         out_specs=VMEM,
         scratch_shapes=[pltpu.VMEM((B, RELS * B), jnp.float32)],
         compiler_params=PARAMS,
         name="weight",
-    )(grad_all, p_wide)
+    )(side, grad_all, p_own, p_other)
     weight_parts = swap(weight_parts, "row")
     kept, given, bias_sum = pl.pallas_call(
         backward_kernel,
@@ -272,13 +291,11 @@
             jax.ShapeDtypeStruct((chips, B, B), jnp.bfloat16),
             jax.ShapeDtypeStruct((8, B), jnp.float32),
         ),
-        in_specs=[SMEM] * 3 + [VMEM, ANY, VMEM],
+        in_specs=[SMEM] * 3 + [VMEM] * 3,
         out_specs=(VMEM,) * 3,
         scratch_shapes=[
             pltpu.VMEM((RB, RELS * B, B), jnp.bfloat16),
             pltpu.VMEM((2, chips, B, B), jnp.float32),
-            pltpu.VMEM((TILES, B, B), jnp.bfloat16),
-            pltpu.SemaphoreType.DMA((GROUPS,)),
         ],
         compiler_params=PARAMS,
         cost_estimate=pl.CostEstimate(flops=10**9, bytes_accessed=10**7, transcendentals=0),

time: 165 us -> 162 us (0.982)
  blocking collectives: 127 us -> 113 us
  starting transfers between devices: 22.5 us -> 31.1 us
    ppermute x0 -> x1, starting transfers between devices: none -> 11.7 us  [on_device(): z_other = lax.ppermute(z_other, ('row', 'col'), pairs)]
    all_to_all x5, blocking collectives: 97.9 us -> 90.1 us  [swap(): lax.all_to_all(blocks, axis, 0, 0, tiled=True, axis_index_groups=groups)]
    all_gather x1, blocking collectives: 28.7 us -> 22.7 us  [on_device(): grad_all = lax.all_gather(grad_t, 'col', axis=0, tiled=False)]
    ppermute x3, starting transfers between devices: 22.5 us -> 19.3 us  [other_core(): return lax.ppermute(block, 'row', [(r, r ^ 1) for r in range(CB)])]
    pallas_call x1 -> x2, Pallas kernels: 4.28 us -> 6.47 us  [forward(): pl.pallas_call(functools.partial(forward_kernel, which), out_shape=(jax.S...]
  transfers between devices with their start and end apart: 3 -> 4, of which waited for: 2 -> 3; matrix products, arithmetic and copies ran while one was open for 0% -> 0% of each run, Pallas kernels for 1% -> 3%
where the time goes in v4:
time: 162 us; the launch traced here: 161 us
  blocking collectives  113 us (70%)
  starting transfers between devices  31.1 us (19%)
  Pallas kernels  12 us (7%)
  local copies, waits for them, and re-layouts  1.77 us (1%)
    all_to_all x5, blocking collectives, swap(): lax.all_to_all(blocks, axis, 0, 0, tiled=True, axis_index_groups=groups)  90.1 us
    all_gather x1, blocking collectives, on_device(): grad_all = lax.all_gather(grad_t, 'col', axis=0, tiled=False)  22.7 us
    ppermute x3, starting transfers between devices, other_core(): return lax.ppermute(block, 'row', [(r, r ^ 1) for r in range(CB)])  19.3 us
    ppermute x1, starting transfers between devices, on_device(): z_other = lax.ppermute(z_other, ('row', 'col'), pairs)  11.7 us
    pallas_call x2, Pallas kernels, forward(): pl.pallas_call(functools.partial(forward_kernel, which), out_shape=(jax.S...  6.47 us
  transfers between devices with their start and end apart: 4, of which 3 were waited for; matrix products, arithmetic and copies ran while one was open for 0% of the time, Pallas kernels for 3%

profile of v4, /device:TPU:1, one launch (start us, length us, event | category | flops | bytes accessed | tf_op | source)
XLA Modules:
  0.0 161.1 jit_solution(14383823310257391938)
XLA Ops:
  0.6 0.9 broadcast_in_dim.2
  1.5 16.6 %all_to_all.25.own_x = bf16[16,128,128]{2,1,0:T(8,128)(2,1)S(1)} all-to-all(bf16[16,128,128]{2,1,0:T(8,128)(2,1)S(1)} %broadcast_in_dim.2), channel_id=1, replica_groups={{0,32,64,96,128,160,192,224,256,288,320,352,384,416,448,480},{16,48,80,..., dimensions={0} | all-to-all | bytes 1048576 | tf_op jit(solution)/shard_map/all_to_all | solution.py:215
  18.1 5.1 %collective-permute-start = (bf16[16,128,128]{2,1,0:T(8,128)(2,1)S(1)}, bf16[16,128,128]{2,1,0:T(8,128)(2,1)S(1)}, u32[]{:S(2)}, u32[]{:S(2)}) collective-permute-start(bf16[16,128,128]{2,1,0:T(8,128)(2,1)S(1)} %all_to_all.25.own_x), channel_id=1, source_target_pairs={{0,16},{16,0},{32,48},{48,32},{64,80},{80,64},{96,112},{112,96},{1... | collective-permute-start | bytes 1572872 | tf_op jit(solution)/shard_map/ppermute | solution.py:219
  23.9 0.7 shift-left_add_fusion.ids
  24.6 0.2 collective-permute-done.other_x
  24.7 0.0 copy-start.1
  24.7 0.9 copy-done.1
  25.6 3.2 %forward.3 = (bf16[8,128,128]{2,1,0:T(8,128)(2,1)S(1)}, bf16[8,128,512]{2,1,0:T(8,128)(2,1)S(1)}) custom-call(s32[1,1,96]{2,1,0:T(1,128)S(1)} %shift-left_add_fusion.ids, s32[1,1]{1,0:T(1,128)S(6)} %copy.15.live, s32[1,1]{1,0:T(1,128)} %bitcast.side, s32[1,1]{1,0:T(1,128)} %bitcast.1.core, bf16[16,128,128]{2,1,0:T(8,128)(2,1)S(1)} %all_to_all.25.own_x, ...), custom_call_target="tpu_custom_call" | custom-call | flops 1000000000 | bytes 10000000 | tf_op jit(solution)/shard_map/forward/pallas_call | solution.py:235
  28.9 0.0 copy-start.2
  28.9 0.0 copy-start.3
  28.9 0.0 copy-start
  28.9 11.7 %collective-permute-start.1 = (bf16[8,128,128]{2,1,0:T(8,128)(2,1)S(1)}, bf16[8,128,128]{2,1,0:T(8,128)(2,1)S(1)}, u32[]{:S(2)}, u32[]{:S(2)}) collective-permute-start(bf16[8,128,128]{2,1,0:T(8,128)(2,1)S(1)} %get-tuple-element.17), channel_id=1, source_target_pairs={{0,1},{1,0},{2,3},{3,2},{4,5},{5,4},{6,7},{7,6},{8,9},{9,8},{10,11... | collective-permute-start | bytes 786440 | tf_op jit(solution)/shard_map/ppermute | solution.py:261
  40.7 3.2 %forward.2 = (f32[8,128,128]{2,1,0:T(8,128)S(1)}, bf16[8,128,512]{2,1,0:T(8,128)(2,1)S(1)}) custom-call(s32[1,1,96]{2,1,0:T(1,128)S(1)} %shift-left_add_fusion.ids, s32[1,1]{1,0:T(1,128)S(6)} %copy.15.live, s32[1,1]{1,0:T(1,128)} %bitcast.side, s32[1,1]{1,0:T(1,128)} %bitcast.1.core, bf16[16,128,128]{2,1,0:T(8,128)(2,1)S(1)} %all_to_all.25.own_x, ...), custom_call_target="tpu_custom_call" | custom-call | flops 1000000000 | bytes 10000000 | tf_op jit(solution)/shard_map/forward/pallas_call | solution.py:235
  43.9 0.5 collective-permute-done.1
  44.4 0.1 add_convert_fusion
  44.5 28.6 %all_to_all.26.parts = bf16[8,128,128]{2,1,0:T(8,128)(2,1)S(1)} all-to-all(bf16[8,128,128]{2,1,0:T(8,128)(2,1)S(1)} %add_convert_fusion), channel_id=1, replica_groups={{0,2,4,6,8,10,12,14},{1,3,5,7,9,11,13,15},{16,18,20,22,24,26,28,30},{17..., dimensions={0} | all-to-all | bytes 524288 | tf_op jit(solution)/shard_map/all_to_all | solution.py:215
  73.1 0.0 copy-done.2
  73.1 0.0 copy-done.3
  73.1 0.7 middle.1
  73.8 22.7 %all-gather = bf16[2048,128]{1,0:T(8,128)(2,1)S(1)} all-gather(bf16[128,128]{1,0:T(8,128)(2,1)S(1)} %get-tuple-element.19), channel_id=2, replica_groups=mesh['row'=32,'col'=16] {'col'}, dimensions={0}, use_global_device_ids=true | all-gather | bytes 557056 | tf_op jit(solution)/shard_map/all_gather | solution.py:276
  96.5 0.0 copy-done
  96.5 2.8 %backward.1 = (bf16[16,128,128]{2,1,0:T(8,128)(2,1)S(1)}, bf16[16,128,128]{2,1,0:T(8,128)(2,1)S(1)}, f32[8,128]{1,0:T(8,128)S(1)}) custom-call(s32[1,1,96]{2,1,0:T(1,128)S(1)} %shift-left_add_fusion.ids, s32[1,1]{1,0:T(1,128)S(6)} %copy.15.live, s32[1,1]{1,0:T(1,128)} %bitcast.1.core, bf16[16,128,128]{2,1,0:T(8,128)(2,1)S(1)} %bitcast.6, ...), custom_call_target="tpu_custom_call" | custom-call | flops 1000000000 | bytes 10000000 | tf_op jit(solution)/shard_map/backward/pallas_call | solution.py:287
  99.3 10.3 %collective-permute-start.2 = (bf16[16,128,128]{2,1,0:T(8,128)(2,1)S(1)}, bf16[16,128,128]{2,1,0:T(8,128)(2,1)S(1)}, u32[]{:S(2)}, u32[]{:S(2)}) collective-permute-start(bf16[16,128,128]{2,1,0:T(8,128)(2,1)S(1)} %get-tuple-element.21), channel_id=1, source_target_pairs={{0,16},{16,0},{32,48},{48,32},{64,80},{80,64},{96,112},{112,96},{1... | collective-permute-start | bytes 1572872 | tf_op jit(solution)/shard_map/ppermute | solution.py:219
  109.6 1.0 weight.1
  110.6 12.6 %all_to_all.27.parts = f32[32,16,128]{2,1,0:T(8,128)S(1)} all-to-all(f32[32,16,128]{2,1,0:T(8,128)S(1)} %weight.1), channel_id=1, replica_groups=mesh['row'=32,'col'=16] {'row'}, dimensions={0} | all-to-all | bytes 524288 | tf_op jit(solution)/shard_map/all_to_all | solution.py:215
  123.2 16.9 %all_to_all.28.parts = bf16[16,16,128]{2,1,0:T(8,128)(2,1)S(1)} all-to-all(bf16[16,16,128]{2,1,0:T(8,128)(2,1)S(1)} %spread.1), channel_id=1, replica_groups=mesh['row'=32,'col'=16] {'col'}, dimensions={0} | all-to-all | bytes 131072 | tf_op jit(solution)/shard_map/all_to_all | solution.py:215
  140.1 3.9 %collective-permute-start.3 = (bf16[32,128]{1,0:T(8,128)(2,1)S(1)}, bf16[32,128]{1,0:T(8,128)(2,1)S(1)}, u32[]{:S(2)}, u32[]{:S(2)}) collective-permute-start(bf16[32,128]{1,0:T(8,128)(2,1)S(1)} %total.1.own), channel_id=1, source_target_pairs={{0,16},{16,0},{32,48},{48,32},{64,80},{80,64},{96,112},{112,96},{1... | collective-permute-start | bytes 24584 | tf_op jit(solution)/shard_map/ppermute | solution.py:219
  144.0 0.0 collective-permute-done.2.taken
  144.1 0.1 join.1.sent
  144.2 0.6 collective-permute-done.3.other
  144.9 15.4 %all_to_all.29.received = bf16[16,176,128]{2,1,0:T(8,128)(2,1)S(1)} all-to-all(bf16[16,176,128]{2,1,0:T(8,128)(2,1)S(1)} %append.1), channel_id=1, replica_groups={{0,32,64,96,128,160,192,224,256,288,320,352,384,416,448,480},{16,48,80,..., dimensions={0} | all-to-all | bytes 1441792 | tf_op jit(solution)/shard_map/all_to_all | solution.py:215
  160.2 0.9 final.1
  (3 shorter events, 0.1 us)
Async XLA Ops:
  18.1 6.7 %collective-permute-start = (bf16[16,128,128]{2,1,0:T(8,128)(2,1)S(1)}, bf16[16,128,128]{2,1,0:T(8,128)(2,1)S(1)}, u32[]{:S(2)}, u32[]{:S(2)}) collective-permute-start(bf16[16,128,128]{2,1,0:T(8,128)(2,1)S(1)} %all_to_all.25.own_x), channel_id=1, source_target_pairs={{0,16},{16,0},{32,48},{48,32},{64,80},{80,64},{96,112},{112,96},{1... | collective-permute-start | bytes 1572872 | tf_op jit(solution)/shard_map/ppermute | solution.py:219
  24.7 0.9 copy-start.1
  28.9 44.3 %copy-start.2 = (bf16[128,128]{1,0:T(8,128)(2,1)S(1)}, bf16[128,128]{1,0:T(8,128)(2,1)}, u32[]{:S(2)}) copy-start(bf16[128,128]{1,0:T(8,128)(2,1)} %out_grad.1) | copy-start | bytes 98308
  28.9 44.2 %copy-start.3 = (f32[128]{0:T(128)S(1)}, f32[128]{0:T(128)}, u32[]{:S(2)}) copy-start(f32[128]{0:T(128)} %param.16) | copy-start | bytes 1540
  28.9 67.6 %copy-start = (bf16[1,1,96,128,128]{4,3,2,1,0:T(8,128)(2,1)S(1)}, bf16[1,1,96,128,128]{4,3,2,1,0:T(8,128)(2,1)}, u32[]{:S(2)}) copy-start(bf16[1,1,96,128,128]{4,3,2,1,0:T(8,128)(2,1)} %v.5) | copy-start | bytes 9437188
  28.9 15.5 %collective-permute-start.1 = (bf16[8,128,128]{2,1,0:T(8,128)(2,1)S(1)}, bf16[8,128,128]{2,1,0:T(8,128)(2,1)S(1)}, u32[]{:S(2)}, u32[]{:S(2)}) collective-permute-start(bf16[8,128,128]{2,1,0:T(8,128)(2,1)S(1)} %get-tuple-element.17), channel_id=1, source_target_pairs={{0,1},{1,0},{2,3},{3,2},{4,5},{5,4},{6,7},{7,6},{8,9},{9,8},{10,11... | collective-permute-start | bytes 786440 | tf_op jit(solution)/shard_map/ppermute | solution.py:261
  99.3 44.8 %collective-permute-start.2 = (bf16[16,128,128]{2,1,0:T(8,128)(2,1)S(1)}, bf16[16,128,128]{2,1,0:T(8,128)(2,1)S(1)}, u32[]{:S(2)}, u32[]{:S(2)}) collective-permute-start(bf16[16,128,128]{2,1,0:T(8,128)(2,1)S(1)} %get-tuple-element.21), channel_id=1, source_target_pairs={{0,16},{16,0},{32,48},{48,32},{64,80},{80,64},{96,112},{112,96},{1... | collective-permute-start | bytes 1572872 | tf_op jit(solution)/shard_map/ppermute | solution.py:219
  140.1 4.7 %collective-permute-start.3 = (bf16[32,128]{1,0:T(8,128)(2,1)S(1)}, bf16[32,128]{1,0:T(8,128)(2,1)S(1)}, u32[]{:S(2)}, u32[]{:S(2)}) collective-permute-start(bf16[32,128]{1,0:T(8,128)(2,1)S(1)} %total.1.own), channel_id=1, source_target_pairs={{0,16},{16,0},{32,48},{48,32},{64,80},{80,64},{96,112},{112,96},{1... | collective-permute-start | bytes 24584 | tf_op jit(solution)/shard_map/ppermute | solution.py:219

commit v5 on v4

--- a/solution.py
+++ b/solution.py
@@ -11,11 +11,12 @@
 CB = 32
 RELS = 4
 B = 128
-STEP = 24
 TILES = 96
 BATCH = 4
 SHORT = 16
-GROUPS = TILES // STEP
+CHUNK_BITS = 4
+CHUNK = 1 << CHUNK_BITS
+CHUNKS = TILES // CHUNK
 SLICE = CB // RELS
 PART = B // SLICE
 
@@ -30,14 +31,17 @@
 
 
 def forward_kernel(
-    which, ids, live, side, core, own_x, other_x, v, w, z, p, x, acc, tiles, wide, listed, sems
+    which, ids, live, side, core, own_x, other_x, v, w, z, p, *rest
 ):
+    lists = rest[0] if which == 0 else None
+    x, acc, tiles, wide, listed, sems = rest[-6:]
+
     def chunk(g):
-        span = pl.ds(g * STEP, STEP)
+        span = pl.ds(g * CHUNK, CHUNK)
         return pltpu.make_async_copy(v.at[0, 0, span], tiles.at[span], sems.at[g])
 
-    load_w = pltpu.make_async_copy(w, wide, sems.at[GROUPS])
-    for g in range(GROUPS):
+    load_w = pltpu.make_async_copy(w.at[: RELS * B], wide, sems.at[CHUNKS])
+    for g in range(CHUNKS):
         chunk(g).start()
     load_w.start()
     acc[...] = jnp.zeros_like(acc)
@@ -54,10 +58,15 @@
     count = lax.fori_loop(0, live[0, 0], put, 0)
     for u in range(SHORT):
         listed[count + u] = 0
-    for g in range(GROUPS):
+
+    def arrive(g, carry):
         chunk(g).wait()
-
-    def group(g, carry):
+        return carry
+
+    def group(g, arrived):
+        last = jnp.minimum(g * SHORT + SHORT, count) - 1
+        needed = jnp.maximum((listed[last] >> (11 + CHUNK_BITS)) + 1, arrived)
+        lax.fori_loop(arrived, needed, arrive, 0)
         for u in range(SHORT):
             i = g * SHORT + u
             code = listed[i]
@@ -65,9 +74,10 @@
             product = dot(tiles[code >> 11], x[(col & 1) ^ mine, col >> 1])
             product = jnp.where(i < count, product, 0.0)
             acc[row >> 1, :, pl.ds(lane, B)] += product
-        return carry
-
-    lax.fori_loop(0, (count + SHORT - 1) // SHORT, group, 0)
+        return needed
+
+    arrived = lax.fori_loop(0, (count + SHORT - 1) // SHORT, group, 0)
+    lax.fori_loop(arrived, CHUNKS, arrive, 0)
     load_w.wait()
 
     def finish(i, carry):
@@ -79,6 +89,23 @@
         return carry
 
     lax.fori_loop(0, RB // 2 // BATCH, finish, 0, unroll=2)
+    if which == 0:
+        both_lists(ids, live[0, 0], side[0, 0], lists)
+
+
+def both_lists(ids, live, side, lists):
+    def put(k, at):
+        code = ids[0, 0, k]
+        other = (code & 1) ^ side
+        lists[other, jnp.where(other == 1, at, k - at)] = code + (k << 11)
+        return at + other
+
+    given = lax.fori_loop(0, live, put, 0)
+    for u in range(SHORT):
+        lists[0, live - given + u] = 0
+        lists[1, given + u] = 0
+    lists[0, TILES + SHORT] = live - given
+    lists[1, TILES + SHORT] = given
 
 
 def middle_kernel(parts, bias, out_grad, activated, grad_t):
@@ -90,19 +117,65 @@
     activated[...] = (z * s).astype(jnp.bfloat16)
     slope = s * (1.0 + z * (1.0 - s))
     grad = (out_grad[...].astype(jnp.float32) * slope).astype(jnp.bfloat16)
-    grad_t[...] = grad.astype(jnp.float32).T.astype(jnp.bfloat16)
-
-
-def weight_kernel(side, grad_t, p_own, p_other, out, total):
+    turned = grad.astype(jnp.float32).T.astype(jnp.bfloat16)
+    for i in range(grad_t.shape[0]):
+        grad_t[i] = turned
+
+
+def early_kernel(lists, core, grad_t, p, v, w, total, bias_sum, acc, back):
     total[...] = jnp.zeros_like(total)
-    mine = side[0, 0]
+    bias_sum[...] = jnp.zeros_like(bias_sum)
+    acc[...] = jnp.zeros_like(acc)
+    weight_rows(grad_t, p, total, bias_sum)
+    back_rows(grad_t, w[...], back)
+    back_tiles(0, lists, core[0, 0], v, back, acc)
+
+
+def back_tiles(which, lists, mine, v, back, acc):
+    count = lists[which, TILES + SHORT]
+
+    def group(g, carry):
+        for u in range(SHORT):
+            i = g * SHORT + u
+            code = lists[which, i]
+            row, col, at = place(code)
+            product = dot(back[row >> 1, pl.ds(at, B), :], v[0, 0, code >> 11])
+            product = jnp.where(i < count, product, 0.0)
+            acc[(col & 1) ^ mine, col >> 1] += product
+        return carry
+
+    lax.fori_loop(0, (count + SHORT - 1) // SHORT, group, 0)
+
+
+def weight_rows(grad_t, p, total, bias_sum):
+    ones = jnp.ones((8, 2 * B), jnp.bfloat16)
 
     def add(i, carry):
-        g = jnp.concatenate([grad_t[2 * i + mine], grad_t[2 * i + 1 - mine]], axis=1)
-        total[...] += dot(g, jnp.concatenate([p_own[i], p_other[i]], axis=0))
+        g = jnp.concatenate([grad_t[2 * i], grad_t[2 * i + 1]], axis=1)
+        total[...] += dot(g, p[pl.ds(2 * i, 2)].reshape(2 * B, RELS * B))
+        bias_sum[...] += lax.dot_general(
+            ones, g, (((1,), (1,)), ((), ())), preferred_element_type=jnp.float32
+        )
         return carry
 
-    lax.fori_loop(0, RB // 2, add, 0, unroll=2)
+    lax.fori_loop(0, RB // 4, add, 0, unroll=2)
+
+
+def back_rows(grad_t, wide, back):
+    def start(i, carry):
+        g = jnp.concatenate([grad_t[2 * i], grad_t[2 * i + 1]], axis=1)
+        both = dot(wide, g).astype(jnp.bfloat16)
+        back[2 * i] = both[:, :B]
+        back[2 * i + 1] = both[:, B:]
+        return carry
+
+    lax.fori_loop(0, RB // 4, start, 0, unroll=2)
+
+
+def weight_kernel(grad_t, p, early_total, early_bias, out, bias_sum, total):
+    total[...] = early_total[...]
+    bias_sum[...] = early_bias[...]
+    weight_rows(grad_t, p, total, bias_sum)
     for b in range(CB):
         rel, part = b // SLICE, b % SLICE
         out[b] = total[part * PART : (part + 1) * PART, rel * B : (rel + 1) * B]
@@ -117,43 +190,10 @@
         out[c] = total
 
 
-def backward_kernel(
-    ids, live, core, grad_t, v, w, kept, given, bias_sum, back, acc
-):
-    acc[...] = jnp.zeros_like(acc)
-    wide = w[...]
-    count = live[0, 0]
-    mine = core[0, 0]
-    ones = jnp.ones((8, 2 * B), jnp.bfloat16)
-    bias_sum[...] = jnp.zeros_like(bias_sum)
-
-    def start(i, carry):
-        g = jnp.concatenate([grad_t[2 * i], grad_t[2 * i + 1]], axis=1)
-        both = dot(wide, g).astype(jnp.bfloat16)
-        back[2 * i] = both[:, :B]
-        back[2 * i + 1] = both[:, B:]
-        bias_sum[...] += lax.dot_general(
-            ones, g, (((1,), (1,)), ((), ())), preferred_element_type=jnp.float32
-        )
-        return carry
-
-    lax.fori_loop(0, RB // 2, start, 0, unroll=2)
-
-    def group(g, carry):
-        first = g * STEP
-
-        @pl.when(first < count)
-        def _():
-            for u in range(STEP):
-                k = first + u
-                row, col, at = place(ids[0, 0, k])
-                product = dot(back[row, pl.ds(at, B), :], v[0, 0, k])
-                product = jnp.where(k < count, product, 0.0)
-                acc[(col & 1) ^ mine, col >> 1] += product
-
-        return carry
-
-    lax.fori_loop(0, GROUPS, group, 0)
+def backward_kernel(lists, core, grad_t, early_acc, v, w, kept, given, back, acc):
+    acc[...] = early_acc[...]
+    back_rows(grad_t, w[...], back)
+    back_tiles(1, lists, core[0, 0], v, back, acc)
     kept[...] = acc[0].astype(jnp.bfloat16)
     given[...] = acc[1].astype(jnp.bfloat16)
 
@@ -231,27 +271,30 @@
     other_x = other_core(own_x)
     side = jnp.reshape(lax.axis_index("col") % 2, (1, 1)).astype(jnp.int32)
 
+    early_weights = jnp.pad(wide_weights, ((0, PART), (0, 0)))
+
     def forward(which, z_type):
         return pl.pallas_call(
             functools.partial(forward_kernel, which),
             out_shape=(
                 jax.ShapeDtypeStruct((RB // 2, B, B), z_type),
                 jax.ShapeDtypeStruct((RB // 2, B, RELS * B), jnp.bfloat16),
-            ),
+            )
+            + (jax.ShapeDtypeStruct((2, TILES + SHORT + 1), jnp.int32),) * (1 - which),
             in_specs=[SMEM] * 4 + [VMEM] * 2 + [ANY] * 2,
-            out_specs=(VMEM, VMEM),
+            out_specs=(VMEM, VMEM) + (SMEM,) * (1 - which),
             scratch_shapes=[
                 pltpu.VMEM((2, chips, B, B), jnp.bfloat16),
                 pltpu.VMEM((RB // 2, B, RELS * B), jnp.float32),
                 pltpu.VMEM((TILES, B, B), jnp.bfloat16),
                 pltpu.VMEM((RELS * B, B), jnp.bfloat16),
                 pltpu.SMEM((TILES + SHORT,), jnp.int32),
-                pltpu.SemaphoreType.DMA((GROUPS + 1,)),
+                pltpu.SemaphoreType.DMA((CHUNKS + 1,)),
             ],
             compiler_params=WIDE,
             cost_estimate=pl.CostEstimate(flops=10**9, bytes_accessed=10**7, transcendentals=0),
             name="forward",
-        )(ids, live, side, core, own_x, other_x, tile_values, wide_weights)
+        )(ids, live, side, core, own_x, other_x, tile_values, early_weights)
 
     def partner(r, c):
         return c ^ 1 if r % 2 == 0 else ((c + 1) ^ 1) - 1
@@ -259,48 +302,65 @@
     pairs = [(r * RB + c, r * RB + partner(r, c) % RB) for r in range(CB) for c in range(RB)]
     z_other, p_other = forward(1, jnp.bfloat16)
     z_other = lax.ppermute(z_other, ("row", "col"), pairs)
-    z_own, p_own = forward(0, jnp.float32)
+    z_own, p_own, lists = forward(0, jnp.float32)
     z_parts = (z_own + z_other.astype(jnp.float32)).astype(jnp.bfloat16)
     same_side = [[2 * i + c for i in range(RB // 2)] for c in range(2)]
     activated, grad_t = pl.pallas_call(
         middle_kernel,
         out_shape=(
             jax.ShapeDtypeStruct((B, B), jnp.bfloat16),
-            jax.ShapeDtypeStruct((B, B), jnp.bfloat16),
+            jax.ShapeDtypeStruct((RB // 2, B, B), jnp.bfloat16),
         ),
         in_specs=[VMEM] * 3,
         out_specs=(VMEM,) * 2,
         compiler_params=PARAMS,
         name="middle",
     )(swap(z_parts, "col", same_side), bias.reshape(1, B), out_grad)
-    grad_all = lax.all_gather(grad_t, "col", axis=0, tiled=False)
-    weight_parts = pl.pallas_call(
+    grad_own = swap(grad_t, "col", same_side)
+    grad_other = lax.ppermute(grad_own, ("row", "col"), pairs)
+    early_total, early_bias, early_acc = pl.pallas_call(
+        early_kernel,
+        out_shape=(
+            jax.ShapeDtypeStruct((B, RELS * B), jnp.float32),
+            jax.ShapeDtypeStruct((8, B), jnp.float32),
+            jax.ShapeDtypeStruct((2, chips, B, B), jnp.float32),
+        ),
+        in_specs=[SMEM] * 2 + [VMEM] * 4,
+        out_specs=(VMEM,) * 3,
+        scratch_shapes=[pltpu.VMEM((RB // 2, RELS * B, B), jnp.bfloat16)],
+        compiler_params=PARAMS,
+        cost_estimate=pl.CostEstimate(flops=10**9, bytes_accessed=10**7, transcendentals=0),
+        name="early",
+    )(lists, core, grad_own, p_own, tile_values, wide_weights)
+    weight_parts, bias_sum = pl.pallas_call(
         weight_kernel,
-        out_shape=jax.ShapeDtypeStruct((CB, PART, B), jnp.float32),
-        in_specs=[SMEM] + [VMEM] * 3,
-        out_specs=VMEM,
+        out_shape=(
+            jax.ShapeDtypeStruct((CB, PART, B), jnp.float32),
+            jax.ShapeDtypeStruct((8, B), jnp.float32),
+        ),
+        in_specs=[VMEM] * 4,
+        out_specs=(VMEM, VMEM),
         scratch_shapes=[pltpu.VMEM((B, RELS * B), jnp.float32)],
         compiler_params=PARAMS,
         name="weight",
-    )(side, grad_all, p_own, p_other)
+    )(grad_other, p_other, early_total, early_bias)
     weight_parts = swap(weight_parts, "row")
-    kept, given, bias_sum = pl.pallas_call(
+    kept, given = pl.pallas_call(
         backward_kernel,
         out_shape=(
             jax.ShapeDtypeStruct((chips, B, B), jnp.bfloat16),
             jax.ShapeDtypeStruct((chips, B, B), jnp.bfloat16),
-            jax.ShapeDtypeStruct((8, B), jnp.float32),
         ),
-        in_specs=[SMEM] * 3 + [VMEM] * 3,
-        out_specs=(VMEM,) * 3,
+        in_specs=[SMEM] * 2 + [VMEM] * 4,
+        out_specs=(VMEM,) * 2,
         scratch_shapes=[
-            pltpu.VMEM((RB, RELS * B, B), jnp.bfloat16),
+            pltpu.VMEM((RB // 2, RELS * B, B), jnp.bfloat16),
             pltpu.VMEM((2, chips, B, B), jnp.float32),
         ],
         compiler_params=PARAMS,
         cost_estimate=pl.CostEstimate(flops=10**9, bytes_accessed=10**7, transcendentals=0),
         name="backward",
-    )(ids, live, core, grad_all, tile_values, wide_weights)
+    )(lists, core, grad_other, early_acc, tile_values, wide_weights)
     taken = other_core(given)
     own = pl.pallas_call(
         spread_kernel,

time: 162 us -> 159 us (0.981)
  blocking collectives: 113 us -> 107 us
  Pallas kernels: 12 us -> 15.8 us
    all_gather x1 -> x0, blocking collectives: 22.7 us -> none  [on_device(): grad_all = lax.all_gather(grad_t, 'col', axis=0, tiled=False)]
    all_to_all x5 -> x6, blocking collectives: 90.1 us -> 107 us  [swap(): lax.all_to_all(blocks, axis, 0, 0, tiled=True, axis_index_groups=groups)]
    ppermute x3, starting transfers between devices: 19.3 us -> 14.3 us  [other_core(): return lax.ppermute(block, 'row', [(r, r ^ 1) for r in range(CB)])]
    ppermute x0 -> x1, starting transfers between devices: none -> 4.57 us  [on_device(): grad_other = lax.ppermute(grad_own, ('row', 'col'), pairs)]
    pallas_call x1 -> x2, Pallas kernels: 0.99 us -> 3.29 us  [the longest x1 2.74 us: on_device(): pl.pallas_call(early_kernel, out_shape=(jax.ShapeDtypeStruct((B, RELS * B...]
    pallas_call x2, Pallas kernels: 6.47 us -> 8.42 us  [forward(): pl.pallas_call(functools.partial(forward_kernel, which), out_shape=(jax.S...]
  transfers between devices with their start and end apart: 4 -> 5, of which waited for: 3 -> 2; matrix products, arithmetic and copies ran while one was open for 0% -> 1% of each run, Pallas kernels for 3% -> 5%
where the time goes in v5:
time: 159 us
  blocking collectives  107 us (67%)
  starting transfers between devices  30.1 us (19%)
  Pallas kernels  15.8 us (10%)
  local copies, waits for them, and re-layouts  1.79 us (1%)
  waiting for transfers between devices  1.63 us (1%)
    all_to_all x6, blocking collectives, swap(): lax.all_to_all(blocks, axis, 0, 0, tiled=True, axis_index_groups=groups)  107 us
    ppermute x3, starting transfers between devices, other_core(): return lax.ppermute(block, 'row', [(r, r ^ 1) for r in range(CB)])  14.3 us
    ppermute x1, starting transfers between devices, on_device(): z_other = lax.ppermute(z_other, ('row', 'col'), pairs)  11.2 us
    pallas_call x2, Pallas kernels, forward(): pl.pallas_call(functools.partial(forward_kernel, which), out_shape=(jax.S...  8.42 us
    ppermute x1, starting transfers between devices, on_device(): grad_other = lax.ppermute(grad_own, ('row', 'col'), pairs)  4.57 us
  transfers between devices with their start and end apart: 5, of which 2 were waited for; matrix products, arithmetic and copies ran while one was open for 1% of the time, Pallas kernels for 5%

profile of v5, /device:TPU:1, one launch (start us, length us, event | category | flops | bytes accessed | tf_op | source)
XLA Modules:
  0.0 158.7 jit_solution(2798684281933572659)
XLA Ops:
  0.6 0.9 broadcast_in_dim.2
  1.5 16.6 %all_to_all.30.own_x = bf16[16,128,128]{2,1,0:T(8,128)(2,1)S(1)} all-to-all(bf16[16,128,128]{2,1,0:T(8,128)(2,1)S(1)} %broadcast_in_dim.2), channel_id=1, replica_groups={{0,32,64,96,128,160,192,224,256,288,320,352,384,416,448,480},{16,48,80,..., dimensions={0} | all-to-all | bytes 1048576 | tf_op jit(solution)/shard_map/all_to_all | solution.py:255
  18.1 5.1 %collective-permute-start = (bf16[16,128,128]{2,1,0:T(8,128)(2,1)S(1)}, bf16[16,128,128]{2,1,0:T(8,128)(2,1)S(1)}, u32[]{:S(2)}, u32[]{:S(2)}) collective-permute-start(bf16[16,128,128]{2,1,0:T(8,128)(2,1)S(1)} %all_to_all.30.own_x), channel_id=1, source_target_pairs={{0,16},{16,0},{32,48},{48,32},{64,80},{80,64},{96,112},{112,96},{1... | collective-permute-start | bytes 1572872 | tf_op jit(solution)/shard_map/ppermute | solution.py:259
  23.9 0.9 pad.4.w
  24.8 0.7 shift-left_add_fusion.ids
  25.5 0.0 collective-permute-done.other_x
  25.5 3.5 %forward.3 = (bf16[8,128,128]{2,1,0:T(8,128)(2,1)S(1)}, bf16[8,128,512]{2,1,0:T(8,128)(2,1)S(1)}) custom-call(s32[1,1,96]{2,1,0:T(1,128)S(1)} %shift-left_add_fusion.ids, s32[1,1]{1,0:T(1,128)S(6)} %copy.15.live, s32[1,1]{1,0:T(1,128)} %bitcast.side, s32[1,1]{1,0:T(1,128)} %bitcast.1.core, bf16[16,128,128]{2,1,0:T(8,128)(2,1)S(1)} %all_to_all.30.own_x, ...), custom_call_target="tpu_custom_call" | custom-call | flops 1000000000 | bytes 10000000 | tf_op jit(solution)/shard_map/forward/pallas_call | solution.py:277
  29.0 0.0 copy-start.2
  29.0 0.0 copy-start.3
  29.1 0.0 copy-start
  29.1 0.0 copy-start.1
  29.1 11.2 %collective-permute-start.1 = (bf16[8,128,128]{2,1,0:T(8,128)(2,1)S(1)}, bf16[8,128,128]{2,1,0:T(8,128)(2,1)S(1)}, u32[]{:S(2)}, u32[]{:S(2)}) collective-permute-start(bf16[8,128,128]{2,1,0:T(8,128)(2,1)S(1)} %get-tuple-element.22), channel_id=1, source_target_pairs={{0,1},{1,0},{2,3},{3,2},{4,5},{5,4},{6,7},{7,6},{8,9},{9,8},{10,11... | collective-permute-start | bytes 786440 | tf_op jit(solution)/shard_map/ppermute | solution.py:304
  40.3 4.9 %forward.2 = (f32[8,128,128]{2,1,0:T(8,128)S(1)}, bf16[8,128,512]{2,1,0:T(8,128)(2,1)S(1)}, s32[2,113]{1,0:T(2,128)S(1)}) custom-call(s32[1,1,96]{2,1,0:T(1,128)S(1)} %shift-left_add_fusion.ids, s32[1,1]{1,0:T(1,128)S(6)} %copy.15.live, s32[1,1]{1,0:T(1,128)} %bitcast.side, s32[1,1]{1,0:T(1,128)} %bitcast.1.core, ...), custom_call_target="tpu_custom_call" | custom-call | flops 1000000000 | bytes 10000000 | tf_op jit(solution)/shard_map/forward/pallas_call | solution.py:277
  45.2 0.0 collective-permute-done.1
  45.2 0.1 add_convert_fusion
  45.3 24.7 %all_to_all.31.parts = bf16[8,128,128]{2,1,0:T(8,128)(2,1)S(1)} all-to-all(bf16[8,128,128]{2,1,0:T(8,128)(2,1)S(1)} %add_convert_fusion), channel_id=1, replica_groups={{0,2,4,6,8,10,12,14},{1,3,5,7,9,11,13,15},{16,18,20,22,24,26,28,30},{17..., dimensions={0} | all-to-all | bytes 524288 | tf_op jit(solution)/shard_map/all_to_all | solution.py:255
  70.0 0.0 copy-done.2
  70.0 0.0 copy-done.3
  70.0 0.7 middle.1
  70.7 21.8 %all_to_all.32.grad_t = bf16[8,128,128]{2,1,0:T(8,128)(2,1)S(1)} all-to-all(bf16[8,128,128]{2,1,0:T(8,128)(2,1)S(1)} %get-tuple-element.25), channel_id=1, replica_groups={{0,2,4,6,8,10,12,14},{1,3,5,7,9,11,13,15},{16,18,20,22,24,26,28,30},{17..., dimensions={0} | all-to-all | bytes 524288 | tf_op jit(solution)/shard_map/all_to_all | solution.py:255
  92.5 4.6 %collective-permute-start.2 = (bf16[8,128,128]{2,1,0:T(8,128)(2,1)S(1)}, bf16[8,128,128]{2,1,0:T(8,128)(2,1)S(1)}, u32[]{:S(2)}, u32[]{:S(2)}) collective-permute-start(bf16[8,128,128]{2,1,0:T(8,128)(2,1)S(1)} %all_to_all.32.grad_t), channel_id=1, source_target_pairs={{0,1},{1,0},{2,3},{3,2},{4,5},{5,4},{6,7},{7,6},{8,9},{9,8},{10,11... | collective-permute-start | bytes 786440 | tf_op jit(solution)/shard_map/ppermute | solution.py:320
  97.1 0.0 copy-done
  97.1 0.0 copy-done.1
  97.1 2.7 %early.1 = (f32[128,512]{1,0:T(8,128)S(1)}, f32[8,128]{1,0:T(8,128)S(1)}, f32[2,16,128,128]{3,2,1,0:T(8,128)S(1)}) custom-call(s32[2,113]{1,0:T(2,128)S(1)} %get-tuple-element.24.lists, s32[1,1]{1,0:T(1,128)} %bitcast.1.core, bf16[8,128,128]{2,1,0:T(8,128)(2,1)S(1)} %all_to_all.32.grad_t, bf16[8,128,512]{2,1,0:T(8,128)(2,1)S(1)} %get-tuple-element.26.p, ...), custom_call_target="tpu_custom_call" | custom-call | flops 1000000000 | bytes 10000000 | tf_op jit(solution)/shard_map/early/pallas_call | solution.py:321
  99.9 1.0 collective-permute-done.2.grad_t
  100.8 2.3 %backward.1 = (bf16[16,128,128]{2,1,0:T(8,128)(2,1)S(1)}, bf16[16,128,128]{2,1,0:T(8,128)(2,1)S(1)}) custom-call(s32[2,113]{1,0:T(2,128)S(1)} %get-tuple-element.24.lists, s32[1,1]{1,0:T(1,128)} %bitcast.1.core, bf16[8,128,128]{2,1,0:T(8,128)(2,1)S(1)} %collective-permute-done.2.grad_t, f32[2,16,128,128]{3,2,1,0:T(8,128)S(1)} %get-tuple-element.27.early_acc, ...), custom_call_target="tpu_custom_call" | custom-call | flops 1000000000 | bytes 10000000 | tf_op jit(solution)/shard_map/backward/pallas_call | solution.py:348
  103.2 5.5 %collective-permute-start.3 = (bf16[16,128,128]{2,1,0:T(8,128)(2,1)S(1)}, bf16[16,128,128]{2,1,0:T(8,128)(2,1)S(1)}, u32[]{:S(2)}, u32[]{:S(2)}) collective-permute-start(bf16[16,128,128]{2,1,0:T(8,128)(2,1)S(1)} %get-tuple-element.29), channel_id=1, source_target_pairs={{0,16},{16,0},{32,48},{48,32},{64,80},{80,64},{96,112},{112,96},{1... | collective-permute-start | bytes 1572872 | tf_op jit(solution)/shard_map/ppermute | solution.py:259
  108.7 0.6 weight.1
  109.2 14.3 %all_to_all.33.parts = f32[32,16,128]{2,1,0:T(8,128)S(1)} all-to-all(f32[32,16,128]{2,1,0:T(8,128)S(1)} %get-tuple-element.33), channel_id=1, replica_groups=mesh['row'=32,'col'=16] {'row'}, dimensions={0} | all-to-all | bytes 524288 | tf_op jit(solution)/shard_map/all_to_all | solution.py:255
  123.6 14.3 %all_to_all.34.parts = bf16[16,16,128]{2,1,0:T(8,128)(2,1)S(1)} all-to-all(bf16[16,16,128]{2,1,0:T(8,128)(2,1)S(1)} %spread.1), channel_id=1, replica_groups=mesh['row'=32,'col'=16] {'col'}, dimensions={0} | all-to-all | bytes 131072 | tf_op jit(solution)/shard_map/all_to_all | solution.py:255
  137.9 3.7 %collective-permute-start.4 = (bf16[32,128]{1,0:T(8,128)(2,1)S(1)}, bf16[32,128]{1,0:T(8,128)(2,1)S(1)}, u32[]{:S(2)}, u32[]{:S(2)}) collective-permute-start(bf16[32,128]{1,0:T(8,128)(2,1)S(1)} %total.1.own), channel_id=1, source_target_pairs={{0,16},{16,0},{32,48},{48,32},{64,80},{80,64},{96,112},{112,96},{1... | collective-permute-start | bytes 24584 | tf_op jit(solution)/shard_map/ppermute | solution.py:259
  141.6 0.0 collective-permute-done.3.taken
  141.6 0.1 join.1.sent
  141.8 0.6 collective-permute-done.4.other
  142.4 15.3 %all_to_all.35.received = bf16[16,176,128]{2,1,0:T(8,128)(2,1)S(1)} all-to-all(bf16[16,176,128]{2,1,0:T(8,128)(2,1)S(1)} %append.1), channel_id=1, replica_groups={{0,32,64,96,128,160,192,224,256,288,320,352,384,416,448,480},{16,48,80,..., dimensions={0} | all-to-all | bytes 1441792 | tf_op jit(solution)/shard_map/all_to_all | solution.py:255
  157.8 0.9 final.1
  (3 shorter events, 0.1 us)
Async XLA Ops:
  18.1 7.4 %collective-permute-start = (bf16[16,128,128]{2,1,0:T(8,128)(2,1)S(1)}, bf16[16,128,128]{2,1,0:T(8,128)(2,1)S(1)}, u32[]{:S(2)}, u32[]{:S(2)}) collective-permute-start(bf16[16,128,128]{2,1,0:T(8,128)(2,1)S(1)} %all_to_all.30.own_x), channel_id=1, source_target_pairs={{0,16},{16,0},{32,48},{48,32},{64,80},{80,64},{96,112},{112,96},{1... | collective-permute-start | bytes 1572872 | tf_op jit(solution)/shard_map/ppermute | solution.py:259
  29.0 41.0 %copy-start.2 = (bf16[128,128]{1,0:T(8,128)(2,1)S(1)}, bf16[128,128]{1,0:T(8,128)(2,1)}, u32[]{:S(2)}) copy-start(bf16[128,128]{1,0:T(8,128)(2,1)} %out_grad.1) | copy-start | bytes 98308
  29.0 41.0 %copy-start.3 = (f32[128]{0:T(128)S(1)}, f32[128]{0:T(128)}, u32[]{:S(2)}) copy-start(f32[128]{0:T(128)} %param.16) | copy-start | bytes 1540
  29.1 68.0 %copy-start = (bf16[1,1,96,128,128]{4,3,2,1,0:T(8,128)(2,1)S(1)}, bf16[1,1,96,128,128]{4,3,2,1,0:T(8,128)(2,1)}, u32[]{:S(2)}) copy-start(bf16[1,1,96,128,128]{4,3,2,1,0:T(8,128)(2,1)} %v.7) | copy-start | bytes 9437188
  29.1 68.0 %copy-start.1 = (bf16[4,128,128]{2,1,0:T(8,128)(2,1)S(1)}, bf16[4,128,128]{2,1,0:T(8,128)(2,1)}, u32[]{:S(2)}) copy-start(bf16[4,128,128]{2,1,0:T(8,128)(2,1)} %param.15) | copy-start | bytes 393220
  29.1 16.2 %collective-permute-start.1 = (bf16[8,128,128]{2,1,0:T(8,128)(2,1)S(1)}, bf16[8,128,128]{2,1,0:T(8,128)(2,1)S(1)}, u32[]{:S(2)}, u32[]{:S(2)}) collective-permute-start(bf16[8,128,128]{2,1,0:T(8,128)(2,1)S(1)} %get-tuple-element.22), channel_id=1, source_target_pairs={{0,1},{1,0},{2,3},{3,2},{4,5},{5,4},{6,7},{7,6},{8,9},{9,8},{10,11... | collective-permute-start | bytes 786440 | tf_op jit(solution)/shard_map/ppermute | solution.py:304
  92.5 8.3 %collective-permute-start.2 = (bf16[8,128,128]{2,1,0:T(8,128)(2,1)S(1)}, bf16[8,128,128]{2,1,0:T(8,128)(2,1)S(1)}, u32[]{:S(2)}, u32[]{:S(2)}) collective-permute-start(bf16[8,128,128]{2,1,0:T(8,128)(2,1)S(1)} %all_to_all.32.grad_t), channel_id=1, source_target_pairs={{0,1},{1,0},{2,3},{3,2},{4,5},{5,4},{6,7},{7,6},{8,9},{9,8},{10,11... | collective-permute-start | bytes 786440 | tf_op jit(solution)/shard_map/ppermute | solution.py:320
  103.2 38.4 %collective-permute-start.3 = (bf16[16,128,128]{2,1,0:T(8,128)(2,1)S(1)}, bf16[16,128,128]{2,1,0:T(8,128)(2,1)S(1)}, u32[]{:S(2)}, u32[]{:S(2)}) collective-permute-start(bf16[16,128,128]{2,1,0:T(8,128)(2,1)S(1)} %get-tuple-element.29), channel_id=1, source_target_pairs={{0,16},{16,0},{32,48},{48,32},{64,80},{80,64},{96,112},{112,96},{1... | collective-permute-start | bytes 1572872 | tf_op jit(solution)/shard_map/ppermute | solution.py:259
  137.9 4.5 %collective-permute-start.4 = (bf16[32,128]{1,0:T(8,128)(2,1)S(1)}, bf16[32,128]{1,0:T(8,128)(2,1)S(1)}, u32[]{:S(2)}, u32[]{:S(2)}) collective-permute-start(bf16[32,128]{1,0:T(8,128)(2,1)S(1)} %total.1.own), channel_id=1, source_target_pairs={{0,16},{16,0},{32,48},{48,32},{64,80},{80,64},{96,112},{112,96},{1... | collective-permute-start | bytes 24584 | tf_op jit(solution)/shard_map/ppermute | solution.py:259

commit v6 on v5

--- a/solution.py
+++ b/solution.py
@@ -172,15 +172,6 @@
     lax.fori_loop(0, RB // 4, start, 0, unroll=2)
 
 
-def weight_kernel(grad_t, p, early_total, early_bias, out, bias_sum, total):
-    total[...] = early_total[...]
-    bias_sum[...] = early_bias[...]
-    weight_rows(grad_t, p, total, bias_sum)
-    for b in range(CB):
-        rel, part = b // SLICE, b % SLICE
-        out[b] = total[part * PART : (part + 1) * PART, rel * B : (rel + 1) * B]
-
-
 def spread_kernel(parts, out):
     total = parts[0]
     for r in range(1, parts.shape[0]):
@@ -190,43 +181,49 @@
         out[c] = total
 
 
-def backward_kernel(lists, core, grad_t, early_acc, v, w, kept, given, back, acc):
+def late_kernel(
+    lists, core, grad_t, p, v, w, early_total, early_bias, early_acc,
+    weight_parts, bias_sum, kept, given, total, back, acc
+):
+    total[...] = early_total[...]
+    bias_sum[...] = early_bias[...]
+    weight_rows(grad_t, p, total, bias_sum)
+    for b in range(CB):
+        rel, part = b // SLICE, b % SLICE
+        weight_parts[b] = total[part * PART : (part + 1) * PART, rel * B : (rel + 1) * B]
     acc[...] = early_acc[...]
     back_rows(grad_t, w[...], back)
     back_tiles(1, lists, core[0, 0], v, back, acc)
     kept[...] = acc[0].astype(jnp.bfloat16)
-    given[...] = acc[1].astype(jnp.bfloat16)
-
-
-def join_kernel(kept, taken, out):
-    total = kept[...].astype(jnp.float32) + taken[...].astype(jnp.float32)
-    out[:, :B, :] = total.astype(jnp.bfloat16)
-    out[:, B:, :] = jnp.zeros((out.shape[0], 3 * PART, B), jnp.bfloat16)
-
-
-def total_kernel(parts, bias_sum, out):
+    given[: CB // 2] = acc[1].astype(jnp.bfloat16)
+    given[CB // 2] = jnp.zeros((B, B), jnp.bfloat16)
+
+
+def total_kernel(given, parts, bias_sum, out):
     total = parts[0].astype(jnp.float32)
     for c in range(1, parts.shape[0]):
         total = total + parts[c].astype(jnp.float32)
-    out[:PART] = total.astype(jnp.bfloat16)
     row = lax.broadcasted_iota(jnp.int32, (PART, B), 0)
     term = jnp.broadcast_to(bias_sum[0:1, :], (PART, B))
     high = term.astype(jnp.bfloat16).astype(jnp.float32)
     pair = jnp.where(row == 0, high, jnp.where(row == 1, term - high, 0.0))
-    out[PART:] = pair.astype(jnp.bfloat16)
-
-
-def append_kernel(core, sent, own, other, out):
+    out[CB // 2, : 2 * PART, :] = jnp.concatenate([total, pair], axis=0).astype(jnp.bfloat16)
+
+
+def join_kernel(core, kept, given, taken, out):
+    chips = out.shape[0]
+    total = kept[...].astype(jnp.float32) + taken[:chips].astype(jnp.float32)
+    out[:, :B, :] = total.astype(jnp.bfloat16)
     first = core[0, 0] == 0
-    mine = own[...].astype(jnp.float32)
-    theirs = other[...].astype(jnp.float32)
+    mine = given[chips, : 2 * PART, :].astype(jnp.float32)
+    theirs = taken[chips, : 2 * PART, :].astype(jnp.float32)
     low = jnp.where(first, mine, theirs)
     high = jnp.where(first, theirs, mine)
     row = lax.broadcasted_iota(jnp.int32, (PART, B), 0)
     second = jnp.concatenate([high[PART + 8 :], high[PART : PART + 8]], axis=0)
     pair = jnp.where(row < 8, low[PART:], second)
     rows = jnp.concatenate([low[:PART], high[:PART], pair], axis=0).astype(jnp.bfloat16)
-    for r in range(out.shape[0]):
+    for r in range(chips):
         out[r, B:, :] = rows
 
 
@@ -266,10 +263,10 @@
     wide_weights = weights.reshape(RELS * B, B)
     chips = CB // 2
     same_core = [[2 * chip + core for chip in range(chips)] for core in range(2)]
-    core = jnp.reshape(lax.axis_index("row") % 2, (1, 1)).astype(jnp.int32)
+    core = jnp.reshape(lax.axis_index("row") & 1, (1, 1)).astype(jnp.int32)
     own_x = swap(jnp.broadcast_to(features[None], (chips, B, B)), "row", same_core)
     other_x = other_core(own_x)
-    side = jnp.reshape(lax.axis_index("col") % 2, (1, 1)).astype(jnp.int32)
+    side = jnp.reshape(lax.axis_index("col") & 1, (1, 1)).astype(jnp.int32)
 
     early_weights = jnp.pad(wide_weights, ((0, PART), (0, 0)))
 
@@ -332,36 +329,24 @@
         cost_estimate=pl.CostEstimate(flops=10**9, bytes_accessed=10**7, transcendentals=0),
         name="early",
     )(lists, core, grad_own, p_own, tile_values, wide_weights)
-    weight_parts, bias_sum = pl.pallas_call(
-        weight_kernel,
+    weight_parts, bias_sum, kept, given = pl.pallas_call(
+        late_kernel,
         out_shape=(
             jax.ShapeDtypeStruct((CB, PART, B), jnp.float32),
             jax.ShapeDtypeStruct((8, B), jnp.float32),
+            jax.ShapeDtypeStruct((chips, B, B), jnp.bfloat16),
+            jax.ShapeDtypeStruct((chips + 1, B, B), jnp.bfloat16),
         ),
-        in_specs=[VMEM] * 4,
-        out_specs=(VMEM, VMEM),
-        scratch_shapes=[pltpu.VMEM((B, RELS * B), jnp.float32)],
-        compiler_params=PARAMS,
-        name="weight",
-    )(grad_other, p_other, early_total, early_bias)
-    weight_parts = swap(weight_parts, "row")
-    kept, given = pl.pallas_call(
-        backward_kernel,
-        out_shape=(
-            jax.ShapeDtypeStruct((chips, B, B), jnp.bfloat16),
-            jax.ShapeDtypeStruct((chips, B, B), jnp.bfloat16),
-        ),
-        in_specs=[SMEM] * 2 + [VMEM] * 4,
-        out_specs=(VMEM,) * 2,
+        in_specs=[SMEM] * 2 + [VMEM] * 7,
+        out_specs=(VMEM,) * 4,
         scratch_shapes=[
+            pltpu.VMEM((B, RELS * B), jnp.float32),
             pltpu.VMEM((RB // 2, RELS * B, B), jnp.bfloat16),
             pltpu.VMEM((2, chips, B, B), jnp.float32),
         ],
         compiler_params=PARAMS,
-        cost_estimate=pl.CostEstimate(flops=10**9, bytes_accessed=10**7, transcendentals=0),
-        name="backward",
-    )(lists, core, grad_other, early_acc, tile_values, wide_weights)
-    taken = other_core(given)
+        name="late",
+    )(lists, core, grad_other, p_other, tile_values, wide_weights, early_total, early_bias, early_acc)
     own = pl.pallas_call(
         spread_kernel,
         out_shape=jax.ShapeDtypeStruct((RB, PART, B), jnp.bfloat16),
@@ -369,34 +354,24 @@
         out_specs=VMEM,
         compiler_params=PARAMS,
         name="spread",
-    )(weight_parts)
-    own = swap(own, "col")
+    )(swap(weight_parts, "row"))
+    given = pl.pallas_call(
+        total_kernel,
+        out_shape=jax.ShapeDtypeStruct(given.shape, given.dtype),
+        in_specs=[VMEM] * 3,
+        out_specs=VMEM,
+        input_output_aliases={0: 0},
+        compiler_params=PARAMS,
+        name="total",
+    )(given, swap(own, "col"), bias_sum)
     sent = pl.pallas_call(
         join_kernel,
         out_shape=jax.ShapeDtypeStruct((chips, B + 3 * PART, B), jnp.bfloat16),
-        in_specs=[VMEM] * 2,
-        out_specs=VMEM,
-        compiler_params=PARAMS,
-        cost_estimate=pl.CostEstimate(flops=10**6, bytes_accessed=10**6, transcendentals=0),
-        name="join",
-    )(kept, taken)
-    own = pl.pallas_call(
-        total_kernel,
-        out_shape=jax.ShapeDtypeStruct((2 * PART, B), jnp.bfloat16),
-        in_specs=[VMEM] * 2,
-        out_specs=VMEM,
-        compiler_params=PARAMS,
-        name="total",
-    )(own, bias_sum)
-    sent = pl.pallas_call(
-        append_kernel,
-        out_shape=jax.ShapeDtypeStruct(sent.shape, sent.dtype),
         in_specs=[SMEM] + [VMEM] * 3,
         out_specs=VMEM,
-        input_output_aliases={1: 0},
-        compiler_params=PARAMS,
-        name="append",
-    )(core, sent, own, other_core(own))
+        compiler_params=PARAMS,
+        name="join",
+    )(core, kept, given, other_core(given))
     feature_grad, weight_grad, bias_grad = pl.pallas_call(
         final_kernel,
         out_shape=(

time: 159 us -> 158 us (level)
  starting transfers between devices: 30.1 us -> 21.6 us
  waiting for transfers between devices: 1.63 us -> 5.2 us
  blocking collectives: 107 us -> 110 us
    ppermute x3 -> x2, starting transfers between devices: 14.3 us -> 9.02 us  [other_core(): return lax.ppermute(block, 'row', [(r, r ^ 1) for r in range(CB)])]
    all_to_all x6, blocking collectives: 107 us -> 110 us  [swap(): lax.all_to_all(blocks, axis, 0, 0, tiled=True, axis_index_groups=groups)]
    ppermute x1, starting transfers between devices: 4.57 us -> 1.91 us  [on_device(): grad_other = lax.ppermute(grad_own, ('row', 'col'), pairs)]
    ppermute x1, waiting for transfers between devices: 0.98 us -> 3.63 us  [on_device(): grad_other = lax.ppermute(grad_own, ('row', 'col'), pairs)]
    pallas_call x4 -> x2, Pallas kernels: 2.9 us -> 3.19 us  [the longest x1 3.17 us: on_device(): pl.pallas_call(late_kernel, out_shape=(jax.ShapeDtypeStruct((CB, PART, B)...]
  transfers between devices with their start and end apart: 5 -> 4, of which waited for: 2 -> 2; matrix products, arithmetic and copies ran while one was open for 1% -> 1% of each run, Pallas kernels for 5% -> 5%
where the time goes in v6:
time: 158 us; the launch traced here: 157 us
  blocking collectives  110 us (70%)
  starting transfers between devices  21.6 us (14%)
  Pallas kernels  16.4 us (10%)
  waiting for transfers between devices  5.2 us (3%)
  local copies, waits for them, and re-layouts  1.79 us (1%)
    all_to_all x6, blocking collectives, swap(): lax.all_to_all(blocks, axis, 0, 0, tiled=True, axis_index_groups=groups)  110 us
    ppermute x1, starting transfers between devices, on_device(): z_other = lax.ppermute(z_other, ('row', 'col'), pairs)  10.6 us
    ppermute x2, starting transfers between devices, other_core(): return lax.ppermute(block, 'row', [(r, r ^ 1) for r in range(CB)])  9.02 us
    pallas_call x2, Pallas kernels, forward(): pl.pallas_call(functools.partial(forward_kernel, which), out_shape=(jax.S...  8.75 us
    ppermute x1, waiting for transfers between devices, on_device(): grad_other = lax.ppermute(grad_own, ('row', 'col'), pairs)  3.63 us
    pallas_call x1, Pallas kernels, on_device(): pl.pallas_call(late_kernel, out_shape=(jax.ShapeDtypeStruct((CB, PART, B)...  3.17 us
  transfers between devices with their start and end apart: 4, of which 2 were waited for; matrix products, arithmetic and copies ran while one was open for 1% of the time, Pallas kernels for 5%

profile of v6, /device:TPU:1, one launch (start us, length us, event | category | flops | bytes accessed | tf_op | source)
XLA Modules:
  0.0 157.4 jit_solution(14274677976213564305)
XLA Ops:
  0.6 0.9 broadcast_in_dim.2
  1.5 16.6 %all_to_all.30.own_x = bf16[16,128,128]{2,1,0:T(8,128)(2,1)S(1)} all-to-all(bf16[16,128,128]{2,1,0:T(8,128)(2,1)S(1)} %broadcast_in_dim.2), channel_id=1, replica_groups={{0,32,64,96,128,160,192,224,256,288,320,352,384,416,448,480},{16,48,80,..., dimensions={0} | all-to-all | bytes 1048576 | tf_op jit(solution)/shard_map/all_to_all | solution.py:252
  18.1 5.1 %collective-permute-start = (bf16[16,128,128]{2,1,0:T(8,128)(2,1)S(1)}, bf16[16,128,128]{2,1,0:T(8,128)(2,1)S(1)}, u32[]{:S(2)}, u32[]{:S(2)}) collective-permute-start(bf16[16,128,128]{2,1,0:T(8,128)(2,1)S(1)} %all_to_all.30.own_x), channel_id=1, source_target_pairs={{0,16},{16,0},{32,48},{48,32},{64,80},{80,64},{96,112},{112,96},{1... | collective-permute-start | bytes 1572872 | tf_op jit(solution)/shard_map/ppermute | solution.py:256
  23.9 0.9 pad.4.w
  24.8 0.7 shift-left_add_fusion.ids
  25.5 0.0 collective-permute-done.other_x
  25.5 3.8 %forward.3 = (bf16[8,128,128]{2,1,0:T(8,128)(2,1)S(1)}, bf16[8,128,512]{2,1,0:T(8,128)(2,1)S(1)}) custom-call(s32[1,1,96]{2,1,0:T(1,128)S(1)} %shift-left_add_fusion.ids, s32[1,1]{1,0:T(1,128)S(6)} %copy.15.live, s32[1,1]{1,0:T(1,128)} %bitcast.side, s32[1,1]{1,0:T(1,128)} %bitcast.1.core, bf16[16,128,128]{2,1,0:T(8,128)(2,1)S(1)} %all_to_all.30.own_x, ...), custom_call_target="tpu_custom_call" | custom-call | flops 1000000000 | bytes 10000000 | tf_op jit(solution)/shard_map/forward/pallas_call | solution.py:274
  29.3 0.0 copy-start.2
  29.3 0.0 copy-start.3
  29.3 0.0 copy-start
  29.3 0.0 copy-start.1
  29.3 10.6 %collective-permute-start.1 = (bf16[8,128,128]{2,1,0:T(8,128)(2,1)S(1)}, bf16[8,128,128]{2,1,0:T(8,128)(2,1)S(1)}, u32[]{:S(2)}, u32[]{:S(2)}) collective-permute-start(bf16[8,128,128]{2,1,0:T(8,128)(2,1)S(1)} %get-tuple-element.22), channel_id=1, source_target_pairs={{0,1},{1,0},{2,3},{3,2},{4,5},{5,4},{6,7},{7,6},{8,9},{9,8},{10,11... | collective-permute-start | bytes 786440 | tf_op jit(solution)/shard_map/ppermute | solution.py:301
  40.0 5.0 %forward.2 = (f32[8,128,128]{2,1,0:T(8,128)S(1)}, bf16[8,128,512]{2,1,0:T(8,128)(2,1)S(1)}, s32[2,113]{1,0:T(2,128)S(1)}) custom-call(s32[1,1,96]{2,1,0:T(1,128)S(1)} %shift-left_add_fusion.ids, s32[1,1]{1,0:T(1,128)S(6)} %copy.15.live, s32[1,1]{1,0:T(1,128)} %bitcast.side, s32[1,1]{1,0:T(1,128)} %bitcast.1.core, ...), custom_call_target="tpu_custom_call" | custom-call | flops 1000000000 | bytes 10000000 | tf_op jit(solution)/shard_map/forward/pallas_call | solution.py:274
  45.0 0.0 collective-permute-done.1
  45.0 0.1 add_convert_fusion
  45.0 27.6 %all_to_all.31.parts = bf16[8,128,128]{2,1,0:T(8,128)(2,1)S(1)} all-to-all(bf16[8,128,128]{2,1,0:T(8,128)(2,1)S(1)} %add_convert_fusion), channel_id=1, replica_groups={{0,2,4,6,8,10,12,14},{1,3,5,7,9,11,13,15},{16,18,20,22,24,26,28,30},{17..., dimensions={0} | all-to-all | bytes 524288 | tf_op jit(solution)/shard_map/all_to_all | solution.py:252
  72.6 0.0 copy-done.2
  72.6 0.0 copy-done.3
  72.6 0.7 middle.1
  73.3 21.9 %all_to_all.32.grad_t = bf16[8,128,128]{2,1,0:T(8,128)(2,1)S(1)} all-to-all(bf16[8,128,128]{2,1,0:T(8,128)(2,1)S(1)} %get-tuple-element.25), channel_id=1, replica_groups={{0,2,4,6,8,10,12,14},{1,3,5,7,9,11,13,15},{16,18,20,22,24,26,28,30},{17..., dimensions={0} | all-to-all | bytes 524288 | tf_op jit(solution)/shard_map/all_to_all | solution.py:252
  95.2 1.9 %collective-permute-start.2 = (bf16[8,128,128]{2,1,0:T(8,128)(2,1)S(1)}, bf16[8,128,128]{2,1,0:T(8,128)(2,1)S(1)}, u32[]{:S(2)}, u32[]{:S(2)}) collective-permute-start(bf16[8,128,128]{2,1,0:T(8,128)(2,1)S(1)} %all_to_all.32.grad_t), channel_id=1, source_target_pairs={{0,1},{1,0},{2,3},{3,2},{4,5},{5,4},{6,7},{7,6},{8,9},{9,8},{10,11... | collective-permute-start | bytes 786440 | tf_op jit(solution)/shard_map/ppermute | solution.py:317
  97.1 0.0 copy-done
  97.1 0.0 copy-done.1
  97.1 2.7 %early.1 = (f32[128,512]{1,0:T(8,128)S(1)}, f32[8,128]{1,0:T(8,128)S(1)}, f32[2,16,128,128]{3,2,1,0:T(8,128)S(1)}) custom-call(s32[2,113]{1,0:T(2,128)S(1)} %get-tuple-element.24.lists, s32[1,1]{1,0:T(1,128)} %bitcast.1.core, bf16[8,128,128]{2,1,0:T(8,128)(2,1)S(1)} %all_to_all.32.grad_t, bf16[8,128,512]{2,1,0:T(8,128)(2,1)S(1)} %get-tuple-element.27.p, ...), custom_call_target="tpu_custom_call" | custom-call | flops 1000000000 | bytes 10000000 | tf_op jit(solution)/shard_map/early/pallas_call | solution.py:318
  99.8 3.6 %collective-permute-done.2.grad_t = bf16[8,128,128]{2,1,0:T(8,128)(2,1)S(1)} collective-permute-done((bf16[8,128,128]{2,1,0:T(8,128)(2,1)S(1)}, bf16[8,128,128]{2,1,0:T(8,128)(2,1)S(1)}, u32[]{:S(2)}, u32[]{:S(2)}) %collective-permute-start.2) | collective-permute-done | bytes 262176 | tf_op jit(solution)/shard_map/ppermute | solution.py:317
  103.5 3.2 %late.1 = (f32[32,16,128]{2,1,0:T(8,128)S(1)}, f32[8,128]{1,0:T(8,128)S(1)}, bf16[16,128,128]{2,1,0:T(8,128)(2,1)S(1)}, bf16[17,128,128]{2,1,0:T(8,128)(2,1)S(1)}) custom-call(s32[2,113]{1,0:T(2,128)S(1)} %get-tuple-element.24.lists, s32[1,1]{1,0:T(1,128)} %bitcast.1.core, bf16[8,128,128]{2,1,0:T(8,128)(2,1)S(1)} %collective-permute-done.2.grad_t, ...), custom_call_target="tpu_custom_call" | custom-call | tf_op jit(solution)/shard_map/late/pallas_call | solution.py:332
  106.7 14.4 %all_to_all.33.parts = f32[32,16,128]{2,1,0:T(8,128)S(1)} all-to-all(f32[32,16,128]{2,1,0:T(8,128)S(1)} %get-tuple-element.33), channel_id=1, replica_groups=mesh['row'=32,'col'=16] {'row'}, dimensions={0} | all-to-all | bytes 524288 | tf_op jit(solution)/shard_map/all_to_all | solution.py:252
  121.2 14.4 %all_to_all.34.parts = bf16[16,16,128]{2,1,0:T(8,128)(2,1)S(1)} all-to-all(bf16[16,16,128]{2,1,0:T(8,128)(2,1)S(1)} %spread.1), channel_id=1, replica_groups=mesh['row'=32,'col'=16] {'col'}, dimensions={0} | all-to-all | bytes 131072 | tf_op jit(solution)/shard_map/all_to_all | solution.py:252
  135.5 3.9 %collective-permute-start.3 = (bf16[17,128,128]{2,1,0:T(8,128)(2,1)S(1)}, bf16[17,128,128]{2,1,0:T(8,128)(2,1)S(1)}, u32[]{:S(2)}, u32[]{:S(2)}) collective-permute-start(bf16[17,128,128]{2,1,0:T(8,128)(2,1)S(1)} %total.1.given), channel_id=1, source_target_pairs={{0,16},{16,0},{32,48},{48,32},{64,80},{80,64},{96,112},{112,96},{1... | collective-permute-start | bytes 1671176 | tf_op jit(solution)/shard_map/ppermute | solution.py:256
  139.4 1.6 collective-permute-done.3.taken
  141.0 0.1 join.1
  141.1 15.3 %all_to_all.35.received = bf16[16,176,128]{2,1,0:T(8,128)(2,1)S(1)} all-to-all(bf16[16,176,128]{2,1,0:T(8,128)(2,1)S(1)} %join.1), channel_id=1, replica_groups={{0,32,64,96,128,160,192,224,256,288,320,352,384,416,448,480},{16,48,80,..., dimensions={0} | all-to-all | bytes 1441792 | tf_op jit(solution)/shard_map/all_to_all | solution.py:252
  156.5 0.9 final.1
  (2 shorter events, 0.1 us)
Async XLA Ops:
  18.1 7.4 %collective-permute-start = (bf16[16,128,128]{2,1,0:T(8,128)(2,1)S(1)}, bf16[16,128,128]{2,1,0:T(8,128)(2,1)S(1)}, u32[]{:S(2)}, u32[]{:S(2)}) collective-permute-start(bf16[16,128,128]{2,1,0:T(8,128)(2,1)S(1)} %all_to_all.30.own_x), channel_id=1, source_target_pairs={{0,16},{16,0},{32,48},{48,32},{64,80},{80,64},{96,112},{112,96},{1... | collective-permute-start | bytes 1572872 | tf_op jit(solution)/shard_map/ppermute | solution.py:256
  29.3 43.4 %copy-start.2 = (bf16[128,128]{1,0:T(8,128)(2,1)S(1)}, bf16[128,128]{1,0:T(8,128)(2,1)}, u32[]{:S(2)}) copy-start(bf16[128,128]{1,0:T(8,128)(2,1)} %out_grad.1) | copy-start | bytes 98308
  29.3 43.4 %copy-start.3 = (f32[128]{0:T(128)S(1)}, f32[128]{0:T(128)}, u32[]{:S(2)}) copy-start(f32[128]{0:T(128)} %param.16) | copy-start | bytes 1540
  29.3 67.8 %copy-start = (bf16[1,1,96,128,128]{4,3,2,1,0:T(8,128)(2,1)S(1)}, bf16[1,1,96,128,128]{4,3,2,1,0:T(8,128)(2,1)}, u32[]{:S(2)}) copy-start(bf16[1,1,96,128,128]{4,3,2,1,0:T(8,128)(2,1)} %v.7) | copy-start | bytes 9437188
  29.3 67.8 %copy-start.1 = (bf16[4,128,128]{2,1,0:T(8,128)(2,1)S(1)}, bf16[4,128,128]{2,1,0:T(8,128)(2,1)}, u32[]{:S(2)}) copy-start(bf16[4,128,128]{2,1,0:T(8,128)(2,1)} %param.15) | copy-start | bytes 393220
  29.3 15.7 %collective-permute-start.1 = (bf16[8,128,128]{2,1,0:T(8,128)(2,1)S(1)}, bf16[8,128,128]{2,1,0:T(8,128)(2,1)S(1)}, u32[]{:S(2)}, u32[]{:S(2)}) collective-permute-start(bf16[8,128,128]{2,1,0:T(8,128)(2,1)S(1)} %get-tuple-element.22), channel_id=1, source_target_pairs={{0,1},{1,0},{2,3},{3,2},{4,5},{5,4},{6,7},{7,6},{8,9},{9,8},{10,11... | collective-permute-start | bytes 786440 | tf_op jit(solution)/shard_map/ppermute | solution.py:301
  95.2 8.3 %collective-permute-start.2 = (bf16[8,128,128]{2,1,0:T(8,128)(2,1)S(1)}, bf16[8,128,128]{2,1,0:T(8,128)(2,1)S(1)}, u32[]{:S(2)}, u32[]{:S(2)}) collective-permute-start(bf16[8,128,128]{2,1,0:T(8,128)(2,1)S(1)} %all_to_all.32.grad_t), channel_id=1, source_target_pairs={{0,1},{1,0},{2,3},{3,2},{4,5},{5,4},{6,7},{7,6},{8,9},{9,8},{10,11... | collective-permute-start | bytes 786440 | tf_op jit(solution)/shard_map/ppermute | solution.py:317
  135.5 5.5 %collective-permute-start.3 = (bf16[17,128,128]{2,1,0:T(8,128)(2,1)S(1)}, bf16[17,128,128]{2,1,0:T(8,128)(2,1)S(1)}, u32[]{:S(2)}, u32[]{:S(2)}) collective-permute-start(bf16[17,128,128]{2,1,0:T(8,128)(2,1)S(1)} %total.1.given), channel_id=1, source_target_pairs={{0,16},{16,0},{32,48},{48,32},{64,80},{80,64},{96,112},{112,96},{1... | collective-permute-start | bytes 1671176 | tf_op jit(solution)/shard_map/ppermute | solution.py:256

commit v7 on v6

--- a/solution.py
+++ b/solution.py
@@ -173,9 +173,9 @@
 
 
 def spread_kernel(parts, out):
-    total = parts[0]
+    total = parts[0].astype(jnp.float32)
     for r in range(1, parts.shape[0]):
-        total = total + parts[r]
+        total = total + parts[r].astype(jnp.float32)
     total = total.astype(jnp.bfloat16)
     for c in range(out.shape[0]):
         out[c] = total
@@ -190,7 +190,8 @@
     weight_rows(grad_t, p, total, bias_sum)
     for b in range(CB):
         rel, part = b // SLICE, b % SLICE
-        weight_parts[b] = total[part * PART : (part + 1) * PART, rel * B : (rel + 1) * B]
+        term = total[part * PART : (part + 1) * PART, rel * B : (rel + 1) * B]
+        weight_parts[b] = term.astype(jnp.bfloat16)
     acc[...] = early_acc[...]
     back_rows(grad_t, w[...], back)
     back_tiles(1, lists, core[0, 0], v, back, acc)
@@ -332,7 +333,7 @@
     weight_parts, bias_sum, kept, given = pl.pallas_call(
         late_kernel,
         out_shape=(
-            jax.ShapeDtypeStruct((CB, PART, B), jnp.float32),
+            jax.ShapeDtypeStruct((CB, PART, B), jnp.bfloat16),
             jax.ShapeDtypeStruct((8, B), jnp.float32),
             jax.ShapeDtypeStruct((chips, B, B), jnp.bfloat16),
             jax.ShapeDtypeStruct((chips + 1, B, B), jnp.bfloat16),

time: 158 us -> 156 us (0.987)
  Pallas kernels: 16.4 us -> 14.7 us
  transfers between devices with their start and end apart: 4 -> 4, of which waited for: 2 -> 2; matrix products, arithmetic and copies ran while one was open for 1% -> 1% of each run, Pallas kernels for 5% -> 4%
where the time goes in v7:
time: 156 us
  blocking collectives  109 us (70%)
  starting transfers between devices  22.2 us (14%)
  Pallas kernels  14.7 us (9%)
  waiting for transfers between devices  5.51 us (4%)
  local copies, waits for them, and re-layouts  1.79 us (1%)
    all_to_all x6, blocking collectives, swap(): lax.all_to_all(blocks, axis, 0, 0, tiled=True, axis_index_groups=groups)  109 us
    ppermute x1, starting transfers between devices, on_device(): z_other = lax.ppermute(z_other, ('row', 'col'), pairs)  11.2 us
    ppermute x2, starting transfers between devices, other_core(): return lax.ppermute(block, 'row', [(r, r ^ 1) for r in range(CB)])  9.14 us
    pallas_call x2, Pallas kernels, forward(): pl.pallas_call(functools.partial(forward_kernel, which), out_shape=(jax.S...  7.66 us
    ppermute x1, waiting for transfers between devices, on_device(): grad_other = lax.ppermute(grad_own, ('row', 'col'), pairs)  3.94 us
  transfers between devices with their start and end apart: 4, of which 2 were waited for; matrix products, arithmetic and copies ran while one was open for 1% of the time, Pallas kernels for 4%

profile of v7, /device:TPU:1, one launch (start us, length us, event | category | flops | bytes accessed | tf_op | source)
XLA Modules:
  0.0 155.8 jit_solution(3187950716781520181)
XLA Ops:
  0.6 0.9 broadcast_in_dim.2
  1.5 16.6 %all_to_all.30.own_x = bf16[16,128,128]{2,1,0:T(8,128)(2,1)S(1)} all-to-all(bf16[16,128,128]{2,1,0:T(8,128)(2,1)S(1)} %broadcast_in_dim.2), channel_id=1, replica_groups={{0,32,64,96,128,160,192,224,256,288,320,352,384,416,448,480},{16,48,80,..., dimensions={0} | all-to-all | bytes 1048576 | tf_op jit(solution)/shard_map/all_to_all | solution.py:253
  18.1 5.1 %collective-permute-start = (bf16[16,128,128]{2,1,0:T(8,128)(2,1)S(1)}, bf16[16,128,128]{2,1,0:T(8,128)(2,1)S(1)}, u32[]{:S(2)}, u32[]{:S(2)}) collective-permute-start(bf16[16,128,128]{2,1,0:T(8,128)(2,1)S(1)} %all_to_all.30.own_x), channel_id=1, source_target_pairs={{0,16},{16,0},{32,48},{48,32},{64,80},{80,64},{96,112},{112,96},{1... | collective-permute-start | bytes 1572872 | tf_op jit(solution)/shard_map/ppermute | solution.py:257
  23.9 0.9 pad.4.w
  24.8 0.7 shift-left_add_fusion.ids
  25.5 0.0 collective-permute-done.other_x
  25.5 3.4 %forward.3 = (bf16[8,128,128]{2,1,0:T(8,128)(2,1)S(1)}, bf16[8,128,512]{2,1,0:T(8,128)(2,1)S(1)}) custom-call(s32[1,1,96]{2,1,0:T(1,128)S(1)} %shift-left_add_fusion.ids, s32[1,1]{1,0:T(1,128)S(6)} %copy.15.live, s32[1,1]{1,0:T(1,128)} %bitcast.side, s32[1,1]{1,0:T(1,128)} %bitcast.1.core, bf16[16,128,128]{2,1,0:T(8,128)(2,1)S(1)} %all_to_all.30.own_x, ...), custom_call_target="tpu_custom_call" | custom-call | flops 1000000000 | bytes 10000000 | tf_op jit(solution)/shard_map/forward/pallas_call | solution.py:275
  28.9 0.0 copy-start.2
  28.9 0.0 copy-start.3
  28.9 0.0 copy-start
  28.9 0.0 copy-start.1
  28.9 11.2 %collective-permute-start.1 = (bf16[8,128,128]{2,1,0:T(8,128)(2,1)S(1)}, bf16[8,128,128]{2,1,0:T(8,128)(2,1)S(1)}, u32[]{:S(2)}, u32[]{:S(2)}) collective-permute-start(bf16[8,128,128]{2,1,0:T(8,128)(2,1)S(1)} %get-tuple-element.22), channel_id=1, source_target_pairs={{0,1},{1,0},{2,3},{3,2},{4,5},{5,4},{6,7},{7,6},{8,9},{9,8},{10,11... | collective-permute-start | bytes 786440 | tf_op jit(solution)/shard_map/ppermute | solution.py:302
  40.1 4.3 %forward.2 = (f32[8,128,128]{2,1,0:T(8,128)S(1)}, bf16[8,128,512]{2,1,0:T(8,128)(2,1)S(1)}, s32[2,113]{1,0:T(2,128)S(1)}) custom-call(s32[1,1,96]{2,1,0:T(1,128)S(1)} %shift-left_add_fusion.ids, s32[1,1]{1,0:T(1,128)S(6)} %copy.15.live, s32[1,1]{1,0:T(1,128)} %bitcast.side, s32[1,1]{1,0:T(1,128)} %bitcast.1.core, ...), custom_call_target="tpu_custom_call" | custom-call | flops 1000000000 | bytes 10000000 | tf_op jit(solution)/shard_map/forward/pallas_call | solution.py:275
  44.4 0.0 collective-permute-done.1
  44.4 0.1 add_convert_fusion
  44.5 27.4 %all_to_all.31.parts = bf16[8,128,128]{2,1,0:T(8,128)(2,1)S(1)} all-to-all(bf16[8,128,128]{2,1,0:T(8,128)(2,1)S(1)} %add_convert_fusion), channel_id=1, replica_groups={{0,2,4,6,8,10,12,14},{1,3,5,7,9,11,13,15},{16,18,20,22,24,26,28,30},{17..., dimensions={0} | all-to-all | bytes 524288 | tf_op jit(solution)/shard_map/all_to_all | solution.py:253
  71.9 0.0 copy-done.2
  71.9 0.0 copy-done.3
  71.9 0.7 middle.1
  72.6 22.5 %all_to_all.32.grad_t = bf16[8,128,128]{2,1,0:T(8,128)(2,1)S(1)} all-to-all(bf16[8,128,128]{2,1,0:T(8,128)(2,1)S(1)} %get-tuple-element.25), channel_id=1, replica_groups={{0,2,4,6,8,10,12,14},{1,3,5,7,9,11,13,15},{16,18,20,22,24,26,28,30},{17..., dimensions={0} | all-to-all | bytes 524288 | tf_op jit(solution)/shard_map/all_to_all | solution.py:253
  95.1 1.9 %collective-permute-start.2 = (bf16[8,128,128]{2,1,0:T(8,128)(2,1)S(1)}, bf16[8,128,128]{2,1,0:T(8,128)(2,1)S(1)}, u32[]{:S(2)}, u32[]{:S(2)}) collective-permute-start(bf16[8,128,128]{2,1,0:T(8,128)(2,1)S(1)} %all_to_all.32.grad_t), channel_id=1, source_target_pairs={{0,1},{1,0},{2,3},{3,2},{4,5},{5,4},{6,7},{7,6},{8,9},{9,8},{10,11... | collective-permute-start | bytes 786440 | tf_op jit(solution)/shard_map/ppermute | solution.py:318
  97.0 0.0 copy-done
  97.0 0.0 copy-done.1
  97.0 2.4 %early.1 = (f32[128,512]{1,0:T(8,128)S(1)}, f32[8,128]{1,0:T(8,128)S(1)}, f32[2,16,128,128]{3,2,1,0:T(8,128)S(1)}) custom-call(s32[2,113]{1,0:T(2,128)S(1)} %get-tuple-element.24.lists, s32[1,1]{1,0:T(1,128)} %bitcast.1.core, bf16[8,128,128]{2,1,0:T(8,128)(2,1)S(1)} %all_to_all.32.grad_t, bf16[8,128,512]{2,1,0:T(8,128)(2,1)S(1)} %get-tuple-element.27.p, ...), custom_call_target="tpu_custom_call" | custom-call | flops 1000000000 | bytes 10000000 | tf_op jit(solution)/shard_map/early/pallas_call | solution.py:319
  99.5 3.9 %collective-permute-done.2.grad_t = bf16[8,128,128]{2,1,0:T(8,128)(2,1)S(1)} collective-permute-done((bf16[8,128,128]{2,1,0:T(8,128)(2,1)S(1)}, bf16[8,128,128]{2,1,0:T(8,128)(2,1)S(1)}, u32[]{:S(2)}, u32[]{:S(2)}) %collective-permute-start.2) | collective-permute-done | bytes 262176 | tf_op jit(solution)/shard_map/ppermute | solution.py:318
  103.4 2.9 %late.1 = (bf16[32,16,128]{2,1,0:T(8,128)(2,1)S(1)}, f32[8,128]{1,0:T(8,128)S(1)}, bf16[16,128,128]{2,1,0:T(8,128)(2,1)S(1)}, bf16[17,128,128]{2,1,0:T(8,128)(2,1)S(1)}) custom-call(s32[2,113]{1,0:T(2,128)S(1)} %get-tuple-element.24.lists, s32[1,1]{1,0:T(1,128)} %bitcast.1.core, bf16[8,128,128]{2,1,0:T(8,128)(2,1)S(1)} %collective-permute-done.2.grad_t, ...), custom_call_target="tpu_custom_call" | custom-call | tf_op jit(solution)/shard_map/late/pallas_call | solution.py:333
  106.3 13.3 %all_to_all.33.parts = bf16[32,16,128]{2,1,0:T(8,128)(2,1)S(1)} all-to-all(bf16[32,16,128]{2,1,0:T(8,128)(2,1)S(1)} %get-tuple-element.33), channel_id=1, replica_groups=mesh['row'=32,'col'=16] {'row'}, dimensions={0} | all-to-all | bytes 262144 | tf_op jit(solution)/shard_map/all_to_all | solution.py:253
  119.6 14.4 %all_to_all.34.parts = bf16[16,16,128]{2,1,0:T(8,128)(2,1)S(1)} all-to-all(bf16[16,16,128]{2,1,0:T(8,128)(2,1)S(1)} %spread.1), channel_id=1, replica_groups=mesh['row'=32,'col'=16] {'col'}, dimensions={0} | all-to-all | bytes 131072 | tf_op jit(solution)/shard_map/all_to_all | solution.py:253
  134.0 4.0 %collective-permute-start.3 = (bf16[17,128,128]{2,1,0:T(8,128)(2,1)S(1)}, bf16[17,128,128]{2,1,0:T(8,128)(2,1)S(1)}, u32[]{:S(2)}, u32[]{:S(2)}) collective-permute-start(bf16[17,128,128]{2,1,0:T(8,128)(2,1)S(1)} %total.1.given), channel_id=1, source_target_pairs={{0,16},{16,0},{32,48},{48,32},{64,80},{80,64},{96,112},{112,96},{1... | collective-permute-start | bytes 1671176 | tf_op jit(solution)/shard_map/ppermute | solution.py:257
  138.0 1.6 %collective-permute-done.3.taken = bf16[17,128,128]{2,1,0:T(8,128)(2,1)S(1)} collective-permute-done((bf16[17,128,128]{2,1,0:T(8,128)(2,1)S(1)}, bf16[17,128,128]{2,1,0:T(8,128)(2,1)S(1)}, u32[]{:S(2)}, u32[]{:S(2)}) %collective-permute-start.3) | collective-permute-done | bytes 557088 | tf_op jit(solution)/shard_map/ppermute | solution.py:257
  139.6 0.1 join.1
  139.7 15.2 %all_to_all.35.received = bf16[16,176,128]{2,1,0:T(8,128)(2,1)S(1)} all-to-all(bf16[16,176,128]{2,1,0:T(8,128)(2,1)S(1)} %join.1), channel_id=1, replica_groups={{0,32,64,96,128,160,192,224,256,288,320,352,384,416,448,480},{16,48,80,..., dimensions={0} | all-to-all | bytes 1441792 | tf_op jit(solution)/shard_map/all_to_all | solution.py:253
  154.9 0.9 final.1
  (2 shorter events, 0.1 us)
Async XLA Ops:
  18.1 7.4 %collective-permute-start = (bf16[16,128,128]{2,1,0:T(8,128)(2,1)S(1)}, bf16[16,128,128]{2,1,0:T(8,128)(2,1)S(1)}, u32[]{:S(2)}, u32[]{:S(2)}) collective-permute-start(bf16[16,128,128]{2,1,0:T(8,128)(2,1)S(1)} %all_to_all.30.own_x), channel_id=1, source_target_pairs={{0,16},{16,0},{32,48},{48,32},{64,80},{80,64},{96,112},{112,96},{1... | collective-permute-start | bytes 1572872 | tf_op jit(solution)/shard_map/ppermute | solution.py:257
  28.9 43.0 %copy-start.2 = (bf16[128,128]{1,0:T(8,128)(2,1)S(1)}, bf16[128,128]{1,0:T(8,128)(2,1)}, u32[]{:S(2)}) copy-start(bf16[128,128]{1,0:T(8,128)(2,1)} %out_grad.1) | copy-start | bytes 98308
  28.9 43.0 %copy-start.3 = (f32[128]{0:T(128)S(1)}, f32[128]{0:T(128)}, u32[]{:S(2)}) copy-start(f32[128]{0:T(128)} %param.16) | copy-start | bytes 1540
  28.9 68.1 %copy-start = (bf16[1,1,96,128,128]{4,3,2,1,0:T(8,128)(2,1)S(1)}, bf16[1,1,96,128,128]{4,3,2,1,0:T(8,128)(2,1)}, u32[]{:S(2)}) copy-start(bf16[1,1,96,128,128]{4,3,2,1,0:T(8,128)(2,1)} %v.7) | copy-start | bytes 9437188
  28.9 68.1 %copy-start.1 = (bf16[4,128,128]{2,1,0:T(8,128)(2,1)S(1)}, bf16[4,128,128]{2,1,0:T(8,128)(2,1)}, u32[]{:S(2)}) copy-start(bf16[4,128,128]{2,1,0:T(8,128)(2,1)} %param.15) | copy-start | bytes 393220
  28.9 15.5 %collective-permute-start.1 = (bf16[8,128,128]{2,1,0:T(8,128)(2,1)S(1)}, bf16[8,128,128]{2,1,0:T(8,128)(2,1)S(1)}, u32[]{:S(2)}, u32[]{:S(2)}) collective-permute-start(bf16[8,128,128]{2,1,0:T(8,128)(2,1)S(1)} %get-tuple-element.22), channel_id=1, source_target_pairs={{0,1},{1,0},{2,3},{3,2},{4,5},{5,4},{6,7},{7,6},{8,9},{9,8},{10,11... | collective-permute-start | bytes 786440 | tf_op jit(solution)/shard_map/ppermute | solution.py:302
  95.1 8.3 %collective-permute-start.2 = (bf16[8,128,128]{2,1,0:T(8,128)(2,1)S(1)}, bf16[8,128,128]{2,1,0:T(8,128)(2,1)S(1)}, u32[]{:S(2)}, u32[]{:S(2)}) collective-permute-start(bf16[8,128,128]{2,1,0:T(8,128)(2,1)S(1)} %all_to_all.32.grad_t), channel_id=1, source_target_pairs={{0,1},{1,0},{2,3},{3,2},{4,5},{5,4},{6,7},{7,6},{8,9},{9,8},{10,11... | collective-permute-start | bytes 786440 | tf_op jit(solution)/shard_map/ppermute | solution.py:318
  134.0 5.6 %collective-permute-start.3 = (bf16[17,128,128]{2,1,0:T(8,128)(2,1)S(1)}, bf16[17,128,128]{2,1,0:T(8,128)(2,1)S(1)}, u32[]{:S(2)}, u32[]{:S(2)}) collective-permute-start(bf16[17,128,128]{2,1,0:T(8,128)(2,1)S(1)} %total.1.given), channel_id=1, source_target_pairs={{0,16},{16,0},{32,48},{48,32},{64,80},{80,64},{96,112},{112,96},{1... | collective-permute-start | bytes 1671176 | tf_op jit(solution)/shard_map/ppermute | solution.py:257

commit v8 on v7

--- a/solution.py
+++ b/solution.py
@@ -13,7 +13,7 @@
 B = 128
 TILES = 96
 BATCH = 4
-SHORT = 16
+SHORT = 24
 CHUNK_BITS = 4
 CHUNK = 1 << CHUNK_BITS
 CHUNKS = TILES // CHUNK
@@ -31,7 +31,7 @@
 
 
 def forward_kernel(
-    which, ids, live, side, core, own_x, other_x, v, w, z, p, *rest
+    which, ids, side, core, own_x, other_x, v, w, z, p, *rest
 ):
     lists = rest[0] if which == 0 else None
     x, acc, tiles, wide, listed, sems = rest[-6:]
@@ -51,11 +51,11 @@
     wanted = side[0, 0] ^ which
 
     def put(k, at):
-        code = ids[0, 0, k]
+        code = ids[0, 0, k] & ((1 << 11) - 1)
         listed[at] = code + (k << 11)
         return at + jnp.where((code & 1) == wanted, 1, 0)
 
-    count = lax.fori_loop(0, live[0, 0], put, 0)
+    count = lax.fori_loop(0, ids[0, 0, 0] >> 11, put, 0)
     for u in range(SHORT):
         listed[count + u] = 0
 
@@ -90,12 +90,12 @@
 
     lax.fori_loop(0, RB // 2 // BATCH, finish, 0, unroll=2)
     if which == 0:
-        both_lists(ids, live[0, 0], side[0, 0], lists)
+        both_lists(ids, ids[0, 0, 0] >> 11, side[0, 0], lists)
 
 
 def both_lists(ids, live, side, lists):
     def put(k, at):
-        code = ids[0, 0, k]
+        code = ids[0, 0, k] & ((1 << 11) - 1)
         other = (code & 1) ^ side
         lists[other, jnp.where(other == 1, at, k - at)] = code + (k << 11)
         return at + other
@@ -260,7 +260,7 @@
 def on_device(
     features, tile_values, tile_rows, tile_cols, tile_rels, live, weights, bias, out_grad
 ):
-    ids = tile_rows + (tile_cols << 4) + (tile_rels << 9)
+    ids = tile_rows + (tile_cols << 4) + (tile_rels << 9) + (live.reshape(1, 1, 1) << 11)
     wide_weights = weights.reshape(RELS * B, B)
     chips = CB // 2
     same_core = [[2 * chip + core for chip in range(chips)] for core in range(2)]
@@ -279,7 +279,7 @@
                 jax.ShapeDtypeStruct((RB // 2, B, RELS * B), jnp.bfloat16),
             )
             + (jax.ShapeDtypeStruct((2, TILES + SHORT + 1), jnp.int32),) * (1 - which),
-            in_specs=[SMEM] * 4 + [VMEM] * 2 + [ANY] * 2,
+            in_specs=[SMEM] * 3 + [VMEM] * 2 + [ANY] * 2,
             out_specs=(VMEM, VMEM) + (SMEM,) * (1 - which),
             scratch_shapes=[
                 pltpu.VMEM((2, chips, B, B), jnp.bfloat16),
@@ -292,7 +292,7 @@
             compiler_params=WIDE,
             cost_estimate=pl.CostEstimate(flops=10**9, bytes_accessed=10**7, transcendentals=0),
             name="forward",
-        )(ids, live, side, core, own_x, other_x, tile_values, early_weights)
+        )(ids, side, core, own_x, other_x, tile_values, early_weights)
 
     def partner(r, c):
         return c ^ 1 if r % 2 == 0 else ((c + 1) ^ 1) - 1

time: 156 us -> 157 us (level)
  transfers between devices with their start and end apart: 4 -> 4, of which waited for: 2 -> 2; matrix products, arithmetic and copies ran while one was open for 1% -> 1% of each run, Pallas kernels for 4% -> 5%
where the time goes in v8:
time: 157 us; the launch traced here: 156 us
  blocking collectives  109 us (69%)
  starting transfers between devices  22.4 us (14%)
  Pallas kernels  15.3 us (10%)
  waiting for transfers between devices  5.33 us (3%)
  local copies, waits for them, and re-layouts  1.79 us (1%)
    all_to_all x6, blocking collectives, swap(): lax.all_to_all(blocks, axis, 0, 0, tiled=True, axis_index_groups=groups)  109 us
    ppermute x1, starting transfers between devices, on_device(): z_other = lax.ppermute(z_other, ('row', 'col'), pairs)  11.4 us
    ppermute x2, starting transfers between devices, other_core(): return lax.ppermute(block, 'row', [(r, r ^ 1) for r in range(CB)])  9.14 us
    pallas_call x2, Pallas kernels, forward(): pl.pallas_call(functools.partial(forward_kernel, which), out_shape=(jax.S...  8.22 us
    ppermute x1, waiting for transfers between devices, on_device(): grad_other = lax.ppermute(grad_own, ('row', 'col'), pairs)  3.77 us
  transfers between devices with their start and end apart: 4, of which 2 were waited for; matrix products, arithmetic and copies ran while one was open for 1% of the time, Pallas kernels for 5%

profile of v8, /device:TPU:1, one launch (start us, length us, event | category | flops | bytes accessed | tf_op | source)
XLA Modules:
  0.0 156.1 jit_solution(7162501448716242595)
XLA Ops:
  0.6 0.9 broadcast_in_dim.2
  1.5 16.6 %all_to_all.30.own_x = bf16[16,128,128]{2,1,0:T(8,128)(2,1)S(1)} all-to-all(bf16[16,128,128]{2,1,0:T(8,128)(2,1)S(1)} %broadcast_in_dim.2), channel_id=1, replica_groups={{0,32,64,96,128,160,192,224,256,288,320,352,384,416,448,480},{16,48,80,..., dimensions={0} | all-to-all | bytes 1048576 | tf_op jit(solution)/shard_map/all_to_all | solution.py:253
  18.1 5.1 %collective-permute-start = (bf16[16,128,128]{2,1,0:T(8,128)(2,1)S(1)}, bf16[16,128,128]{2,1,0:T(8,128)(2,1)S(1)}, u32[]{:S(2)}, u32[]{:S(2)}) collective-permute-start(bf16[16,128,128]{2,1,0:T(8,128)(2,1)S(1)} %all_to_all.30.own_x), channel_id=1, source_target_pairs={{0,16},{16,0},{32,48},{48,32},{64,80},{80,64},{96,112},{112,96},{1... | collective-permute-start | bytes 1572872 | tf_op jit(solution)/shard_map/ppermute | solution.py:257
  23.9 0.9 pad.4.w
  24.8 0.7 add_add_fusion.ids
  25.5 0.0 collective-permute-done.other_x
  25.5 3.4 %forward.3 = (bf16[8,128,128]{2,1,0:T(8,128)(2,1)S(1)}, bf16[8,128,512]{2,1,0:T(8,128)(2,1)S(1)}) custom-call(s32[1,1,96]{2,1,0:T(1,128)S(1)} %add_add_fusion.ids, s32[1,1]{1,0:T(1,128)} %bitcast.1.side, s32[1,1]{1,0:T(1,128)} %bitcast.2.core, bf16[16,128,128]{2,1,0:T(8,128)(2,1)S(1)} %all_to_all.30.own_x, ...), custom_call_target="tpu_custom_call" | custom-call | flops 1000000000 | bytes 10000000 | tf_op jit(solution)/shard_map/forward/pallas_call | solution.py:275
  28.9 0.0 copy-start.2
  28.9 0.0 copy-start.3
  28.9 0.0 copy-start
  28.9 0.0 copy-start.1
  28.9 11.4 %collective-permute-start.1 = (bf16[8,128,128]{2,1,0:T(8,128)(2,1)S(1)}, bf16[8,128,128]{2,1,0:T(8,128)(2,1)S(1)}, u32[]{:S(2)}, u32[]{:S(2)}) collective-permute-start(bf16[8,128,128]{2,1,0:T(8,128)(2,1)S(1)} %get-tuple-element.22), channel_id=1, source_target_pairs={{0,1},{1,0},{2,3},{3,2},{4,5},{5,4},{6,7},{7,6},{8,9},{9,8},{10,11... | collective-permute-start | bytes 786440 | tf_op jit(solution)/shard_map/ppermute | solution.py:302
  40.3 4.8 %forward.2 = (f32[8,128,128]{2,1,0:T(8,128)S(1)}, bf16[8,128,512]{2,1,0:T(8,128)(2,1)S(1)}, s32[2,121]{1,0:T(2,128)S(1)}) custom-call(s32[1,1,96]{2,1,0:T(1,128)S(1)} %add_add_fusion.ids, s32[1,1]{1,0:T(1,128)} %bitcast.1.side, s32[1,1]{1,0:T(1,128)} %bitcast.2.core, bf16[16,128,128]{2,1,0:T(8,128)(2,1)S(1)} %all_to_all.30.own_x, ...), custom_call_target="tpu_custom_call" | custom-call | flops 1000000000 | bytes 10000000 | tf_op jit(solution)/shard_map/forward/pallas_call | solution.py:275
  45.2 0.0 collective-permute-done.1
  45.2 0.1 add_convert_fusion
  45.3 27.5 %all_to_all.31.parts = bf16[8,128,128]{2,1,0:T(8,128)(2,1)S(1)} all-to-all(bf16[8,128,128]{2,1,0:T(8,128)(2,1)S(1)} %add_convert_fusion), channel_id=1, replica_groups={{0,2,4,6,8,10,12,14},{1,3,5,7,9,11,13,15},{16,18,20,22,24,26,28,30},{17..., dimensions={0} | all-to-all | bytes 524288 | tf_op jit(solution)/shard_map/all_to_all | solution.py:253
  72.8 0.0 copy-done.2
  72.8 0.0 copy-done.3
  72.8 0.7 middle.1
  73.5 22.4 %all_to_all.32.grad_t = bf16[8,128,128]{2,1,0:T(8,128)(2,1)S(1)} all-to-all(bf16[8,128,128]{2,1,0:T(8,128)(2,1)S(1)} %get-tuple-element.25), channel_id=1, replica_groups={{0,2,4,6,8,10,12,14},{1,3,5,7,9,11,13,15},{16,18,20,22,24,26,28,30},{17..., dimensions={0} | all-to-all | bytes 524288 | tf_op jit(solution)/shard_map/all_to_all | solution.py:253
  95.8 1.9 %collective-permute-start.2 = (bf16[8,128,128]{2,1,0:T(8,128)(2,1)S(1)}, bf16[8,128,128]{2,1,0:T(8,128)(2,1)S(1)}, u32[]{:S(2)}, u32[]{:S(2)}) collective-permute-start(bf16[8,128,128]{2,1,0:T(8,128)(2,1)S(1)} %all_to_all.32.grad_t), channel_id=1, source_target_pairs={{0,1},{1,0},{2,3},{3,2},{4,5},{5,4},{6,7},{7,6},{8,9},{9,8},{10,11... | collective-permute-start | bytes 786440 | tf_op jit(solution)/shard_map/ppermute | solution.py:318
  97.8 0.0 copy-done
  97.8 0.0 copy-done.1
  97.8 2.6 %early.1 = (f32[128,512]{1,0:T(8,128)S(1)}, f32[8,128]{1,0:T(8,128)S(1)}, f32[2,16,128,128]{3,2,1,0:T(8,128)S(1)}) custom-call(s32[2,121]{1,0:T(2,128)S(1)} %get-tuple-element.24.lists, s32[1,1]{1,0:T(1,128)} %bitcast.2.core, bf16[8,128,128]{2,1,0:T(8,128)(2,1)S(1)} %all_to_all.32.grad_t, bf16[8,128,512]{2,1,0:T(8,128)(2,1)S(1)} %get-tuple-element.27.p, ...), custom_call_target="tpu_custom_call" | custom-call | flops 1000000000 | bytes 10000000 | tf_op jit(solution)/shard_map/early/pallas_call | solution.py:319
  100.4 3.8 %collective-permute-done.2.grad_t = bf16[8,128,128]{2,1,0:T(8,128)(2,1)S(1)} collective-permute-done((bf16[8,128,128]{2,1,0:T(8,128)(2,1)S(1)}, bf16[8,128,128]{2,1,0:T(8,128)(2,1)S(1)}, u32[]{:S(2)}, u32[]{:S(2)}) %collective-permute-start.2) | collective-permute-done | bytes 262176 | tf_op jit(solution)/shard_map/ppermute | solution.py:318
  104.2 2.7 %late.1 = (bf16[32,16,128]{2,1,0:T(8,128)(2,1)S(1)}, f32[8,128]{1,0:T(8,128)S(1)}, bf16[16,128,128]{2,1,0:T(8,128)(2,1)S(1)}, bf16[17,128,128]{2,1,0:T(8,128)(2,1)S(1)}) custom-call(s32[2,121]{1,0:T(2,128)S(1)} %get-tuple-element.24.lists, s32[1,1]{1,0:T(1,128)} %bitcast.2.core, bf16[8,128,128]{2,1,0:T(8,128)(2,1)S(1)} %collective-permute-done.2.grad_t, ...), custom_call_target="tpu_custom_call" | custom-call | tf_op jit(solution)/shard_map/late/pallas_call | solution.py:333
  106.9 12.6 %all_to_all.33.parts = bf16[32,16,128]{2,1,0:T(8,128)(2,1)S(1)} all-to-all(bf16[32,16,128]{2,1,0:T(8,128)(2,1)S(1)} %get-tuple-element.33), channel_id=1, replica_groups=mesh['row'=32,'col'=16] {'row'}, dimensions={0} | all-to-all | bytes 262144 | tf_op jit(solution)/shard_map/all_to_all | solution.py:253
  119.5 14.8 %all_to_all.34.parts = bf16[16,16,128]{2,1,0:T(8,128)(2,1)S(1)} all-to-all(bf16[16,16,128]{2,1,0:T(8,128)(2,1)S(1)} %spread.1), channel_id=1, replica_groups=mesh['row'=32,'col'=16] {'col'}, dimensions={0} | all-to-all | bytes 131072 | tf_op jit(solution)/shard_map/all_to_all | solution.py:253
  134.3 4.0 %collective-permute-start.3 = (bf16[17,128,128]{2,1,0:T(8,128)(2,1)S(1)}, bf16[17,128,128]{2,1,0:T(8,128)(2,1)S(1)}, u32[]{:S(2)}, u32[]{:S(2)}) collective-permute-start(bf16[17,128,128]{2,1,0:T(8,128)(2,1)S(1)} %total.1.given), channel_id=1, source_target_pairs={{0,16},{16,0},{32,48},{48,32},{64,80},{80,64},{96,112},{112,96},{1... | collective-permute-start | bytes 1671176 | tf_op jit(solution)/shard_map/ppermute | solution.py:257
  138.3 1.6 %collective-permute-done.3.taken = bf16[17,128,128]{2,1,0:T(8,128)(2,1)S(1)} collective-permute-done((bf16[17,128,128]{2,1,0:T(8,128)(2,1)S(1)}, bf16[17,128,128]{2,1,0:T(8,128)(2,1)S(1)}, u32[]{:S(2)}, u32[]{:S(2)}) %collective-permute-start.3) | collective-permute-done | bytes 557088 | tf_op jit(solution)/shard_map/ppermute | solution.py:257
  139.9 0.1 join.1
  140.0 15.2 %all_to_all.35.received = bf16[16,176,128]{2,1,0:T(8,128)(2,1)S(1)} all-to-all(bf16[16,176,128]{2,1,0:T(8,128)(2,1)S(1)} %join.1), channel_id=1, replica_groups={{0,32,64,96,128,160,192,224,256,288,320,352,384,416,448,480},{16,48,80,..., dimensions={0} | all-to-all | bytes 1441792 | tf_op jit(solution)/shard_map/all_to_all | solution.py:253
  155.2 0.9 final.1
  (2 shorter events, 0.1 us)
Async XLA Ops:
  18.1 7.4 %collective-permute-start = (bf16[16,128,128]{2,1,0:T(8,128)(2,1)S(1)}, bf16[16,128,128]{2,1,0:T(8,128)(2,1)S(1)}, u32[]{:S(2)}, u32[]{:S(2)}) collective-permute-start(bf16[16,128,128]{2,1,0:T(8,128)(2,1)S(1)} %all_to_all.30.own_x), channel_id=1, source_target_pairs={{0,16},{16,0},{32,48},{48,32},{64,80},{80,64},{96,112},{112,96},{1... | collective-permute-start | bytes 1572872 | tf_op jit(solution)/shard_map/ppermute | solution.py:257
  28.9 43.9 %copy-start.2 = (bf16[128,128]{1,0:T(8,128)(2,1)S(1)}, bf16[128,128]{1,0:T(8,128)(2,1)}, u32[]{:S(2)}) copy-start(bf16[128,128]{1,0:T(8,128)(2,1)} %out_grad.1) | copy-start | bytes 98308
  28.9 43.9 %copy-start.3 = (f32[128]{0:T(128)S(1)}, f32[128]{0:T(128)}, u32[]{:S(2)}) copy-start(f32[128]{0:T(128)} %param.16) | copy-start | bytes 1540
  28.9 68.9 %copy-start = (bf16[1,1,96,128,128]{4,3,2,1,0:T(8,128)(2,1)S(1)}, bf16[1,1,96,128,128]{4,3,2,1,0:T(8,128)(2,1)}, u32[]{:S(2)}) copy-start(bf16[1,1,96,128,128]{4,3,2,1,0:T(8,128)(2,1)} %v.7) | copy-start | bytes 9437188
  28.9 68.8 %copy-start.1 = (bf16[4,128,128]{2,1,0:T(8,128)(2,1)S(1)}, bf16[4,128,128]{2,1,0:T(8,128)(2,1)}, u32[]{:S(2)}) copy-start(bf16[4,128,128]{2,1,0:T(8,128)(2,1)} %param.15) | copy-start | bytes 393220
  28.9 16.2 %collective-permute-start.1 = (bf16[8,128,128]{2,1,0:T(8,128)(2,1)S(1)}, bf16[8,128,128]{2,1,0:T(8,128)(2,1)S(1)}, u32[]{:S(2)}, u32[]{:S(2)}) collective-permute-start(bf16[8,128,128]{2,1,0:T(8,128)(2,1)S(1)} %get-tuple-element.22), channel_id=1, source_target_pairs={{0,1},{1,0},{2,3},{3,2},{4,5},{5,4},{6,7},{7,6},{8,9},{9,8},{10,11... | collective-permute-start | bytes 786440 | tf_op jit(solution)/shard_map/ppermute | solution.py:302
  95.8 8.3 %collective-permute-start.2 = (bf16[8,128,128]{2,1,0:T(8,128)(2,1)S(1)}, bf16[8,128,128]{2,1,0:T(8,128)(2,1)S(1)}, u32[]{:S(2)}, u32[]{:S(2)}) collective-permute-start(bf16[8,128,128]{2,1,0:T(8,128)(2,1)S(1)} %all_to_all.32.grad_t), channel_id=1, source_target_pairs={{0,1},{1,0},{2,3},{3,2},{4,5},{5,4},{6,7},{7,6},{8,9},{9,8},{10,11... | collective-permute-start | bytes 786440 | tf_op jit(solution)/shard_map/ppermute | solution.py:318
  134.3 5.6 %collective-permute-start.3 = (bf16[17,128,128]{2,1,0:T(8,128)(2,1)S(1)}, bf16[17,128,128]{2,1,0:T(8,128)(2,1)S(1)}, u32[]{:S(2)}, u32[]{:S(2)}) collective-permute-start(bf16[17,128,128]{2,1,0:T(8,128)(2,1)S(1)} %total.1.given), channel_id=1, source_target_pairs={{0,16},{16,0},{32,48},{48,32},{64,80},{80,64},{96,112},{112,96},{1... | collective-permute-start | bytes 1671176 | tf_op jit(solution)/shard_map/ppermute | solution.py:257
